TPU v7x, 32 devices: a whole 2x2x4 slice. The times are simulated.
32 devices in a mesh: ctx: 4 (over x, core), fsdp: 8 (over z, y).
Axes of the slice: x: 2, y: 2, z: 4, core: 2. Of those that a mesh axis runs over, the one named last changes fastest.
Arguments:
- inputs: bfloat16 [48, 512, 1024], P('fsdp', 'ctx'), may hold values from -6 to 6
- lengths: int32 [48], P('fsdp'), may hold values from 128 to 512, as said below
- cotangent: bfloat16 [48, 512, 1024], P('fsdp', 'ctx'), may hold values from -6 to 6
- query_weight: bfloat16 [1024, 1024], P('fsdp'), may hold values from -0.1875 to 0.1875
- key_weight: bfloat16 [1024, 1024], P('fsdp'), may hold values from -0.1875 to 0.1875
- value_weight: bfloat16 [1024, 1024], P('fsdp'), may hold values from -0.1875 to 0.1875
- out_weight: bfloat16 [1024, 1024], P('fsdp'), may hold values from -3 to 3
- inner_weight: bfloat16 [1024, 4096], P('fsdp'), may hold values from -0.1875 to 0.1875
- outer_weight: bfloat16 [4096, 1024], P('fsdp'), may hold values from -0.09375 to 0.09375
- query_bias: bfloat16 [1024], P('fsdp'), may hold values from -3 to 3
- value_bias: bfloat16 [1024], P('fsdp'), may hold values from -3 to 3
- out_bias: bfloat16 [1024], P('fsdp'), may hold values from -3 to 3
- inner_bias: bfloat16 [4096], P('fsdp'), may hold values from -3 to 3
- outer_bias: bfloat16 [1024], P('fsdp'), may hold values from -3 to 3
- first_gain: bfloat16 [1024], P('fsdp'), may hold values from 0.5 to 1.5
- first_shift: bfloat16 [1024], P('fsdp'), may hold values from -3 to 3
- second_gain: bfloat16 [1024], P('fsdp'), may hold values from 0.5 to 1.5
- second_shift: bfloat16 [1024], P('fsdp'), may hold values from -3 to 3
Outputs:
- layer_out: bfloat16 [48, 512, 1024], P('fsdp', 'ctx')
- input_grad: float32 [48, 512, 1024], P('fsdp', 'ctx')
- query_weight_grad: float32 [1024, 1024], P('fsdp')
- key_weight_grad: float32 [1024, 1024], P('fsdp')
- value_weight_grad: float32 [1024, 1024], P('fsdp')
- out_weight_grad: float32 [1024, 1024], P('fsdp')
- inner_weight_grad: float32 [1024, 4096], P('fsdp')
- outer_weight_grad: float32 [4096, 1024], P('fsdp')
- query_bias_grad: float32 [1024], P('fsdp')
- value_bias_gradient: float32 [1024], P('fsdp')
- out_bias_grad: float32 [1024], P('fsdp')
- inner_bias_grad: float32 [4096], P('fsdp')
- outer_bias_grad: float32 [1024], P('fsdp')
- first_gain_grad: float32 [1024], P('fsdp')
- first_shift_grad: float32 [1024], P('fsdp')
- second_gain_grad: float32 [1024], P('fsdp')
- second_shift_grad: float32 [1024], P('fsdp')
Inputs may be any that keep to these rules, and one draw needn't show every extreme that they name: Each sequence's valid slots are its first lengths[s]; some sequence is full and some holds 128.
All inputs are finite; a program needn't handle non-finite values.
Results may differ from a plain program's by a relative error of at most 0.02.
Values may be sent and summed in bfloat16 or wider, within the bound.
A program may use at most 256 MiB of HBM per device.

v0:
```python
import jax
import jax.numpy as jnp
from jax import lax
from jax.sharding import PartitionSpec as P

HD = 64


NEGATIVE = -1e30
EPSILON = 1e-05


def layer_norm(hidden, gain, shift):
    centre = hidden - jnp.mean(hidden, -1, keepdims=True)
    spread = jnp.mean(centre * centre, -1, keepdims=True)
    return centre * lax.rsqrt(spread + EPSILON) * gain + shift


def gelu_exact(values_in):
    return jax.nn.gelu(values_in, approximate=False)


def affine(first_factor_matrix, matrix, offset):
    return jnp.dot(first_factor_matrix, matrix, preferred_element_type=jnp.float32) + offset.astype(
        jnp.float32
    )


def transpose_dot(first_factor_matrix, second_factor_matrix):
    return lax.dot_general(
        first_factor_matrix,
        second_factor_matrix,
        (((0,), (0,)), ((), ())),
        preferred_element_type=jnp.float32,
    )


def back_dot(derivative_tokens, matrix):
    return lax.dot_general(
        derivative_tokens, matrix, (((1,), (1,)), ((), ())), preferred_element_type=jnp.float32
    )


def column_sum(values_in):
    return jnp.sum(values_in.astype(jnp.float32), 0)


def per_device(
    inputs,
    lengths,
    cotangent,
    query_weight,
    key_weight,
    value_weight,
    out_weight,
    inner_weight,
    outer_weight,
    query_bias,
    value_bias,
    out_bias,
    inner_bias,
    outer_bias,
    first_gain,
    first_shift,
    second_gain,
    second_shift,
):
    shards = (
        query_weight,
        key_weight,
        value_weight,
        out_weight,
        inner_weight,
        outer_weight,
        query_bias,
        value_bias,
        out_bias,
        inner_bias,
        outer_bias,
        first_gain,
        first_shift,
        second_gain,
        second_shift,
    )
    gathered = (
        lax.all_gather(shards[0], "fsdp", axis=0, tiled=True),
        lax.all_gather(shards[1], "fsdp", axis=0, tiled=True),
        lax.all_gather(shards[2], "fsdp", axis=0, tiled=True),
        lax.all_gather(shards[3], "fsdp", axis=0, tiled=True),
        lax.all_gather(shards[4], "fsdp", axis=0, tiled=True),
        lax.all_gather(shards[5], "fsdp", axis=0, tiled=True),
        lax.all_gather(shards[6], "fsdp", axis=0, tiled=True),
        lax.all_gather(shards[7], "fsdp", axis=0, tiled=True),
        lax.all_gather(shards[8], "fsdp", axis=0, tiled=True),
        lax.all_gather(shards[9], "fsdp", axis=0, tiled=True),
        lax.all_gather(shards[10], "fsdp", axis=0, tiled=True),
        lax.all_gather(shards[11], "fsdp", axis=0, tiled=True),
        lax.all_gather(shards[12], "fsdp", axis=0, tiled=True),
        lax.all_gather(shards[13], "fsdp", axis=0, tiled=True),
        lax.all_gather(shards[14], "fsdp", axis=0, tiled=True),
    )
    (
        query_w,
        key_w,
        value_w,
        out_w,
        inner_w,
        outer_w,
        query_b,
        payload_offset_entries,
        out_b,
        inner_b,
        outer_b,
        gain_one,
        shift_one,
        gain_two,
        shift_two,
    ) = gathered
    seq_count, part_len, width = inputs.shape
    head_count = width // HD
    row_count = seq_count * part_len
    key_len = part_len * lax.axis_size("ctx")
    score_scale = HD ** (-0.5)
    offsets = lax.axis_index("ctx") * part_len + jnp.arange(part_len)
    row_valid = (offsets[None, :] < lengths[:, None]).astype(jnp.float32).reshape(row_count, 1)
    key_valid = (jnp.arange(key_len)[None, :] < lengths[:, None])[:, None, None, :]
    flat_in = inputs.reshape(row_count, width)
    queries = affine(flat_in, query_w, query_b).astype(jnp.bfloat16)
    keys_here = jnp.dot(flat_in, key_w, preferred_element_type=jnp.float32).astype(jnp.bfloat16)
    values_here = affine(flat_in, value_w, payload_offset_entries).astype(jnp.bfloat16)
    keys_all, values_all = (
        lax.all_gather(keys_here.reshape(seq_count, part_len, width), "ctx", axis=1, tiled=True),
        lax.all_gather(values_here.reshape(seq_count, part_len, width), "ctx", axis=1, tiled=True),
    )
    query_four = queries.reshape(seq_count, part_len, head_count, HD)
    key_four = keys_all.reshape(seq_count, key_len, head_count, HD)
    value_four = values_all.reshape(seq_count, key_len, head_count, HD)

    def scores_of():
        raw_scores = score_scale * jnp.einsum(
            "sqhd,skhd->shqk", query_four, key_four, preferred_element_type=jnp.float32
        )
        return jnp.where(key_valid, raw_scores, NEGATIVE)

    scores = scores_of()
    row_top = jnp.max(scores, -1, keepdims=True)
    exponent = jnp.exp(scores - row_top)
    row_total = jnp.sum(exponent, -1, keepdims=True)
    log_total = row_top + jnp.log(row_total)
    attend_low = (exponent / row_total).astype(jnp.bfloat16)
    context_rows = jnp.einsum(
        "shqk,skhd->sqhd", attend_low, value_four, preferred_element_type=jnp.float32
    )
    context_rows = context_rows.reshape(row_count, width).astype(jnp.bfloat16)
    gain_onef = gain_one.astype(jnp.float32)
    shift_onef = shift_one.astype(jnp.float32)
    gain_twof = gain_two.astype(jnp.float32)
    shift_twof = shift_two.astype(jnp.float32)
    initial_layer_input = flat_in.astype(jnp.float32) + affine(context_rows, out_w, out_b)
    standardized_activations = layer_norm(initial_layer_input, gain_onef, shift_onef)
    normed_low = standardized_activations.astype(jnp.bfloat16)
    inner_pre = affine(normed_low, inner_w, inner_b)
    activated = gelu_exact(inner_pre).astype(jnp.bfloat16)
    second_in = standardized_activations + affine(activated, outer_w, outer_b)
    layer_out = (
        layer_norm(second_in, gain_twof, shift_twof)
        .astype(jnp.bfloat16)
        .reshape(seq_count, part_len, width)
    )
    again = (
        lax.all_gather(shards[0], "fsdp", axis=0, tiled=True),
        lax.all_gather(shards[1], "fsdp", axis=0, tiled=True),
        lax.all_gather(shards[2], "fsdp", axis=0, tiled=True),
        lax.all_gather(shards[3], "fsdp", axis=0, tiled=True),
        lax.all_gather(shards[4], "fsdp", axis=0, tiled=True),
        lax.all_gather(shards[5], "fsdp", axis=0, tiled=True),
        lax.all_gather(shards[6], "fsdp", axis=0, tiled=True),
        lax.all_gather(shards[7], "fsdp", axis=0, tiled=True),
        lax.all_gather(shards[8], "fsdp", axis=0, tiled=True),
        lax.all_gather(shards[9], "fsdp", axis=0, tiled=True),
        lax.all_gather(shards[10], "fsdp", axis=0, tiled=True),
        lax.all_gather(shards[11], "fsdp", axis=0, tiled=True),
        lax.all_gather(shards[12], "fsdp", axis=0, tiled=True),
        lax.all_gather(shards[13], "fsdp", axis=0, tiled=True),
        lax.all_gather(shards[14], "fsdp", axis=0, tiled=True),
    )
    query_wb, key_wb, value_wb, out_wb, inner_wb, outer_wb = (
        again[0],
        again[1],
        again[2],
        again[3],
        again[4],
        again[5],
    )
    out_grad = cotangent.reshape(row_count, width).astype(jnp.float32) * row_valid
    ignored, pull_second = jax.vjp(layer_norm, second_in, gain_twof, shift_twof)
    d_second, grad_gain_two, grad_shift_two = pull_second(out_grad)
    d_outer = d_second.astype(jnp.bfloat16)
    grad_outer = transpose_dot(activated, d_outer)
    grad_outer_b = column_sum(d_outer)
    d_activated = back_dot(d_outer, outer_wb)
    ignored, pull_gelu = jax.vjp(gelu_exact, inner_pre)
    d_inner = pull_gelu(d_activated)[0].astype(jnp.bfloat16)
    hidden_derivative = transpose_dot(normed_low, d_inner)
    grad_inner_b = column_sum(d_inner)
    d_normed = d_second + back_dot(d_inner, inner_wb)
    ignored, pull_first = jax.vjp(layer_norm, initial_layer_input, gain_onef, shift_onef)
    d_first, grad_gain_one, grad_shift_one = pull_first(d_normed)
    d_attn = d_first.astype(jnp.bfloat16)
    grad_out = transpose_dot(context_rows, d_attn)
    grad_out_b = column_sum(d_attn)
    d_context = (
        back_dot(d_attn, out_wb).astype(jnp.bfloat16).reshape(seq_count, part_len, head_count, HD)
    )
    attend = jnp.exp(scores_of() - log_total)
    attend_low = attend.astype(jnp.bfloat16)
    d_attend = jnp.einsum(
        "sqhd,skhd->shqk", d_context, value_four, preferred_element_type=jnp.float32
    )
    inner_sum = jnp.sum(d_attend * attend, -1, keepdims=True)
    d_scores = (attend * (d_attend - inner_sum)).astype(jnp.bfloat16)
    d_queries = (
        (
            score_scale
            * jnp.einsum("shqk,skhd->sqhd", d_scores, key_four, preferred_element_type=jnp.float32)
        )
        .reshape(row_count, width)
        .astype(jnp.bfloat16)
    )
    d_keys_part = (
        score_scale
        * jnp.einsum("shqk,sqhd->skhd", d_scores, query_four, preferred_element_type=jnp.float32)
    ).reshape(seq_count, key_len, width)
    d_values_part = jnp.einsum(
        "shqk,sqhd->skhd", attend_low, d_context, preferred_element_type=jnp.float32
    ).reshape(seq_count, key_len, width)
    d_keys_sum, d_values_sum = (
        lax.psum_scatter(
            d_keys_part.astype(jnp.bfloat16), "ctx", scatter_dimension=1, tiled=True
        ).astype(jnp.float32),
        lax.psum_scatter(
            d_values_part.astype(jnp.bfloat16), "ctx", scatter_dimension=1, tiled=True
        ).astype(jnp.float32),
    )
    key_gradient = d_keys_sum.reshape(row_count, width).astype(jnp.bfloat16)
    d_values = d_values_sum.reshape(row_count, width).astype(jnp.bfloat16)
    grad_query = transpose_dot(flat_in, d_queries)
    grad_key = transpose_dot(flat_in, key_gradient)
    grad_value = transpose_dot(flat_in, d_values)
    grad_query_b = column_sum(d_queries)
    grad_value_b = column_sum(d_values)
    input_grad = (
        d_first
        + back_dot(d_queries, query_wb)
        + back_dot(key_gradient, key_wb)
        + back_dot(d_values, value_wb)
    )
    owned = (
        lax.psum_scatter(
            grad_query.astype(jnp.bfloat16), "fsdp", scatter_dimension=0, tiled=True
        ).astype(jnp.float32),
        lax.psum_scatter(
            grad_key.astype(jnp.bfloat16), "fsdp", scatter_dimension=0, tiled=True
        ).astype(jnp.float32),
        lax.psum_scatter(
            grad_value.astype(jnp.bfloat16), "fsdp", scatter_dimension=0, tiled=True
        ).astype(jnp.float32),
        lax.psum_scatter(
            grad_out.astype(jnp.bfloat16), "fsdp", scatter_dimension=0, tiled=True
        ).astype(jnp.float32),
        lax.psum_scatter(
            hidden_derivative.astype(jnp.bfloat16), "fsdp", scatter_dimension=0, tiled=True
        ).astype(jnp.float32),
        lax.psum_scatter(
            grad_outer.astype(jnp.bfloat16), "fsdp", scatter_dimension=0, tiled=True
        ).astype(jnp.float32),
        lax.psum_scatter(
            grad_query_b.astype(jnp.bfloat16), "fsdp", scatter_dimension=0, tiled=True
        ).astype(jnp.float32),
        lax.psum_scatter(
            grad_value_b.astype(jnp.bfloat16), "fsdp", scatter_dimension=0, tiled=True
        ).astype(jnp.float32),
        lax.psum_scatter(
            grad_out_b.astype(jnp.bfloat16), "fsdp", scatter_dimension=0, tiled=True
        ).astype(jnp.float32),
        lax.psum_scatter(
            grad_inner_b.astype(jnp.bfloat16), "fsdp", scatter_dimension=0, tiled=True
        ).astype(jnp.float32),
        lax.psum_scatter(
            grad_outer_b.astype(jnp.bfloat16), "fsdp", scatter_dimension=0, tiled=True
        ).astype(jnp.float32),
        lax.psum_scatter(
            grad_gain_one.astype(jnp.bfloat16), "fsdp", scatter_dimension=0, tiled=True
        ).astype(jnp.float32),
        lax.psum_scatter(
            grad_shift_one.astype(jnp.bfloat16), "fsdp", scatter_dimension=0, tiled=True
        ).astype(jnp.float32),
        lax.psum_scatter(
            grad_gain_two.astype(jnp.bfloat16), "fsdp", scatter_dimension=0, tiled=True
        ).astype(jnp.float32),
        lax.psum_scatter(
            grad_shift_two.astype(jnp.bfloat16), "fsdp", scatter_dimension=0, tiled=True
        ).astype(jnp.float32),
    )
    summed = (
        lax.psum(owned[0].astype(jnp.bfloat16), "ctx").astype(jnp.float32),
        lax.psum(owned[1].astype(jnp.bfloat16), "ctx").astype(jnp.float32),
        lax.psum(owned[2].astype(jnp.bfloat16), "ctx").astype(jnp.float32),
        lax.psum(owned[3].astype(jnp.bfloat16), "ctx").astype(jnp.float32),
        lax.psum(owned[4].astype(jnp.bfloat16), "ctx").astype(jnp.float32),
        lax.psum(owned[5].astype(jnp.bfloat16), "ctx").astype(jnp.float32),
        lax.psum(owned[6].astype(jnp.bfloat16), "ctx").astype(jnp.float32),
        lax.psum(owned[7].astype(jnp.bfloat16), "ctx").astype(jnp.float32),
        lax.psum(owned[8].astype(jnp.bfloat16), "ctx").astype(jnp.float32),
        lax.psum(owned[9].astype(jnp.bfloat16), "ctx").astype(jnp.float32),
        lax.psum(owned[10].astype(jnp.bfloat16), "ctx").astype(jnp.float32),
        lax.psum(owned[11].astype(jnp.bfloat16), "ctx").astype(jnp.float32),
        lax.psum(owned[12].astype(jnp.bfloat16), "ctx").astype(jnp.float32),
        lax.psum(owned[13].astype(jnp.bfloat16), "ctx").astype(jnp.float32),
        lax.psum(owned[14].astype(jnp.bfloat16), "ctx").astype(jnp.float32),
    )
    return (
        layer_out,
        input_grad.reshape(seq_count, part_len, width),
        summed[0],
        summed[1],
        summed[2],
        summed[3],
        summed[4],
        summed[5],
        summed[6],
        summed[7],
        summed[8],
        summed[9],
        summed[10],
        summed[11],
        summed[12],
        summed[13],
        summed[14],
    )


def solution(mesh):
    in_specs = (
        P("fsdp", "ctx", None),
        P("fsdp"),
        P("fsdp", "ctx", None),
        P("fsdp", None),
        P("fsdp", None),
        P("fsdp", None),
        P("fsdp", None),
        P("fsdp", None),
        P("fsdp", None),
        P("fsdp"),
        P("fsdp"),
        P("fsdp"),
        P("fsdp"),
        P("fsdp"),
        P("fsdp"),
        P("fsdp"),
        P("fsdp"),
        P("fsdp"),
    )
    out_specs = (
        P("fsdp", "ctx", None),
        P("fsdp", "ctx", None),
        P("fsdp", None),
        P("fsdp", None),
        P("fsdp", None),
        P("fsdp", None),
        P("fsdp", None),
        P("fsdp", None),
        P("fsdp"),
        P("fsdp"),
        P("fsdp"),
        P("fsdp"),
        P("fsdp"),
        P("fsdp"),
        P("fsdp"),
        P("fsdp"),
        P("fsdp"),
    )
    return jax.shard_map(
        per_device, mesh=mesh, in_specs=in_specs, out_specs=out_specs, check_vma=False
    )
```

profile of v0, /device:TPU:1, one launch (start us, length us, event | category | flops | bytes accessed | tf_op | source)
XLA Modules:
  0.0 1441.7 jit_solution(17263454162664472732)
XLA Ops:
  9.5 51.0 %all-gather.24.cloned.1.call-done = bf16[1024,1024]{1,0:T(8,128)(2,1)} async-done(((bf16[128,1024]{1,0:T(8,128)(2,1)}), bf16[1024,1024]{1,0:T(8,128)(2,1)}) %all-gather.24.cloned.1.call-update) | async-done | bytes 2097168 | tf_op jit(solution)/shard_map/all_gather | solution.py:87
  60.4 5.1 convolution_convert_fusion.4
  65.7 15.2 %all-gather = bf16[8,1,128]{2,1,0:T(2,128)(2,1)S(1)} all-gather(bf16[1,1,128]{2,1,0:T(2,128)(2,1)S(1)} %bitcast.158), channel_id=1, replica_groups=mesh['ctx'=4,'fsdp'=8] {'fsdp'}, dimensions={0}, use_global_device_ids=true | all-gather | bytes 2304 | tf_op jit(solution)/shard_map/all_gather | solution.py:93
  80.9 29.5 %all-gather.18.cloned.1.call-done = bf16[1024,1024]{1,0:T(8,128)(2,1)} async-done(((bf16[128,1024]{1,0:T(8,128)(2,1)}), bf16[1024,1024]{1,0:T(8,128)(2,1)}) %all-gather.18.cloned.1.call-update) | async-done | bytes 2097168 | tf_op jit(solution)/shard_map/all_gather | solution.py:88
  110.4 4.5 add_convert_fusion.3
  117.3 15.2 %all-gather.1 = bf16[8,1,128]{2,1,0:T(2,128)(2,1)S(1)} all-gather(bf16[1,1,128]{2,1,0:T(2,128)(2,1)S(1)} %bitcast.159), channel_id=1, replica_groups=mesh['ctx'=4,'fsdp'=8] {'fsdp'}, dimensions={0}, use_global_device_ids=true | all-gather | bytes 2304 | tf_op jit(solution)/shard_map/all_gather | solution.py:92
  132.5 12.7 all-gather.2
  145.2 15.1 %all-gather.6 = bf16[8,1,128]{2,1,0:T(2,128)(2,1)S(1)} all-gather(bf16[1,1,128]{2,1,0:T(2,128)(2,1)S(1)} %bitcast.161), channel_id=1, replica_groups=mesh['ctx'=4,'fsdp'=8] {'fsdp'}, dimensions={0}, use_global_device_ids=true | all-gather | bytes 2304 | tf_op jit(solution)/shard_map/all_gather | solution.py:96
  160.9 12.7 all-gather.3
  173.6 14.5 %all-gather.4 = bf16[8,1,128]{2,1,0:T(2,128)(2,1)S(1)} all-gather(bf16[1,1,128]{2,1,0:T(2,128)(2,1)S(1)} %bitcast.163), channel_id=1, replica_groups=mesh['ctx'=4,'fsdp'=8] {'fsdp'}, dimensions={0}, use_global_device_ids=true | all-gather | bytes 2304 | tf_op jit(solution)/shard_map/all_gather | solution.py:98
  188.1 13.1 all-gather.7
  201.8 14.5 %all-gather.8 = bf16[8,1,128]{2,1,0:T(2,128)(2,1)S(1)} all-gather(bf16[1,1,128]{2,1,0:T(2,128)(2,1)S(1)} %bitcast.165), channel_id=1, replica_groups=mesh['ctx'=4,'fsdp'=8] {'fsdp'}, dimensions={0}, use_global_device_ids=true | all-gather | bytes 2304 | tf_op jit(solution)/shard_map/all_gather | solution.py:100
  217.6 21.6 %all-gather.5 = bf16[8,1,512]{2,1,0:T(2,128)(2,1)S(1)} all-gather(bf16[1,1,512]{2,1,0:T(2,128)(2,1)S(1)} %reshape.225), channel_id=1, replica_groups=mesh['ctx'=4,'fsdp'=8] {'fsdp'}, dimensions={0}, use_global_device_ids=true | all-gather | bytes 9216 | tf_op jit(solution)/shard_map/all_gather | solution.py:95
  239.2 3.4 add_convert_fusion.2
  242.6 3.3 reshape.259
  245.9 4.0 copy.64
  250.0 9.2 copy.63
  259.2 15.6 %fusion.12 = (f32[6,16,128]{2,1,0:T(8,128)S(1)}, f32[6,16,128,512]{3,2,1,0:T(8,128)}) fusion(pred[6,512]{1,0:T(8,128)(4,1)S(1)} %iota_compare_fusion, bf16[6,128,16,64]{1,3,2,0:T(8,128)(2,1)S(1)} %copy.64, bf16[6,512,16,64]{1,3,2,0:T(8,128)(2,1)} %bitcast.127), kind=kOutput, calls=%fused_computation.29 | convolution fusion | flops 824168448 | bytes 33082368 | tf_op jit(solution)/shard_map/sqhd,skhd->shqk/dot_general | solution.py:140
  274.8 11.4 fusion
  286.2 8.7 copy.61
  294.9 13.4 fusion.27
  308.4 2.6 copy.65
  311.0 4.8 fusion.48
  317.3 116.0 %all-gather.30.cloned.1.call-done = bf16[1024,4096]{1,0:T(8,128)(2,1)} async-done(((bf16[128,4096]{1,0:T(8,128)(2,1)}), bf16[1024,4096]{1,0:T(8,128)(2,1)}) %all-gather.30.cloned.1.call-update) | async-done | bytes 8388624 | tf_op jit(solution)/shard_map/all_gather | solution.py:90
  433.3 38.9 %multiply_convert_fusion.2 = (bf16[768,4096]{1,0:T(8,128)(2,1)}, f32[768,4096]{1,0:T(8,128)}, f32[768,4096]{1,0:T(8,128)}) fusion(f32[4096]{0:T(1024)S(1)} %bitcast.149, bf16[1024,4096]{1,0:T(8,128)(2,1)} %all-gather.30.cloned.1.call-done, f32[768,1024]{1,0:T(8,128)S(1)} %get-tuple-element.115, f32[1024]{0:T(1024)S(1)} %bitcast.151, ...), kind=kOutput, calls=%fused_computation.14 | convolution fusion | flops 6654001152 | bytes 43022336 | tf_op jit(solution)/shard_map/dot_general | solution.py:24
  472.1 86.4 %all-gather.32.cloned.1.call-done = bf16[4096,1024]{1,0:T(8,128)(2,1)} async-done(((bf16[512,1024]{1,0:T(8,128)(2,1)}), bf16[4096,1024]{1,0:T(8,128)(2,1)}) %all-gather.32.cloned.1.call-update) | async-done | bytes 8388624 | tf_op jit(solution)/shard_map/all_gather | solution.py:91
  558.6 11.8 fusion.49
  571.8 2.2 multiply_reduce_fusion.2
  573.9 2.7 fusion.46
  576.7 2.0 fusion.42
  578.7 20.5 %fusion.43 = (bf16[4096]{0:T(1024)(128)(2,1)S(1)}, bf16[768,4096]{1,0:T(8,128)(2,1)}) fusion(f32[768,4096]{1,0:T(8,128)} %get-tuple-element.108, f32[768,4096]{1,0:T(8,128)} %get-tuple-element.116, f32[4096]{0:T(1024)S(1)} %bitcast.150, bf16[768,1024]{1,0:T(8,128)(2,1)} %get-tuple-element.98, bf16[4096,1024]{1,0:T(8,128)(2,1)} %all-gather.32.cloned.1.call-done), kind=kOutput, calls=%fused_computation.97 | convolution fusion | flops 6492778496 | bytes 41443328 | tf_op jit(solution)/shard_map/dot_general | solution.py:39
  599.3 12.7 multiply_reduce_fusion.3
  616.0 3.0 convolution_convert_fusion.3
  619.0 4.1 reshape.260
  623.1 3.3 copy.67
  626.5 13.3 fusion.13
  639.8 8.6 copy.72
  649.9 23.1 %multiply_reduce_fusion = (f32[6,16,128]{2,1,0:T(8,128)S(1)}, f32[6,16,128,512]{3,2,1,0:T(8,128)}) fusion(f32[6,16,128]{2,1,0:T(8,128)S(1)} %copy-done.20, f32[6,16,128,512]{3,2,1,0:T(8,128)} %get-tuple-element.113, pred[6,512]{1,0:T(8,128)(4,1)S(1)} %copy-done.19, bf16[6,128,16,64]{1,3,2,0:T(8,128)(2,1)S(1)} %copy-done.10, ...), kind=kOutput, calls=%fused_computation.1 | convolution fusion | flops 836751360 | bytes 58297344 | tf_op jit(solution)/shard_map/sqhd,skhd->shqk/dot_general | solution.py:217
  672.9 17.0 %multiply_convert_fusion = bf16[6,16,128,512]{3,2,1,0:T(8,128)(2,1)S(1)} fusion(f32[6,16,128,512]{3,2,1,0:T(8,128)} %get-tuple-element.121, f32[6,16,128]{2,1,0:T(8,128)S(1)} %get-tuple-element.120, f32[6,16,128]{2,1,0:T(8,128)S(1)} %copy-done.20, f32[6,16,128,512]{3,2,1,0:T(8,128)} %get-tuple-element.113, pred[6,512]{1,0:T(8,128)(4,1)S(1)} %copy-done.19), kind=kLoop, calls=%fused_computation | loop fusion | flops 37748736 | bytes 63015936 | tf_op jit(solution)/shard_map/convert_element_type | solution.py:221
  690.0 4.2 multiply_convert_fusion.1
  694.1 2.2 copy-done
  696.3 8.8 copy.70
  705.2 11.0 fusion.50
  720.6 2.7 copy.80
  723.8 3.7 fusion.20
  727.5 2.6 copy.84
  730.2 36.3 %reduce-scatter.15.cloned.1.call-done = bf16[6,128,1024]{2,1,0:T(8,128)(2,1)} async-done(((bf16[6,512,1024]{2,1,0:T(8,128)(2,1)}), bf16[6,128,1024]{2,1,0:T(8,128)(2,1)}) %reduce-scatter.15.cloned.1.call-update) | async-done | bytes 1572880 | tf_op jit(solution)/shard_map/reduce_scatter | solution.py:238
  766.5 3.7 fusion.19
  770.2 2.6 copy.82
  772.9 5.3 convolution_convert_fusion.2
  778.3 12.1 convolution_convert_fusion.1
  791.8 11.8 convolution_convert_fusion
  806.7 29.4 %reduce-scatter.25.cloned.1.call-done = bf16[128,1024]{1,0:T(8,128)(2,1)} async-done(((bf16[1024,1024]{1,0:T(8,128)(2,1)}), bf16[128,1024]{1,0:T(8,128)(2,1)}) %reduce-scatter.25.cloned.1.call-update) | async-done | bytes 262160
  837.9 68.6 %reduce-scatter.29.cloned.1.call-done = bf16[128,1024]{1,0:T(8,128)(2,1)} async-done(((bf16[1024,1024]{1,0:T(8,128)(2,1)}), bf16[128,1024]{1,0:T(8,128)(2,1)}) %reduce-scatter.29.cloned.1.call-update) | async-done | bytes 262160
  908.4 68.7 %reduce-scatter.27.cloned.1.call-done = bf16[128,1024]{1,0:T(8,128)(2,1)} async-done(((bf16[1024,1024]{1,0:T(8,128)(2,1)}), bf16[128,1024]{1,0:T(8,128)(2,1)}) %reduce-scatter.27.cloned.1.call-update) | async-done | bytes 262160
  978.8 68.5 %reduce-scatter.19.cloned.1.call-done = bf16[128,1024]{1,0:T(8,128)(2,1)} async-done(((bf16[1024,1024]{1,0:T(8,128)(2,1)}), bf16[128,1024]{1,0:T(8,128)(2,1)}) %reduce-scatter.19.cloned.1.call-update) | async-done | bytes 262160 | tf_op jit(solution)/shard_map/reduce_scatter | solution.py:268
  1047.3 153.4 %reduce-scatter.21.cloned.1.call-done = bf16[128,4096]{1,0:T(8,128)(2,1)} async-done(((bf16[1024,4096]{1,0:T(8,128)(2,1)}), bf16[128,4096]{1,0:T(8,128)(2,1)}) %reduce-scatter.21.cloned.1.call-update) | async-done | bytes 1048592 | tf_op jit(solution)/shard_map/reduce_scatter | solution.py:271
  1200.7 151.9 %reduce-scatter.23.cloned.1.call-done = bf16[512,1024]{1,0:T(8,128)(2,1)} async-done(((bf16[4096,1024]{1,0:T(8,128)(2,1)}), bf16[512,1024]{1,0:T(8,128)(2,1)}) %reduce-scatter.23.cloned.1.call-update) | async-done | bytes 1048592 | tf_op jit(solution)/shard_map/reduce_scatter | solution.py:274
  1352.7 5.1 fusion.22
  1359.5 28.2 %all-reduce.9 = (bf16[1024]{0:T(1024)(128)(2,1)S(1)}, bf16[1024]{0:T(1024)(128)(2,1)S(1)}, bf16[1024]{0:T(1024)(128)(2,1)S(1)}, bf16[4096]{0:T(1024)(128)(2,1)S(...) all-reduce(bf16[1024]{0:T(1024)(128)(2,1)S(1)} %reduce_sum.216, ...), channel_id=10, replica_groups=mesh['ctx'=4,'fsdp'=8] {'fsdp'}, use_global_device_ids=true, to_apply=%region_26.27.clone | all-reduce | flops 12288 | bytes 49152
  1388.4 12.8 all-reduce.10
  1405.8 4.0 fusion.51
  1411.0 3.7 add_add_fusion.2
  1414.6 9.6 all-reduce.14.cloned.1.call-done
  (185 shorter events, 47.8 us)
Async XLA Ops:
  7.2 53.3 %all-gather.24.cloned.1.call-start = ((), (), s32[]{:S(2)}) async-start(), calls=%async_computation.11 | async-start | bytes 2359296 | tf_op jit(solution)/shard_map/all_gather | solution.py:87
  7.9 102.5 %all-gather.18.cloned.1.call-start = ((), (), s32[]{:S(2)}) async-start(), calls=%async_computation.8 | async-start | bytes 2359296 | tf_op jit(solution)/shard_map/all_gather | solution.py:88
  8.7 230.5 %all-gather.22.cloned.1.call-start = ((), (), s32[]{:S(2)}) async-start(), calls=%async_computation.10 | async-start | bytes 2359296 | tf_op jit(solution)/shard_map/all_gather | solution.py:86
  9.4 240.5 %all-gather.26.cloned.1.call-start = ((), (), s32[]{:S(2)}) async-start(), calls=%async_computation.12 | async-start | bytes 7864320 | tf_op jit(solution)/shard_map/all_gather | solution.py:132
  60.4 5.2 copy-start.30
  60.4 50.0 %copy-start.40 = (bf16[6,128,1024]{2,1,0:T(8,128)(2,1)S(1)}, bf16[6,128,1024]{2,1,0:T(8,128)(2,1)}, u32[]{:S(2)}) copy-start(bf16[6,128,1024]{2,1,0:T(8,128)(2,1)} %param.18) | copy-start | bytes 4718596
  65.6 220.7 %all-gather.20.cloned.1.call-start = ((), (), s32[]{:S(2)}) async-start(), calls=%async_computation.9 | async-start | bytes 7864320 | tf_op jit(solution)/shard_map/all_gather | solution.py:133
  114.9 2.2 copy-start.29
  114.9 2.3 copy-start.28
  114.9 2.3 copy-start.31
  114.9 17.6 %copy-start.32 = (bf16[128]{0:T(256)(128)(2,1)S(1)}, bf16[128]{0:T(256)(128)(2,1)}, u32[]{:S(2)}) copy-start(bf16[128]{0:T(256)(128)(2,1)} %param.29) | copy-start | bytes 772
  114.9 30.3 %copy-start.33 = (bf16[128]{0:T(256)(128)(2,1)S(1)}, bf16[128]{0:T(256)(128)(2,1)}, u32[]{:S(2)}) copy-start(bf16[128]{0:T(256)(128)(2,1)} %param.31) | copy-start | bytes 772
  114.9 45.9 %copy-start.34 = (bf16[128]{0:T(256)(128)(2,1)S(1)}, bf16[128]{0:T(256)(128)(2,1)}, u32[]{:S(2)}) copy-start(bf16[128]{0:T(256)(128)(2,1)} %param.32) | copy-start | bytes 772
  115.0 58.6 %copy-start.35 = (bf16[128]{0:T(256)(128)(2,1)S(1)}, bf16[128]{0:T(256)(128)(2,1)}, u32[]{:S(2)}) copy-start(bf16[128]{0:T(256)(128)(2,1)} %param.33) | copy-start | bytes 772
  115.0 73.1 %copy-start.36 = (bf16[128]{0:T(256)(128)(2,1)S(1)}, bf16[128]{0:T(256)(128)(2,1)}, u32[]{:S(2)}) copy-start(bf16[128]{0:T(256)(128)(2,1)} %param.34) | copy-start | bytes 772
  115.0 86.8 %copy-start.37 = (bf16[128]{0:T(256)(128)(2,1)S(1)}, bf16[128]{0:T(256)(128)(2,1)}, u32[]{:S(2)}) copy-start(bf16[128]{0:T(256)(128)(2,1)} %param.35) | copy-start | bytes 772
  115.0 196.0 %all-gather.28.cloned.1.call-start = ((), (), s32[]{:S(2)}) async-start(), calls=%async_computation.13 | async-start | bytes 2359296 | tf_op jit(solution)/shard_map/all_gather | solution.py:89
  115.6 317.7 %all-gather.30.cloned.1.call-start = ((), (), s32[]{:S(2)}) async-start(), calls=%async_computation.14 | async-start | bytes 9437184 | tf_op jit(solution)/shard_map/all_gather | solution.py:90
  116.3 442.2 %all-gather.32.cloned.1.call-start = ((), (), s32[]{:S(2)}) async-start(), calls=%async_computation.15 | async-start | bytes 9437184 | tf_op jit(solution)/shard_map/all_gather | solution.py:91
  117.1 606.7 %reduce-scatter.17.cloned.1.call-start = ((), (), s32[]{:S(2)}) async-start(), calls=%async_computation.17 | async-start | bytes 7864320 | tf_op jit(solution)/shard_map/reduce_scatter | solution.py:241
  117.3 177.7 %copy-start.18 = (pred[6,512]{1,0:T(8,128)(4,1)}, pred[6,512]{1,0:T(8,128)(4,1)S(1)}, u32[]{:S(2)}) copy-start(pred[6,512]{1,0:T(8,128)(4,1)S(1)} %iota_compare_fusion) | copy-start | bytes 9220
  249.9 9.3 copy-start.1
  315.8 242.8 %copy-start.7 = (f32[768,1024]{1,0:T(8,128)}, f32[768,1024]{1,0:T(8,128)S(1)}, u32[]{:S(2)}) copy-start(f32[768,1024]{1,0:T(8,128)S(1)} %get-tuple-element.115) | copy-start | bytes 9437188
  433.3 125.3 %copy-start.27 = (f32[8,1,128]{2,1,0:T(1,128)S(1)}, f32[8,1,128]{2,1,0:T(1,128)}, u32[]{:S(2)}) copy-start(f32[8,1,128]{2,1,0:T(1,128)} %convert_element_type.346) | copy-start | bytes 12292
  570.3 1.4 copy-start.3
  570.4 1.4 copy-start.21
  570.4 1.4 copy-start.22
  570.8 3.1 copy-start.23
  599.2 12.7 copy-start.8
  612.9 1.6 copy-start.5
  612.9 3.1 copy-start.39
  613.3 2.0 copy-start.14
  623.1 3.3 copy-start.19
  623.1 3.3 copy-start.20
  648.4 1.4 copy-start.10
  648.5 118.0 %reduce-scatter.15.cloned.1.call-start = ((), (), s32[]{:S(2)}) async-start(), calls=%async_computation.16 | async-start | bytes 7864320 | tf_op jit(solution)/shard_map/reduce_scatter | solution.py:238
  672.9 17.0 %copy-start.2 = (bf16[6,128,16,64]{1,3,2,0:T(8,128)(2,1)S(1)}, bf16[6,128,16,64]{1,3,2,0:T(8,128)(2,1)}, u32[]{:S(2)}) copy-start(bf16[6,128,16,64]{1,3,2,0:T(8,128)(2,1)} %copy-done.1) | copy-start | bytes 4718596
  690.0 6.4 copy-start
  705.1 131.0 %reduce-scatter.25.cloned.1.call-start = ((), (), s32[]{:S(2)}) async-start(), calls=%async_computation.21 | async-start | bytes 2359296
  716.2 2.6 copy-start.41
  717.5 1.3 copy-start.11
  723.3 183.3 %reduce-scatter.29.cloned.1.call-start = ((), (), s32[]{:S(2)}) async-start(), calls=%async_computation.23 | async-start | bytes 2359296
  730.1 246.9 %reduce-scatter.27.cloned.1.call-start = ((), (), s32[]{:S(2)}) async-start(), calls=%async_computation.22 | async-start | bytes 2359296
  772.8 5.5 copy-start.9
  772.8 274.4 %reduce-scatter.19.cloned.1.call-start = ((), (), s32[]{:S(2)}) async-start(), calls=%async_computation.18 | async-start | bytes 2359296 | tf_op jit(solution)/shard_map/reduce_scatter | solution.py:268
  778.3 422.4 %reduce-scatter.21.cloned.1.call-start = ((), (), s32[]{:S(2)}) async-start(), calls=%async_computation.19 | async-start | bytes 9437184 | tf_op jit(solution)/shard_map/reduce_scatter | solution.py:271
  790.4 1.4 copy-start.13
  790.5 562.2 %reduce-scatter.23.cloned.1.call-start = ((), (), s32[]{:S(2)}) async-start(), calls=%async_computation.20 | async-start | bytes 9437184 | tf_op jit(solution)/shard_map/reduce_scatter | solution.py:274
  803.7 0.7 copy-start.42
  803.7 2.5 copy-start.4
  803.7 2.5 copy-start.24
  803.7 620.6 %all-reduce.14.cloned.1.call-start = ((), (), s32[]{:S(2)}) async-start(), calls=%async_computation.24 | async-start | bytes 6291456 | tf_op jit(solution)/shard_map/psum | solution.py:306
  806.6 546.1 %copy-start.12 = (bf16[6,128,16,64]{1,0,3,2:T(8,128)(2,1)S(1)}, bf16[6,128,16,64]{1,0,3,2:T(8,128)(2,1)}, u32[]{:S(2)}) copy-start(bf16[6,128,16,64]{1,0,3,2:T(8,128)(2,1)} %copy-done.11) | copy-start | bytes 4718596
  1352.7 6.8 copy-start.25
  1352.7 6.8 copy-start.26
  1405.8 4.1 copy-start.6
  1405.8 4.1 copy-start.15
  1405.8 4.2 copy-start.38
  1405.8 5.1 copy-start.43
  1424.3 7.6 copy-start.17
  1424.3 9.1 copy-start.16
Sparse Core Ops, SparseCore 0:
  10.1 50.2 all-gather.23
  62.6 47.7 all-gather.17
  112.5 47.8 all-gather.21
  162.4 46.3 all-gather.25
  210.8 46.3 all-gather.19
  259.2 47.7 all-gather.27
  309.1 124.1 all-gather.29
  435.4 123.1 all-gather.31
  648.6 56.9 reduce-scatter.16
  708.1 58.3 reduce-scatter.14
  770.0 66.0 reduce-scatter.24
  839.5 67.0 reduce-scatter.28
  910.1 66.8 reduce-scatter.26
  980.4 66.8 reduce-scatter.18
  1050.8 149.8 reduce-scatter.20
  1204.6 147.9 reduce-scatter.22
  1355.9 68.3 all-reduce.13
where the time goes:
time: 1450 us; the launch traced here: 1440 us
  waiting for transfers between devices  874 us (60%)
  matrix products  237 us (16%)
  blocking collectives  176 us (12%)
  local copies, waits for them, and re-layouts  85.8 us (6%)
  other arithmetic  52.8 us (4%)
  between operations  16.1 us (1%)
    unnamed x20, waiting for transfers between devices  171 us
    reduce_scatter x1, waiting for transfers between devices, per_device(): lax.psum_scatter(hidden_derivative.astype(jnp.bfloat16), 'fsdp', scatter_...  153 us
    reduce_scatter x1, waiting for transfers between devices, per_device(): lax.psum_scatter(grad_outer.astype(jnp.bfloat16), 'fsdp', scatter_dimensi...  152 us
    all_gather x1, waiting for transfers between devices, per_device(): lax.all_gather(shards[4], 'fsdp', axis=0, tiled=True)  116 us
    all_gather x1, waiting for transfers between devices, per_device(): lax.all_gather(shards[5], 'fsdp', axis=0, tiled=True)  86.4 us
    reduce_scatter x1, waiting for transfers between devices, per_device(): lax.psum_scatter(grad_out.astype(jnp.bfloat16), 'fsdp', scatter_dimension...  68.5 us
    dot_general x5, matrix products, affine(): jnp.dot(first_factor_matrix, matrix, preferred_element_type=jnp.float32)  63.3 us
    all_gather x1, waiting for transfers between devices, per_device(): lax.all_gather(shards[1], 'fsdp', axis=0, tiled=True)  51 us
  transfers between devices with their start and end apart: 17, of which 12 were waited for; matrix products, arithmetic and copies ran while one was open for 19% of the time, Pallas kernels for 0%

commit v1 on v0

v1 whole, which is shorter than its diff:
```python
import functools

import jax
import jax.numpy as jnp
from jax import lax
from jax.experimental import pallas as pl
from jax.experimental.pallas import tpu as pltpu
from jax.sharding import PartitionSpec as P

HD = 64
EPSILON = 1e-05
BF = jnp.bfloat16
F32 = jnp.float32
ANY = pl.BlockSpec(memory_space=pl.ANY)
NT = (((1,), (1,)), ((), ()))
TN = (((0,), (0,)), ((), ()))
VMEM_LIMIT = 58 << 20


def dot(a, b):
    return jnp.dot(a, b, preferred_element_type=F32)


def dot_nt(a, b):
    return lax.dot_general(a, b, NT, preferred_element_type=F32)


def dot_tn(a, b):
    return lax.dot_general(a, b, TN, preferred_element_type=F32)


def params(**more):
    return pltpu.CompilerParams(vmem_limit_bytes=VMEM_LIMIT, **more)


def cost(flops, size, trans=0):
    return pl.CostEstimate(flops=int(flops), bytes_accessed=int(size), transcendentals=int(trans))


def qkv_kernel(n, ids, xm, xs, vec, *refs):
    pieces, (q, k, v, w), sem = refs[:n], refs[n : n + 4], refs[n + 4]
    step = pl.program_id(0)
    f = ids[1]
    rs = w.shape[1] // n

    def copies():
        out = []
        for i in range(n):
            at = pl.multiple_of((f ^ i) * rs, rs)
            for j in range(3):
                out.append(
                    pltpu.make_async_copy(
                        pieces[i].at[pl.ds(j * rs, rs)], w.at[j, pl.ds(at, rs)], sem.at[i * 3 + j]
                    )
                )
        return out

    @pl.when(step == 0)
    def _():
        todo = copies()
        for c in todo:
            c.start()
        for c in todo:
            c.wait()

    def do(x_ref):
        x = x_ref[...]
        q[0] = (dot(x, w[0]) + vec[0:1, :]).astype(BF)
        k[0] = dot(x, w[1]).astype(BF)
        v[0] = (dot(x, w[2]) + vec[1:2, :]).astype(BF)

    half = pl.num_programs(0) // 2

    @pl.when(step < half)
    def _():
        do(xm)

    @pl.when(step >= half)
    def _():
        do(xs)


def qkv_call(ids, xm, xs, vec, pieces):
    rows, width = xm.shape
    cols = pieces[0].shape[1]
    n = len(pieces)
    block = rows // 3
    grid_spec = pltpu.PrefetchScalarGridSpec(
        num_scalar_prefetch=1,
        grid=(6,),
        in_specs=[
            pl.BlockSpec((block, width), lambda i, s: (jnp.minimum(i, 2), 0)),
            pl.BlockSpec((block, width), lambda i, s: (jnp.maximum(i - 3, 0), 0)),
            pl.BlockSpec((8, cols), lambda i, s: (0, s[0] % 2)),
        ]
        + [ANY] * n,
        out_specs=[pl.BlockSpec((1, block, cols), lambda i, s: (i // 3, i % 3, 0))] * 3
        + [pl.BlockSpec((3, width, cols), lambda i, s: (0, 0, 0))],
        scratch_shapes=[pltpu.SemaphoreType.DMA((3 * n,))],
    )
    act = jax.ShapeDtypeStruct((2, rows, cols), BF)
    return pl.pallas_call(
        functools.partial(qkv_kernel, n),
        grid_spec=grid_spec,
        out_shape=[act, act, act, jax.ShapeDtypeStruct((3, width, cols), BF)],
        compiler_params=params(),
        cost_estimate=cost(2 * 2 * rows * width * cols * 3, 4 * rows * width + 12 * rows * cols),
        name="qkv",
    )(ids, xm, xs, vec, *pieces)


def lanes_of(shape, head):
    lane = lax.broadcasted_iota(jnp.int32, shape, 1)
    own = (lane < HD) if head == 0 else (lane >= HD)
    return lane, own, (HD if head == 0 else 0)


def split3(a):
    hi = a.astype(BF).astype(F32)
    mid = (a - hi).astype(BF).astype(F32)
    return hi, mid, a - hi - mid


def flat(ref):
    a = ref[...]
    return a.reshape(-1, a.shape[-1])


def attend_kernel(q_ref, k_ref, v_ref, mask_ref, cm_ref, cs_ref, lse_ref):
    q, k, v, mask = flat(q_ref), flat(k_ref), flat(v_ref), flat(mask_ref)
    out = []
    for head in range(2):
        lane, own, other = lanes_of(q.shape, head)
        qh = jnp.where(own, q * BF(HD**-0.5), jnp.where(lane == other, 1.0, 0.0).astype(BF))
        kh = jnp.where(own, k, mask)
        s = dot_nt(qh, kh)
        top = jnp.max(s, -1, keepdims=True)
        e = jnp.exp(s - top)
        total = jnp.sum(e, -1, keepdims=True)
        o = dot(e.astype(BF), v) * (1.0 / total)
        out.append((o, top + jnp.log(total), own))
    (o0, l0, own), (o1, l1, _) = out
    o = jnp.where(own, o0, o1).astype(BF)
    half = o.shape[0] // 2
    cm_ref[...] = o[:half].reshape(cm_ref.shape)
    cs_ref[...] = o[half:].reshape(cs_ref.shape)
    lse_ref[0] = jnp.where(own, l1, l0)


def attend_call(q, k, v, mask):
    slots, seqs, part, cols = q.shape
    pair = 2 * HD
    four = pl.BlockSpec((4, 1, part, pair), lambda s, h: (0, s, 0, h))
    two = pl.BlockSpec((2, 1, part, pair), lambda s, h: (0, s, 0, h))
    half = jax.ShapeDtypeStruct((2, seqs, part, cols), BF)
    full = slots * part
    return pl.pallas_call(
        attend_kernel,
        grid=(seqs, cols // pair),
        in_specs=[four, four, four, pl.BlockSpec((4, 1, part, pair), lambda s, h: (0, s, 0, 0))],
        out_specs=[two, two, pl.BlockSpec((1, full, pair), lambda s, h: (s, 0, h))],
        out_shape=[half, half, jax.ShapeDtypeStruct((seqs, full, cols), F32)],
        compiler_params=params(),
        cost_estimate=cost(
            4 * seqs * full * full * cols * 4, 14 * seqs * full * cols, seqs * full * full * cols // HD
        ),
        name="attend",
    )(q, k, v, mask)


def attend_back_kernel(
    q_ref, k_ref, v_ref, mask_ref, lse_ref, cm_ref, cs_ref, gm_ref, gs_ref, dq_ref, dk_ref, dv_ref
):
    q, k, v, mask = flat(q_ref), flat(k_ref), flat(v_ref), flat(mask_ref)
    lse = lse_ref[0]
    c = jnp.concatenate([flat(cm_ref), flat(cs_ref)], 0)
    g = jnp.concatenate([flat(gm_ref), flat(gs_ref)], 0)
    qs = q * BF(HD**-0.5)
    kt = k.T
    prod = c.astype(F32) * g.astype(F32)
    res = []
    for head in range(2):
        lane, own, o = lanes_of(q.shape, head)
        hi, mid, low = split3(-lse)
        extra = jnp.where(
            lane == o,
            1.0,
            jnp.where(
                lane == o + 1,
                hi,
                jnp.where(lane == o + 2, mid, jnp.where(lane == o + 3, low, 0.0)),
            ),
        ).astype(BF)
        qh = jnp.where(own, qs, extra)
        kh = jnp.where(own, k, jnp.where(lane == o, mask, BF(1)))
        p = jnp.exp(dot_nt(kh, qh))
        delta = jnp.sum(jnp.where(own, prod, 0.0), -1, keepdims=True)
        hi, mid, low = split3(-delta)
        extra = jnp.where(
            lane == o, hi, jnp.where(lane == o + 1, mid, jnp.where(lane == o + 2, low, 0.0))
        ).astype(BF)
        gh = jnp.where(own, g, extra)
        vh = jnp.where(own, v, BF(1))
        ds = (p * dot_nt(vh, gh)).astype(BF)
        dv = dot(p.astype(BF), g)
        dk = dot(ds, qs)
        dqt = dot(kt, ds)
        res.append((dv, dk, dqt, own))
    (dv0, dk0, dq0, own), (dv1, dk1, dq1, _) = res
    dv_ref[...] = jnp.where(own, dv0, dv1).astype(BF).reshape(dv_ref.shape)
    dk_ref[...] = jnp.where(own, dk0, dk1).astype(BF).reshape(dk_ref.shape)
    dqt = jnp.concatenate([dq0[:HD], dq1[HD:]], 0) * (HD**-0.5)
    dq_ref[...] = dqt.T.astype(BF).reshape(dq_ref.shape)


def attend_back_call(q, k, v, mask, lse, cm, cs, gm, gs):
    slots, seqs, part, cols = q.shape
    pair = 2 * HD
    four = pl.BlockSpec((4, 1, part, pair), lambda s, h: (0, s, 0, h))
    two = pl.BlockSpec((2, 1, part, pair), lambda s, h: (0, s, 0, h))
    full = slots * part
    out = jax.ShapeDtypeStruct(q.shape, BF)
    return pl.pallas_call(
        attend_back_kernel,
        grid=(seqs, cols // pair),
        in_specs=[
            four,
            four,
            four,
            pl.BlockSpec((4, 1, part, pair), lambda s, h: (0, s, 0, 0)),
            pl.BlockSpec((1, full, pair), lambda s, h: (s, 0, h)),
            two,
            two,
            two,
            two,
        ],
        out_specs=[four] * 3,
        out_shape=[out] * 3,
        compiler_params=params(),
        cost_estimate=cost(
            10 * seqs * full * full * cols * 4, 20 * seqs * full * cols, seqs * full * full * cols // HD
        ),
        name="attend_back",
    )(q, k, v, mask, lse, cm, cs, gm, gs)


def gelu_pair(u):
    e = jnp.exp(u * u * -0.5)
    t = 1.0 / (1.0 + (0.3275911 * 0.7071067811865476) * jnp.abs(u))
    poly = t * (
        0.254829592 * 0.5
        + t
        * (
            -0.284496736 * 0.5
            + t * (1.421413741 * 0.5 + t * (-1.453152027 * 0.5 + t * (1.061405429 * 0.5)))
        )
    )
    tail = poly * e
    cdf = jnp.where(u >= 0, 1.0 - tail, tail)
    ucdf = u * cdf
    return ucdf, cdf + u * (e * 0.3989422804014327)


def normalise(h):
    c = h - jnp.mean(h, -1, keepdims=True)
    r = lax.rsqrt(jnp.mean(c * c, -1, keepdims=True) + EPSILON)
    return c * r, r


def normalise_back(dyg, hat, r):
    return r * (
        dyg - jnp.mean(dyg, -1, keepdims=True) - hat * jnp.mean(dyg * hat, -1, keepdims=True)
    )


def ffn_kernel(n, ids, cm, cr, xm, cot, valid, vec, ib, *refs):
    pieces = refs[: 4 * n]
    lo, act, dout, dinn, nrm, dattn, dfirst, dco, dcs, acc = refs[4 * n : 4 * n + 10]
    wo, wi, wu, gp, sem = refs[4 * n + 10 :]
    width, ff = wi.shape
    core, f = ids[0] % 2, ids[1]
    step = pl.program_id(0)
    rs, ro = width // n, ff // n
    cq = ff // 4
    q_i, q_u, q_o = rs, ro // 4, rs // 4

    def copies(kind):
        out = []
        for e in range(4):
            qq = ids[0] ^ e
            for i in range(n):
                s = f ^ i
                ref = pieces[e * n + i]
                at = (kind * 4 + e) * n + i
                if kind == 0:
                    half = (s // (n // 2)) ^ core
                    to = half * (width // 2) + (s % (n // 2)) * rs + qq * q_o
                    src = ref.at[pl.ds(q_i + q_u, q_o)]
                    dst = wo.at[pl.ds(pl.multiple_of(to, q_o), q_o)]
                elif kind == 1:
                    src = ref.at[pl.ds(0, q_i)]
                    dst = wi.at[
                        pl.ds(pl.multiple_of(s * rs, rs), rs), pl.ds(pl.multiple_of(qq * cq, cq), cq)
                    ]
                else:
                    src = ref.at[pl.ds(q_i, q_u)]
                    dst = wu.at[pl.ds(pl.multiple_of(s * ro + qq * q_u, q_u), q_u)]
                out.append(pltpu.make_async_copy(src, dst, sem.at[at]))
        return out

    @pl.when(step == 0)
    def _():
        for kind in range(3):
            for c in copies(kind):
                c.start()
        acc[...] = jnp.zeros_like(acc)

    def arrived(kind):
        @pl.when(step == 0)
        def _():
            for c in copies(kind):
                c.wait()

    def add(row, value):
        acc[row : row + 1, :] += jnp.sum(value, 0, keepdims=True)

    arrived(0)
    hw = width // 2
    first = (
        xm[...].astype(F32) + (dot(cm[...], wo[:hw]) + dot(cr[...], wo[hw:])) + vec[2:3, :]
    )
    hat1, r1 = normalise(first)
    normed = hat1 * vec[4:5, :] + vec[5:6, :]
    low = normed.astype(BF)
    nrm[...] = low
    arrived(1)
    for j in range(4):
        cols = slice(j * cq, (j + 1) * cq)
        g, d = gelu_pair(dot(low, wi[:, cols]) + ib[:, cols])
        act[:, cols] = g.astype(BF)
        gp[:, cols] = d
    arrived(2)
    second = normed + (dot(act[...], wu[...]) + vec[3:4, :])
    hat2, r2 = normalise(second)
    lo[...] = (hat2 * vec[6:7, :] + vec[7:8, :]).astype(BF)
    og = cot[...].astype(F32) * valid[...]
    add(6, og * hat2)
    add(7, og)
    d2 = normalise_back(og * vec[6:7, :], hat2, r2)
    d2low = d2.astype(BF)
    dout[...] = d2low
    add(3, d2low.astype(F32))
    for j in range(4):
        cols = slice(j * cq, (j + 1) * cq)
        di = (dot_nt(d2low, wu[cols, :]) * gp[:, cols]).astype(BF)
        dinn[:, cols] = di
        add(8 + j, di.astype(F32))
    dn = d2 + dot_nt(dinn[...], wi[...])
    add(4, dn * hat1)
    add(5, dn)
    d1 = normalise_back(dn * vec[4:5, :], hat1, r1)
    dfirst[...] = d1
    d1low = d1.astype(BF)
    dattn[...] = d1low
    add(2, d1low.astype(F32))
    dc = dot_nt(d1low, wo[...]).astype(BF)
    dco[...] = dc[:, :hw]
    dcs[...] = dc[:, hw:]


def ffn_call(ids, cm, cr, xm, cot, valid, vec, ib, pieces):
    rows, width = xm.shape
    ff = ib.shape[1]
    n = len(pieces) // 4
    block = rows // 3
    hw = width // 2

    def by(cols):
        return pl.BlockSpec((block, cols), lambda i, s: (i, 0))

    def whole(a, b):
        return pl.BlockSpec((a, b), lambda i, s: (0, 0))

    grid_spec = pltpu.PrefetchScalarGridSpec(
        num_scalar_prefetch=1,
        grid=(3,),
        in_specs=[by(hw), by(hw), by(width), by(width), by(1), whole(8, width), whole(1, ff)]
        + [ANY] * (4 * n),
        out_specs=[
            by(width),
            by(ff),
            by(width),
            by(ff),
            by(width),
            by(width),
            by(width),
            by(hw),
            by(hw),
            whole(16, width),
        ],
        scratch_shapes=[
            pltpu.VMEM((width, width), BF),
            pltpu.VMEM((width, ff), BF),
            pltpu.VMEM((ff, width), BF),
            pltpu.VMEM((block, ff), F32),
            pltpu.SemaphoreType.DMA((12 * n,)),
        ],
    )

    def shape(cols, dtype=BF):
        return jax.ShapeDtypeStruct((rows, cols), dtype)

    return pl.pallas_call(
        functools.partial(ffn_kernel, n),
        grid_spec=grid_spec,
        out_shape=[
            shape(width),
            shape(ff),
            shape(width),
            shape(ff),
            shape(width),
            shape(width),
            shape(width, F32),
            shape(hw),
            shape(hw),
            jax.ShapeDtypeStruct((16, width), F32),
        ],
        compiler_params=params(),
        cost_estimate=cost(
            2 * rows * width * (2 * width + 4 * ff), 30 * rows * width + 2 * width * (2 * ff + width)
        ),
        name="ffn",
    )(ids, cm, cr, xm, cot, valid, vec, ib, *pieces)


def outer_grad_kernel(ids, act, dout, keep, send, tmp):
    tmp[...] = dot_tn(act[...], dout[...])
    size = keep.shape[3]
    for ec, ref in ((0, keep), (1, send)):
        for ex in range(2):
            at = pl.multiple_of((ids[0] ^ (2 * ex + ec)) * size, size)
            ref[ex, 0, 0] = tmp[pl.ds(at, size), :].astype(BF)


def outer_grad_call(ids, act, dout, n):
    rows, ff = act.shape
    width = dout.shape[1]
    ro = ff // n
    out = pl.BlockSpec((2, 1, 1, ro // 4, width), lambda i, s: (0, i % 2, i // 2, 0, 0))
    grid_spec = pltpu.PrefetchScalarGridSpec(
        num_scalar_prefetch=1,
        grid=(n,),
        in_specs=[
            pl.BlockSpec((rows, ro), lambda i, s: (0, s[1] ^ i)),
            pl.BlockSpec((rows, width), lambda i, s: (0, 0)),
        ],
        out_specs=[out, out],
        scratch_shapes=[pltpu.VMEM((ro, width), F32)],
    )
    shape = jax.ShapeDtypeStruct((2, 2, n // 2, ro // 4, width), BF)
    return pl.pallas_call(
        outer_grad_kernel,
        grid_spec=grid_spec,
        out_shape=[shape, shape],
        compiler_params=params(),
        cost_estimate=cost(2 * rows * ff * width, 2 * (rows * ff + rows * width + ff * width)),
        name="outer_grad",
    )(ids, act, dout)


def inner_grad_kernel(n, ids, nrm, dinn, keep, send, tmp):
    rs = nrm.shape[1] // n
    tmp[...] = dot_tn(nrm[...], dinn[...])

    def put(ref):
        for i in range(n):
            at = pl.multiple_of((ids[1] ^ i) * rs, rs)
            ref[0, i % 2, i // 2] = tmp[pl.ds(at, rs), :].astype(BF)

    @pl.when(pl.program_id(0) == 0)
    def _():
        put(send)

    @pl.when(pl.program_id(0) == 1)
    def _():
        put(keep)


def inner_grad_call(ids, nrm, dinn, n):
    rows, width = nrm.shape
    ff = dinn.shape[1]
    cq, rs = ff // 4, width // n
    block = (1, 2, n // 2, rs, cq)
    grid_spec = pltpu.PrefetchScalarGridSpec(
        num_scalar_prefetch=1,
        grid=(2, 2),
        in_specs=[
            pl.BlockSpec((rows, width), lambda a, ex, s: (0, 0)),
            pl.BlockSpec((rows, cq), lambda a, ex, s: (0, s[0] ^ (2 * ex + 1 - a))),
        ],
        out_specs=[
            pl.BlockSpec(block, lambda a, ex, s: (jnp.where(a == 1, ex, 0), 0, 0, 0, 0)),
            pl.BlockSpec(block, lambda a, ex, s: (jnp.where(a == 0, ex, 1), 0, 0, 0, 0)),
        ],
        scratch_shapes=[pltpu.VMEM((width, cq), F32)],
    )
    shape = jax.ShapeDtypeStruct((2, 2, n // 2, rs, cq), BF)
    return pl.pallas_call(
        functools.partial(inner_grad_kernel, n),
        grid_spec=grid_spec,
        out_shape=[shape, shape],
        compiler_params=params(),
        cost_estimate=cost(2 * rows * ff * width, 2 * (rows * ff + rows * width + ff * width)),
        name="inner_grad",
    )(ids, nrm, dinn)


def out_grad_kernel(n, ids, cm, cr, dattn, keep, send, tmp):
    width = tmp.shape[0]
    hw, rs = width // 2, width // n
    size = rs // 4
    g = dattn[...]
    tmp[:hw, :] = dot_tn(cm[...], g)
    tmp[hw:, :] = dot_tn(cr[...], g)
    for ec, ref in ((0, keep), (1, send)):
        for ex in range(2):
            for i in range(n):
                s = ids[1] ^ i
                half = (s // (n // 2)) ^ (ids[0] % 2)
                at = half * hw + (s % (n // 2)) * rs + (ids[0] ^ (2 * ex + ec)) * size
                ref[ex, i % 2, i // 2] = tmp[pl.ds(pl.multiple_of(at, size), size), :].astype(BF)


def out_grad_call(ids, cm, cr, dattn, n):
    rows, width = dattn.shape
    shape = jax.ShapeDtypeStruct((2, 2, n // 2, width // n // 4, width), BF)
    vm = pl.BlockSpec(memory_space=pltpu.VMEM)
    return pl.pallas_call(
        functools.partial(out_grad_kernel, n),
        in_specs=[pl.BlockSpec(memory_space=pltpu.SMEM), vm, vm, vm],
        out_specs=[vm, vm],
        out_shape=[shape, shape],
        scratch_shapes=[pltpu.VMEM((width, width), F32)],
        compiler_params=params(),
        cost_estimate=cost(2 * rows * width * width, 4 * rows * width + 2 * width * width),
        name="out_grad",
    )(ids, cm, cr, dattn)


def qkv_grad_kernel(n, ids, xm, xs, dm, ds, out, bias, tmp):
    tmp[...] = dot_tn(xm[...], dm[0]) + dot_tn(xs[...], ds[0])
    bias[...] = jnp.broadcast_to(
        jnp.sum(dm[0].astype(F32), 0, keepdims=True) + jnp.sum(ds[0].astype(F32), 0, keepdims=True),
        bias.shape,
    )
    rs = tmp.shape[0] // n
    for i in range(n):
        at = pl.multiple_of((ids[1] ^ i) * rs, rs)
        out[i % 2, i // 2] = tmp[pl.ds(at, rs), :].astype(BF)


def qkv_grad_call(ids, xm, xs, d, n):
    rows, width = xm.shape
    cols = d.shape[2]
    vm = pl.BlockSpec((rows, width), lambda i, s: (0, 0))
    shape = (2, n // 2, width // n, cols)
    grid_spec = pltpu.PrefetchScalarGridSpec(
        num_scalar_prefetch=1,
        grid=(1,),
        in_specs=[
            vm,
            vm,
            pl.BlockSpec((1, rows, cols), lambda i, s: (0, 0, 0)),
            pl.BlockSpec((1, rows, cols), lambda i, s: (1, 0, 0)),
        ],
        out_specs=[
            pl.BlockSpec(shape, lambda i, s: (0, 0, 0, 0)),
            pl.BlockSpec((8, cols), lambda i, s: (0, 0)),
        ],
        scratch_shapes=[pltpu.VMEM((width, cols), F32)],
    )
    return pl.pallas_call(
        functools.partial(qkv_grad_kernel, n),
        grid_spec=grid_spec,
        out_shape=[jax.ShapeDtypeStruct(shape, BF), jax.ShapeDtypeStruct((8, cols), F32)],
        compiler_params=params(),
        cost_estimate=cost(4 * rows * width * cols, 4 * rows * width + 4 * rows * cols),
        name="qkv_grad",
    )(ids, xm, xs, d, d)


def back_project_kernel(dq, dk, dv, w, out):
    out[...] = dot_nt(dq[0], w[0]) + dot_nt(dk[0], w[1]) + dot_nt(dv[0], w[2])


def back_project_call(which, dq, dk, dv, w):
    _, rows, cols = dq.shape
    width = w.shape[1]
    block = rows // 3
    one = pl.BlockSpec((1, block, cols), lambda i: (which, i, 0))
    return pl.pallas_call(
        back_project_kernel,
        grid=(3,),
        in_specs=[one, one, one, pl.BlockSpec((3, width, cols), lambda i: (0, 0, 0))],
        out_specs=pl.BlockSpec((block, width), lambda i: (i, 0)),
        out_shape=jax.ShapeDtypeStruct((rows, width), F32),
        compiler_params=params(),
        cost_estimate=cost(6 * rows * width * cols, 6 * rows * cols + 4 * rows * width + 6 * width * cols),
        name="back_project",
    )(dq, dk, dv, w)


def per_device(
    inputs,
    lengths,
    cotangent,
    query_weight,
    key_weight,
    value_weight,
    out_weight,
    inner_weight,
    outer_weight,
    query_bias,
    value_bias,
    out_bias,
    inner_bias,
    outer_bias,
    first_gain,
    first_shift,
    second_gain,
    second_shift,
):
    C = lax.axis_index("ctx")
    f = lax.axis_index("fsdp")
    nc, n = lax.axis_size("ctx"), lax.axis_size("fsdp")
    x, core = C // 2, C % 2
    ids = jnp.stack([C, f]).astype(jnp.int32)
    seqs, part, width = inputs.shape
    ff = inner_weight.shape[1]
    sh = seqs // 2
    rows = 2 * sh * part
    rs, ro = width // n, ff // n
    hw = width // 2
    A = n // 2

    def swap(a, dc, df):
        pairs = [
            (c * n + g, (c ^ dc) * n + (g ^ df)) for c in range(nc) for g in range(n)
        ]
        return lax.ppermute(a, ("ctx", "fsdp"), pairs)

    def half_seqs(a, which):
        return lax.dynamic_slice_in_dim(a, which * sh, sh, 0)

    def pick(bit, a, b):
        return jnp.where(bit == 0, a, b), jnp.where(bit == 0, b, a)

    def xor_order(items, index):
        items = list(items)
        step = 1
        while step < len(items):
            bit = (index // step) % 2
            items = [
                jnp.where(bit == 0, items[i], items[i ^ step]) for i in range(len(items))
            ]
            step *= 2
        return items

    def columns(w):
        return lax.dynamic_slice_in_dim(w, core * hw, hw, 1)

    def row_of(v):
        return jnp.pad(v.reshape(1, -1), ((0, 0), (0, hw - v.shape[0])))

    vectors = [
        query_bias,
        value_bias,
        out_bias,
        outer_bias,
        first_gain,
        first_shift,
        second_gain,
        second_shift,
        inner_bias,
    ]
    pack = jnp.concatenate(
        [columns(query_weight), columns(key_weight), columns(value_weight)]
        + [row_of(v) for v in vectors]
        + [jnp.zeros((16 - len(vectors), hw), BF)],
        0,
    )
    got = {0: pack, 1: swap(pack, 0, 1)}
    for k in range(1, A):
        got[2 * k] = swap(pack, 0, 2 * k)
    for k in range(1, A):
        got[2 * k + 1] = swap(got[2 * k], 0, 1)
    qkv_pieces = [got[i] for i in range(n)]

    x_mine, x_other = half_seqs(inputs, x), half_seqs(inputs, 1 - x)
    x_m = jnp.concatenate([x_mine[None], swap(x_other, 2, 0)[None]], 0)
    x_s = swap(x_m, 1, 0)
    xm, xs = x_m.reshape(rows, width), x_s.reshape(rows, width)

    small = xor_order([p[3 * rs : 3 * rs + 16] for p in qkv_pieces], f)
    vec = jnp.concatenate([p[:8, :rs] for p in small], 1).astype(F32)
    ib = jnp.concatenate([p[8:9, :ro] for p in small], 1).astype(F32)

    q, k, v, w_qkv = qkv_call(ids, xm, xs, vec, qkv_pieces)

    quarter_i = lax.dynamic_slice_in_dim(inner_weight, C * (ff // 4), ff // 4, 1)
    quarter_u = lax.dynamic_slice_in_dim(outer_weight, C * (ro // 4), ro // 4, 0)
    quarter_o = lax.dynamic_slice_in_dim(out_weight, C * (rs // 4), rs // 4, 0)
    ffn_pack = jnp.concatenate([quarter_i, quarter_u, quarter_o], 0)
    ffn_pack = lax.optimization_barrier((ffn_pack, got[n - 2]))[0]
    part0 = {0: ffn_pack, 1: swap(ffn_pack, 0, 1)}
    for kk in range(1, A):
        part0[2 * kk] = swap(ffn_pack, 0, 2 * kk)
    for kk in range(1, A):
        part0[2 * kk + 1] = swap(part0[2 * kk], 0, 1)
    part2 = {i: swap(part0[i], 2, 0) for i in range(n)}
    part1 = {i: swap(part0[i], 1, 0) for i in range(n)}
    part3 = {i: swap(part2[i], 1, 0) for i in range(n)}
    ffn_pieces = [p[i] for p in (part0, part1, part2, part3) for i in range(n)]

    c_mine, c_other = half_seqs(cotangent, x), half_seqs(cotangent, 1 - x)
    cot = jnp.concatenate([c_mine[None], swap(c_other, 2, 0)[None]], 0).reshape(rows, width)

    lens = half_seqs(lengths, x)
    order = jnp.stack([C ^ e for e in (0, 2, 1, 3)])
    positions = order[:, None, None] * part + jnp.arange(part)[None, None, :]
    inside = positions < lens[None, :, None]
    valid = inside[:2].astype(F32).reshape(rows, 1)
    mask = jnp.broadcast_to(
        jnp.where(inside, 0.0, -1e30).astype(BF)[..., None], (4, sh, part, 2 * HD)
    )

    four = (4, sh, part, hw)
    two = (2, sh, part, hw)
    q4, k4, v4 = q.reshape(four), k.reshape(four), v.reshape(four)
    c_m, c_s, lse = attend_call(q4, k4, v4, mask)
    c_r = swap(c_s, 1, 0)
    cm, cr = c_m.reshape(rows, hw), c_r.reshape(rows, hw)

    lo, act, dout, dinn, nrm, dattn, dfirst, dco, dcs, acc = ffn_call(
        ids, cm, cr, xm, cot, valid, vec, ib, ffn_pieces
    )

    def give_back(a):
        mine, theirs = a[0], swap(a[1], 2, 0)
        return jnp.concatenate(pick(x, mine, theirs), 0)

    layer_out = give_back(lo.reshape(2, sh, part, width))

    g_r = swap(dcs, 1, 0)

    def total(*items):
        out = items[0].astype(F32)
        for i in items[1:]:
            out = out + i.astype(F32)
        return out.astype(BF)

    def reduce_quarter(keep, send):
        got = swap(send, 1, 0)
        away = total(keep[1], got[1])
        near = total(keep[0], got[0])
        got = swap(away, 2, 0)
        away = total(near[1], got[1])
        near = total(near[0], got[0])
        got = swap(away, 0, 1)
        away = [total(near[a], got[a]) for a in range(A)]
        mine = total(away[0], *[swap(away[a], 0, 2 * a) for a in range(1, A)])
        other = swap(mine, 2, 0)
        quarters = [mine, swap(mine, 1, 0), other, swap(other, 1, 0)]
        return [a.astype(F32) for a in xor_order(quarters, C)]

    ku, su = outer_grad_call(ids, act, dout, n)
    ki, si = inner_grad_call(ids, nrm, dinn, n)
    ko, so = out_grad_call(ids, cm, cr, dattn, n)
    grad_outer = jnp.concatenate(reduce_quarter(ku, su), 0)
    grad_inner = jnp.concatenate(reduce_quarter(ki, si), 1)
    grad_out = jnp.concatenate(reduce_quarter(ko, so), 0)

    dq, dk, dv = attend_back_call(
        q4, k4, v4, mask, lse, c_m, c_s, dco.reshape(two), g_r.reshape(two)
    )
    flat3 = (2, rows, hw)
    dq, dk, dv = dq.reshape(flat3), dk.reshape(flat3), dv.reshape(flat3)

    def reduce_half(g):
        got = swap(g[1], 0, 1)
        away = [total(g[0, a], got[a]) for a in range(A)]
        mine = total(away[0], *[swap(away[a], 0, 2 * a) for a in range(1, A)])
        mine = total(mine, swap(mine, 2, 0))
        return jnp.concatenate(pick(core, mine, swap(mine, 1, 0)), 1).astype(F32)

    gq, bq = qkv_grad_call(ids, xm, xs, dq, n)
    gk, _ = qkv_grad_call(ids, xm, xs, dk, n)
    gv, bv = qkv_grad_call(ids, xm, xs, dv, n)
    grad_query, grad_key, grad_value = reduce_half(gq), reduce_half(gk), reduce_half(gv)

    halves = jnp.concatenate([bq[:1], bv[:1], jnp.zeros((14, hw), F32)], 0)
    none = jnp.zeros_like(halves)
    sums = acc + jnp.concatenate(pick(core, halves, none), 1)
    for dc, df in [(1, 0), (2, 0)] + [(0, 1 << b) for b in range(n.bit_length() - 1)]:
        sums = sums + swap(sums, dc, df)
    own = lax.dynamic_slice_in_dim(sums[:8], f * rs, rs, 1)
    own_inner = lax.dynamic_slice_in_dim(sums[8 : 8 + ff // width].reshape(ff), f * ro, ro, 0)

    theirs = back_project_call(1, dq, dk, dv, w_qkv)
    from_core = swap(theirs, 1, 0)
    own_part = back_project_call(0, dq, dk, dv, w_qkv)
    full = (dfirst + own_part + from_core).reshape(2, sh, part, width)
    away = swap(full[1].astype(BF), 2, 0).astype(F32)
    input_grad = jnp.concatenate(pick(x, full[0], away), 0)

    return (
        layer_out,
        input_grad,
        grad_query,
        grad_key,
        grad_value,
        grad_out,
        grad_inner,
        grad_outer,
        own[0],
        own[1],
        own[2],
        own_inner,
        own[3],
        own[4],
        own[5],
        own[6],
        own[7],
    )


def solution(mesh):
    rowed = P("fsdp", "ctx", None)
    matrix, vector = P("fsdp", None), P("fsdp")
    in_specs = (rowed, vector, rowed) + (matrix,) * 6 + (vector,) * 9
    out_specs = (rowed, rowed) + (matrix,) * 6 + (vector,) * 9
    return jax.shard_map(
        per_device, mesh=mesh, in_specs=in_specs, out_specs=out_specs, check_vma=False
    )
```

time: 1450 us -> 639 us (0.44)
  waiting for transfers between devices: 874 us -> 266 us
  matrix products: 237 us -> 0 us
  blocking collectives: 176 us -> 0 us
  Pallas kernels: 0 us -> 169 us
  starting transfers between devices: 1.26 us -> 127 us
  local copies, waits for them, and re-layouts: 85.8 us -> 31.7 us
  other arithmetic: 52.8 us -> 33.6 us
    reduce_scatter x5 -> x0, waiting for transfers between devices: 410 us -> none  [the longest x1 153 us: per_device(): lax.psum_scatter(hidden_derivative.astype(jnp.bfloat16), 'fsdp', scatter_...]
    all_gather x8 -> x0, waiting for transfers between devices: 283 us -> none  [the longest x1 116 us: per_device(): lax.all_gather(shards[4], 'fsdp', axis=0, tiled=True)]
    ppermute x0 -> x96, waiting for transfers between devices: none -> 266 us  [swap(): return lax.ppermute(a, ('ctx', 'fsdp'), pairs)]
    dot_general x24 -> x0, matrix products: 237 us -> none  [the longest x5 63.3 us: affine(): jnp.dot(first_factor_matrix, matrix, preferred_element_type=jnp.float32)]
    unnamed x20 -> x0, waiting for transfers between devices: 171 us -> none
    pallas_call x0 -> x12, Pallas kernels: none -> 169 us  [the longest x1 53.9 us: ffn_call(): pl.pallas_call(functools.partial(ffn_kernel, n), grid_spec=grid_spec, out...]
    all_gather x9 -> x0, blocking collectives: 135 us -> none  [the longest x1 21.6 us: per_device(): lax.all_gather(shards[9], 'fsdp', axis=0, tiled=True)]
    ppermute x0 -> x96, starting transfers between devices: none -> 127 us  [swap(): return lax.ppermute(a, ('ctx', 'fsdp'), pairs)]
  transfers between devices with their start and end apart: 17 -> 96, of which waited for: 12 -> 38; matrix products, arithmetic and copies ran while one was open for 19% -> 8% of each run, Pallas kernels for 0% -> 18%
where the time goes in v1:
time: 639 us; the launch traced here: 629 us
  waiting for transfers between devices  266 us (42%)
  Pallas kernels  169 us (26%)
  starting transfers between devices  127 us (20%)
  other arithmetic  33.6 us (5%)
  local copies, waits for them, and re-layouts  31.7 us (5%)
    ppermute x96, waiting for transfers between devices, swap(): return lax.ppermute(a, ('ctx', 'fsdp'), pairs)  266 us
    ppermute x96, starting transfers between devices, swap(): return lax.ppermute(a, ('ctx', 'fsdp'), pairs)  127 us
    pallas_call x1, Pallas kernels, ffn_call(): pl.pallas_call(functools.partial(ffn_kernel, n), grid_spec=grid_spec, out...  53.9 us
    pallas_call x1, Pallas kernels, attend_back_call(): pl.pallas_call(attend_back_kernel, grid=(seqs, cols // pair), in_specs=[f...  22.7 us
    pallas_call x3, Pallas kernels, qkv_grad_call(): pl.pallas_call(functools.partial(qkv_grad_kernel, n), grid_spec=grid_spec...  17.9 us
    pallas_call x1, Pallas kernels, attend_call(): pl.pallas_call(attend_kernel, grid=(seqs, cols // pair), in_specs=[four,...  15.8 us
    pallas_call x2, Pallas kernels, back_project_call(): pl.pallas_call(back_project_kernel, grid=(3,), in_specs=[one, one, one, p...  13.9 us
    convert_element_type x21, other arithmetic, total(): return out.astype(BF)  13.9 us
  transfers between devices with their start and end apart: 96, of which 38 were waited for; matrix products, arithmetic and copies ran while one was open for 8% of the time, Pallas kernels for 18%

profile of v1, /device:TPU:1, one launch (start us, length us, event | category | flops | bytes accessed | tf_op | source)
XLA Modules:
  0.0 628.9 jit_solution(11962422320032010368)
XLA Ops:
  9.6 2.2 collective-permute-start.3
  11.8 2.3 collective-permute-start.5
  16.5 2.4 dynamic-slice_bitcast_fusion
  21.3 2.7 concatenate.73
  24.0 1.7 reshape.555.valid
  30.6 10.0 %collective-permute-done.7.refs_6_ = bf16[400,512]{1,0:T(8,128)(2,1)} collective-permute-done((bf16[400,512]{1,0:T(8,128)(2,1)S(1)}, bf16[400,512]{1,0:T(8,128)(2,1)}, u32[]{:S(2)}, u32[]{:S(2)}) %collective-permute-start.7) | collective-permute-done | bytes 409632 | tf_op jit(solution)/shard_map/ppermute | solution.py:650
  42.8 7.4 %collective-permute-done.10 = bf16[3,128,1024]{2,1,0:T(8,128)(2,1)S(1)} collective-permute-done((bf16[3,128,1024]{2,1,0:T(8,128)(2,1)}, bf16[3,128,1024]{2,1,0:T(8,128)(2,1)S(1)}, u32[]{:S(2)}, u32[]{:S(2)}) %collective-permute-start.10) | collective-permute-done | bytes 786464 | tf_op jit(solution)/shard_map/ppermute | solution.py:650
  56.7 3.7 collective-permute-done.8.refs_7_
  62.1 11.3 %collective-permute-done.12.refs_2_ = bf16[288,1024]{1,0:T(8,128)(2,1)S(1)} collective-permute-done((bf16[288,1024]{1,0:T(8,128)(2,1)S(1)}, bf16[288,1024]{1,0:T(8,128)(2,1)S(1)}, u32[]{:S(2)}, u32[]{:S(2)}) %collective-permute-start.12) | collective-permute-done | bytes 589856 | tf_op jit(solution)/shard_map/ppermute | solution.py:650
  73.4 3.0 collective-permute-start.18
  77.7 12.6 %collective-permute-done.16.refs_6_ = bf16[288,1024]{1,0:T(8,128)(2,1)S(1)} collective-permute-done((bf16[288,1024]{1,0:T(8,128)(2,1)S(1)}, bf16[288,1024]{1,0:T(8,128)(2,1)S(1)}, u32[]{:S(2)}, u32[]{:S(2)}) %collective-permute-start.16) | collective-permute-done | bytes 589856 | tf_op jit(solution)/shard_map/ppermute | solution.py:650
  91.8 10.0 %collective-permute-start.1 = (bf16[2,3,128,1024]{3,2,1,0:T(8,128)(2,1)S(1)}, bf16[2,3,128,1024]{3,2,1,0:T(8,128)(2,1)S(1)}, u32[]{:S(2)}, u32[]{:S(2)}) collective-permute-start(bf16[2,3,128,1024]{3,2,1,0:T(8,128)(2,1)S(1)} %pad_maximum_fusion.1), channel_id=1, source_target_pairs={{0,8},{1,9},{2,10},{3,11},{4,12},{5,13},{6,14},{7,15},{8,0},{9,1},... | collective-permute-start | bytes 4718600 | tf_op jit(solution)/shard_map/ppermute | solution.py:650
  104.6 5.3 collective-permute-done.17.refs_7_
  111.8 43.0 %collective-permute-done.27.refs_17_ = bf16[288,1024]{1,0:T(8,128)(2,1)S(1)} collective-permute-done((bf16[288,1024]{1,0:T(8,128)(2,1)S(1)}, bf16[288,1024]{1,0:T(8,128)(2,1)S(1)}, u32[]{:S(2)}, u32[]{:S(2)}) %collective-permute-start.27) | collective-permute-done | bytes 589856 | tf_op jit(solution)/shard_map/ppermute | solution.py:650
  163.0 12.8 %qkv.1 = (bf16[2,768,512]{2,1,0:T(8,128)(2,1)}, bf16[2,768,512]{2,1,0:T(8,128)(2,1)}, bf16[2,768,512]{2,1,0:T(8,128)(2,1)}, bf16[3,1024,512]{2,1,0:T(8,128)(2,1)}) custom-call(s32[2]{0:T(128)} %pad_add_fusion.ids, bf16[768,1024]{1,0:T(8,128)(2,1)} %bitcast.294, bf16[768,1024]{1,0:T(8,128)(2,1)} %bitcast.311, f32[8,1024]{1,0:T(8,128)} %convert_element_type.729.vec, ...), custom_call_target="tpu_custom_call" | custom-call | flops 4831838208 | bytes 7864320 | tf_op jit(solution)/shard_map/qkv/pallas_call | solution.py:102
  176.6 9.0 %collective-permute-done.31.refs_21_ = bf16[288,1024]{1,0:T(8,128)(2,1)} collective-permute-done((bf16[288,1024]{1,0:T(8,128)(2,1)}, bf16[288,1024]{1,0:T(8,128)(2,1)}, u32[]{:S(2)}, u32[]{:S(2)}) %collective-permute-start.31) | collective-permute-done | bytes 589856 | tf_op jit(solution)/shard_map/ppermute | solution.py:650
  185.6 2.0 collective-permute-start.35
  187.6 10.6 %collective-permute-done.33.refs_23_ = bf16[288,1024]{1,0:T(8,128)(2,1)} collective-permute-done((bf16[288,1024]{1,0:T(8,128)(2,1)}, bf16[288,1024]{1,0:T(8,128)(2,1)}, u32[]{:S(2)}, u32[]{:S(2)}) %collective-permute-start.33) | collective-permute-done | bytes 589856 | tf_op jit(solution)/shard_map/ppermute | solution.py:650
  200.5 15.8 %attend.1 = (bf16[2,3,128,512]{3,2,1,0:T(8,128)(2,1)}, bf16[2,3,128,512]{3,2,1,0:T(8,128)(2,1)}, f32[3,512,512]{2,1,0:T(8,128)}) custom-call(bf16[4,3,128,512]{3,2,1,0:T(8,128)(2,1)} %bitcast.333, bf16[4,3,128,512]{3,2,1,0:T(8,128)(2,1)} %bitcast.335, bf16[4,3,128,512]{3,2,1,0:T(8,128)(2,1)} %bitcast.337, bf16[4,3,128,128]{3,2,1,0:T(8,128)(2,1)} %broadcast_in_dim.43.mask_ref), custom_call_target="tpu_custom_call" | custom-call | flops 6442450944 | bytes 11010048 | tf_op jit(solution)/shard_map/attend/pallas_call | solution.py:157
  218.6 1.8 collective-permute-done.40.refs_30_
  223.4 53.9 %ffn.1 = (bf16[768,1024]{1,0:T(8,128)(2,1)}, bf16[768,4096]{1,0:T(8,128)(2,1)}, bf16[768,1024]{1,0:T(8,128)(2,1)}, bf16[768,4096]{1,0:T(8,128)(2,1)}, bf16[768,1...) custom-call(s32[2]{0:T(128)} %pad_add_fusion.ids, ...), custom_call_target="tpu_custom_call" | custom-call | flops 28991029248 | bytes 42467328 | tf_op jit(solution)/shard_map/ffn/pallas_call | solution.py:413
  277.8 13.8 %outer_grad.1 = (bf16[2,2,4,128,1024]{4,3,2,1,0:T(8,128)(2,1)}, bf16[2,2,4,128,1024]{4,3,2,1,0:T(8,128)(2,1)}) custom-call(s32[2]{0:T(128)} %pad_add_fusion.ids, bf16[768,4096]{1,0:T(8,128)(2,1)} %get-tuple-element.74.act, bf16[768,1024]{1,0:T(8,128)(2,1)} %get-tuple-element.75.dout), custom_call_target="tpu_custom_call" | custom-call | flops 6442450944 | bytes 16252928 | tf_op jit(solution)/shard_map/outer_grad/pallas_call | solution.py:461
  291.7 13.0 %inner_grad.1 = (bf16[2,2,4,128,1024]{4,3,2,1,0:T(8,128)(2,1)}, bf16[2,2,4,128,1024]{4,3,2,1,0:T(8,128)(2,1)}) custom-call(s32[2]{0:T(128)} %pad_add_fusion.ids, bf16[768,1024]{1,0:T(8,128)(2,1)} %get-tuple-element.70.nrm, bf16[768,4096]{1,0:T(8,128)(2,1)} %get-tuple-element.71.dinn), custom_call_target="tpu_custom_call" | custom-call | flops 6442450944 | bytes 16252928 | tf_op jit(solution)/shard_map/inner_grad/pallas_call | solution.py:508
  305.1 5.1 out_grad.1
  313.1 22.7 %attend_back.1 = (bf16[4,3,128,512]{3,2,1,0:T(8,128)(2,1)}, bf16[4,3,128,512]{3,2,1,0:T(8,128)(2,1)}, bf16[4,3,128,512]{3,2,1,0:T(8,128)(2,1)}) custom-call(bf16[4,3,128,512]{3,2,1,0:T(8,128)(2,1)} %bitcast.334, bf16[4,3,128,512]{3,2,1,0:T(8,128)(2,1)} %bitcast.336, bf16[4,3,128,512]{3,2,1,0:T(8,128)(2,1)} %bitcast.338, ...), custom_call_target="tpu_custom_call" | custom-call | flops 16106127360 | bytes 15728640 | tf_op jit(solution)/shard_map/attend_back/pallas_call | solution.py:223
  335.8 5.9 qkv_grad.3
  342.4 6.1 qkv_grad.5
  350.0 1.9 slice_bitcast_fusion.4
  351.9 5.9 qkv_grad.4
  358.1 2.2 broadcast_select_fusion.1
  362.3 7.1 %back_project.3 = f32[768,1024]{1,0:T(8,128)} custom-call(bf16[2,768,512]{2,1,0:T(8,128)(2,1)} %bitcast.301, bf16[2,768,512]{2,1,0:T(8,128)(2,1)} %bitcast.305, bf16[2,768,512]{2,1,0:T(8,128)(2,1)} %bitcast.309, bf16[3,1024,512]{2,1,0:T(8,128)(2,1)} %get-tuple-element.63.w), custom_call_target="tpu_custom_call" | custom-call | flops 2415919104 | bytes 8650752 | tf_op jit(solution)/shard_map/back_project/pallas_call | solution.py:601
  370.8 6.8 %back_project.2 = f32[768,1024]{1,0:T(8,128)} custom-call(bf16[2,768,512]{2,1,0:T(8,128)(2,1)} %bitcast.302, bf16[2,768,512]{2,1,0:T(8,128)(2,1)} %bitcast.306, bf16[2,768,512]{2,1,0:T(8,128)(2,1)} %bitcast.310, bf16[3,1024,512]{2,1,0:T(8,128)(2,1)} %get-tuple-element.63.w), custom_call_target="tpu_custom_call" | custom-call | flops 2415919104 | bytes 8650752 | tf_op jit(solution)/shard_map/back_project/pallas_call | solution.py:601
  377.6 8.3 %collective-permute-start.94 = (f32[16,1024]{1,0:T(8,128)S(1)}, f32[16,1024]{1,0:T(8,128)S(1)}, u32[]{:S(2)}, u32[]{:S(2)}) collective-permute-start(f32[16,1024]{1,0:T(8,128)S(1)} %add.384), channel_id=1, source_target_pairs={{0,2},{1,3},{2,0},{3,1},{4,6},{5,7},{6,4},{7,5},{8,10},{9,11},{10,... | collective-permute-start | bytes 196616 | tf_op jit(solution)/shard_map/ppermute | solution.py:650
  388.9 2.5 collective-permute-start.95
  391.4 1.8 add_convert_fusion.5
  397.2 2.0 collective-permute-done.52
  399.3 2.2 collective-permute-start.60
  401.6 8.9 %collective-permute-done.46 = bf16[4,128,512]{2,1,0:T(8,128)(2,1)S(1)} collective-permute-done((bf16[4,128,512]{2,1,0:T(8,128)(2,1)S(1)}, bf16[4,128,512]{2,1,0:T(8,128)(2,1)S(1)}, u32[]{:S(2)}, u32[]{:S(2)}) %collective-permute-start.46) | collective-permute-done | bytes 524320 | tf_op jit(solution)/shard_map/ppermute | solution.py:650
  410.5 2.2 collective-permute-start.61
  414.2 2.2 collective-permute-done.61
  417.6 2.0 collective-permute-done.53
  422.8 2.5 collective-permute-done.55
  425.3 3.2 collective-permute-start.48
  429.8 2.7 collective-permute-done.48
  432.5 10.4 %collective-permute-start.44 = (f32[768,1024]{1,0:T(8,128)S(1)}, f32[768,1024]{1,0:T(8,128)S(1)}, u32[]{:S(2)}, u32[]{:S(2)}) collective-permute-start(f32[768,1024]{1,0:T(8,128)S(1)} %copy-done.9), channel_id=1, source_target_pairs={{0,8},{1,9},{2,10},{3,11},{4,12},{5,13},{6,14},{7,15},{8,0},{9,1},... | collective-permute-start | bytes 9437192 | tf_op jit(solution)/shard_map/ppermute | solution.py:650
  444.7 2.0 collective-permute-done.62
  448.1 3.7 add_convert_fusion.1
  453.3 2.2 add_convert_fusion.3
  455.7 5.5 collective-permute-start.63
  470.4 2.5 collective-permute-done.68
  473.6 1.7 collective-permute-start.71
  476.2 2.3 collective-permute-start.70
  478.5 63.9 %collective-permute-done.71 = bf16[32,1024]{1,0:T(8,128)(2,1)S(1)} collective-permute-done((bf16[32,1024]{1,0:T(8,128)(2,1)S(1)}, bf16[32,1024]{1,0:T(8,128)(2,1)S(1)}, u32[]{:S(2)}, u32[]{:S(2)}) %collective-permute-start.71) | collective-permute-done | bytes 65568 | tf_op jit(solution)/shard_map/ppermute | solution.py:650
  542.4 4.8 collective-permute-start.72
  554.2 19.0 %collective-permute-done.84 = bf16[4,128,1024]{2,1,0:T(8,128)(2,1)S(1)} collective-permute-done((bf16[4,128,1024]{2,1,0:T(8,128)(2,1)S(1)}, bf16[4,128,1024]{2,1,0:T(8,128)(2,1)S(1)}, u32[]{:S(2)}, u32[]{:S(2)}) %collective-permute-start.84) | collective-permute-done | bytes 1048608 | tf_op jit(solution)/shard_map/ppermute | solution.py:650
  574.5 2.6 collective-permute-start.87
  577.9 17.7 %collective-permute-done.75 = bf16[4,128,1024]{2,1,0:T(8,128)(2,1)S(1)} collective-permute-done((bf16[4,128,1024]{2,1,0:T(8,128)(2,1)S(1)}, bf16[4,128,1024]{2,1,0:T(8,128)(2,1)S(1)}, u32[]{:S(2)}, u32[]{:S(2)}) %collective-permute-start.75) | collective-permute-done | bytes 1048608 | tf_op jit(solution)/shard_map/ppermute | solution.py:650
  597.0 2.6 collective-permute-start.78
  600.3 7.4 %collective-permute-done.76 = bf16[128,1024]{1,0:T(8,128)(2,1)S(1)} collective-permute-done((bf16[128,1024]{1,0:T(8,128)(2,1)S(1)}, bf16[128,1024]{1,0:T(8,128)(2,1)S(1)}, u32[]{:S(2)}, u32[]{:S(2)}) %collective-permute-start.76) | collective-permute-done | bytes 262176 | tf_op jit(solution)/shard_map/ppermute | solution.py:650
  607.6 1.7 collective-permute-start.88
  609.3 5.6 collective-permute-done.78
  616.1 3.8 collective-permute-start.90
  620.4 2.0 pad_maximum_fusion
  622.4 2.9 collective-permute-start.81
  (380 shorter events, 108.2 us)
Async XLA Ops:
  9.6 19.5 %collective-permute-start.3 = (bf16[400,512]{1,0:T(8,128)(2,1)S(1)}, bf16[400,512]{1,0:T(8,128)(2,1)}, u32[]{:S(2)}, u32[]{:S(2)}) collective-permute-start(bf16[400,512]{1,0:T(8,128)(2,1)S(1)} %concatenate.74.refs_0_), channel_id=1, source_target_pairs={{0,2},{1,3},{2,0},{3,1},{4,6},{5,7},{6,4},{7,5},{8,10},{9,11},{10,... | collective-permute-start | bytes 1228808 | tf_op jit(solution)/shard_map/ppermute | solution.py:650
  11.8 18.4 %collective-permute-start.5 = (bf16[400,512]{1,0:T(8,128)(2,1)S(1)}, bf16[400,512]{1,0:T(8,128)(2,1)}, u32[]{:S(2)}, u32[]{:S(2)}) collective-permute-start(bf16[400,512]{1,0:T(8,128)(2,1)S(1)} %concatenate.74.refs_0_), channel_id=1, source_target_pairs={{0,4},{1,5},{2,6},{3,7},{4,0},{5,1},{6,2},{7,3},{8,12},{9,13},{10,... | collective-permute-start | bytes 1228808 | tf_op jit(solution)/shard_map/ppermute | solution.py:650
  14.1 26.5 %collective-permute-start.7 = (bf16[400,512]{1,0:T(8,128)(2,1)S(1)}, bf16[400,512]{1,0:T(8,128)(2,1)}, u32[]{:S(2)}, u32[]{:S(2)}) collective-permute-start(bf16[400,512]{1,0:T(8,128)(2,1)S(1)} %concatenate.74.refs_0_), channel_id=1, source_target_pairs={{0,6},{1,7},{2,4},{3,5},{4,2},{5,3},{6,0},{7,1},{8,14},{9,15},{10,... | collective-permute-start | bytes 1228808 | tf_op jit(solution)/shard_map/ppermute | solution.py:650
  15.2 26.6 %collective-permute-start = (bf16[3,128,1024]{2,1,0:T(8,128)(2,1)}, bf16[3,128,1024]{2,1,0:T(8,128)(2,1)S(1)}, u32[]{:S(2)}, u32[]{:S(2)}) collective-permute-start(bf16[3,128,1024]{2,1,0:T(8,128)(2,1)} %get-tuple-element.132), channel_id=1, source_target_pairs={{0,16},{1,17},{2,18},{3,19},{4,20},{5,21},{6,22},{7,23},{8,24},{9,... | collective-permute-start | bytes 2359304 | tf_op jit(solution)/shard_map/ppermute | solution.py:650
  18.9 31.2 %collective-permute-start.10 = (bf16[3,128,1024]{2,1,0:T(8,128)(2,1)}, bf16[3,128,1024]{2,1,0:T(8,128)(2,1)S(1)}, u32[]{:S(2)}, u32[]{:S(2)}) collective-permute-start(bf16[3,128,1024]{2,1,0:T(8,128)(2,1)} %get-tuple-element.130), channel_id=1, source_target_pairs={{0,16},{1,17},{2,18},{3,19},{4,20},{5,21},{6,22},{7,23},{8,24},{9,... | collective-permute-start | bytes 2359304 | tf_op jit(solution)/shard_map/ppermute | solution.py:650
  29.1 24.0 %collective-permute-start.2 = (bf16[400,512]{1,0:T(8,128)(2,1)S(1)}, bf16[400,512]{1,0:T(8,128)(2,1)S(1)}, u32[]{:S(2)}, u32[]{:S(2)}) collective-permute-start(bf16[400,512]{1,0:T(8,128)(2,1)S(1)} %concatenate.74.refs_0_), channel_id=1, source_target_pairs={{0,1},{1,0},{2,3},{3,2},{4,5},{5,4},{6,7},{7,6},{8,9},{9,8},{10,11... | collective-permute-start | bytes 1228808 | tf_op jit(solution)/shard_map/ppermute | solution.py:650
  30.2 24.5 %collective-permute-start.4 = (bf16[400,512]{1,0:T(8,128)(2,1)}, bf16[400,512]{1,0:T(8,128)(2,1)S(1)}, u32[]{:S(2)}, u32[]{:S(2)}) collective-permute-start(bf16[400,512]{1,0:T(8,128)(2,1)} %collective-permute-done.3.refs_2_), channel_id=1, source_target_pairs={{0,1},{1,0},{2,3},{3,2},{4,5},{5,4},{6,7},{7,6},{8,9},{9,8},{10,11... | collective-permute-start | bytes 1228808 | tf_op jit(solution)/shard_map/ppermute | solution.py:650
  40.5 14.9 %collective-permute-start.6 = (bf16[400,512]{1,0:T(8,128)(2,1)}, bf16[400,512]{1,0:T(8,128)(2,1)S(1)}, u32[]{:S(2)}, u32[]{:S(2)}) collective-permute-start(bf16[400,512]{1,0:T(8,128)(2,1)} %collective-permute-done.5.refs_4_), channel_id=1, source_target_pairs={{0,1},{1,0},{2,3},{3,2},{4,5},{5,4},{6,7},{7,6},{8,9},{9,8},{10,11... | collective-permute-start | bytes 1228808 | tf_op jit(solution)/shard_map/ppermute | solution.py:650
  41.8 18.5 %collective-permute-start.8 = (bf16[400,512]{1,0:T(8,128)(2,1)}, bf16[400,512]{1,0:T(8,128)(2,1)S(1)}, u32[]{:S(2)}, u32[]{:S(2)}) collective-permute-start(bf16[400,512]{1,0:T(8,128)(2,1)} %collective-permute-done.7.refs_6_), channel_id=1, source_target_pairs={{0,1},{1,0},{2,3},{3,2},{4,5},{5,4},{6,7},{7,6},{8,9},{9,8},{10,11... | collective-permute-start | bytes 1228808 | tf_op jit(solution)/shard_map/ppermute | solution.py:650
  50.1 23.3 %collective-permute-start.12 = (bf16[288,1024]{1,0:T(8,128)(2,1)S(1)}, bf16[288,1024]{1,0:T(8,128)(2,1)S(1)}, u32[]{:S(2)}, u32[]{:S(2)}) collective-permute-start(bf16[288,1024]{1,0:T(8,128)(2,1)S(1)} %pad_maximum_fusion.4.refs_0_), channel_id=1, source_target_pairs={{0,2},{1,3},{2,0},{3,1},{4,6},{5,7},{6,4},{7,5},{8,10},{9,11},{10,... | collective-permute-start | bytes 1769480 | tf_op jit(solution)/shard_map/ppermute | solution.py:650
  53.1 23.4 %collective-permute-start.14 = (bf16[288,1024]{1,0:T(8,128)(2,1)S(1)}, bf16[288,1024]{1,0:T(8,128)(2,1)S(1)}, u32[]{:S(2)}, u32[]{:S(2)}) collective-permute-start(bf16[288,1024]{1,0:T(8,128)(2,1)S(1)} %pad_maximum_fusion.4.refs_0_), channel_id=1, source_target_pairs={{0,4},{1,5},{2,6},{3,7},{4,0},{5,1},{6,2},{7,3},{8,12},{9,13},{10,... | collective-permute-start | bytes 1769480 | tf_op jit(solution)/shard_map/ppermute | solution.py:650
  54.7 35.6 %collective-permute-start.16 = (bf16[288,1024]{1,0:T(8,128)(2,1)S(1)}, bf16[288,1024]{1,0:T(8,128)(2,1)S(1)}, u32[]{:S(2)}, u32[]{:S(2)}) collective-permute-start(bf16[288,1024]{1,0:T(8,128)(2,1)S(1)} %pad_maximum_fusion.4.refs_0_), channel_id=1, source_target_pairs={{0,6},{1,7},{2,4},{3,5},{4,2},{5,3},{6,0},{7,1},{8,14},{9,15},{10,... | collective-permute-start | bytes 1769480 | tf_op jit(solution)/shard_map/ppermute | solution.py:650
  55.4 36.1 %collective-permute-start.11 = (bf16[288,1024]{1,0:T(8,128)(2,1)S(1)}, bf16[288,1024]{1,0:T(8,128)(2,1)S(1)}, u32[]{:S(2)}, u32[]{:S(2)}) collective-permute-start(bf16[288,1024]{1,0:T(8,128)(2,1)S(1)} %pad_maximum_fusion.4.refs_0_), channel_id=1, source_target_pairs={{0,1},{1,0},{2,3},{3,2},{4,5},{5,4},{6,7},{7,6},{8,9},{9,8},{10,11... | collective-permute-start | bytes 1769480 | tf_op jit(solution)/shard_map/ppermute | solution.py:650
  60.3 31.5 %collective-permute-start.26 = (bf16[288,1024]{1,0:T(8,128)(2,1)S(1)}, bf16[288,1024]{1,0:T(8,128)(2,1)}, u32[]{:S(2)}, u32[]{:S(2)}) collective-permute-start(bf16[288,1024]{1,0:T(8,128)(2,1)S(1)} %pad_maximum_fusion.4.refs_0_), channel_id=1, source_target_pairs={{0,16},{1,17},{2,18},{3,19},{4,20},{5,21},{6,22},{7,23},{8,24},{9,... | collective-permute-start | bytes 1769480 | tf_op jit(solution)/shard_map/ppermute | solution.py:650
  73.4 28.4 %collective-permute-start.18 = (bf16[288,1024]{1,0:T(8,128)(2,1)S(1)}, bf16[288,1024]{1,0:T(8,128)(2,1)S(1)}, u32[]{:S(2)}, u32[]{:S(2)}) collective-permute-start(bf16[288,1024]{1,0:T(8,128)(2,1)S(1)} %pad_maximum_fusion.4.refs_0_), channel_id=1, source_target_pairs={{0,8},{1,9},{2,10},{3,11},{4,12},{5,13},{6,14},{7,15},{8,0},{9,1},... | collective-permute-start | bytes 1769480 | tf_op jit(solution)/shard_map/ppermute | solution.py:650
  76.5 26.7 %collective-permute-start.13 = (bf16[288,1024]{1,0:T(8,128)(2,1)S(1)}, bf16[288,1024]{1,0:T(8,128)(2,1)}, u32[]{:S(2)}, u32[]{:S(2)}) collective-permute-start(bf16[288,1024]{1,0:T(8,128)(2,1)S(1)} %collective-permute-done.12.refs_2_), channel_id=1, source_target_pairs={{0,1},{1,0},{2,3},{3,2},{4,5},{5,4},{6,7},{7,6},{8,9},{9,8},{10,11... | collective-permute-start | bytes 1769480 | tf_op jit(solution)/shard_map/ppermute | solution.py:650
  90.3 13.1 %collective-permute-start.15 = (bf16[288,1024]{1,0:T(8,128)(2,1)S(1)}, bf16[288,1024]{1,0:T(8,128)(2,1)}, u32[]{:S(2)}, u32[]{:S(2)}) collective-permute-start(bf16[288,1024]{1,0:T(8,128)(2,1)S(1)} %collective-permute-done.14.refs_4_), channel_id=1, source_target_pairs={{0,1},{1,0},{2,3},{3,2},{4,5},{5,4},{6,7},{7,6},{8,9},{9,8},{10,11... | collective-permute-start | bytes 1769480 | tf_op jit(solution)/shard_map/ppermute | solution.py:650
  91.6 18.4 %collective-permute-start.17 = (bf16[288,1024]{1,0:T(8,128)(2,1)S(1)}, bf16[288,1024]{1,0:T(8,128)(2,1)}, u32[]{:S(2)}, u32[]{:S(2)}) collective-permute-start(bf16[288,1024]{1,0:T(8,128)(2,1)S(1)} %collective-permute-done.16.refs_6_), channel_id=1, source_target_pairs={{0,1},{1,0},{2,3},{3,2},{4,5},{5,4},{6,7},{7,6},{8,9},{9,8},{10,11... | collective-permute-start | bytes 1769480 | tf_op jit(solution)/shard_map/ppermute | solution.py:650
  91.8 70.0 %collective-permute-start.1 = (bf16[2,3,128,1024]{3,2,1,0:T(8,128)(2,1)S(1)}, bf16[2,3,128,1024]{3,2,1,0:T(8,128)(2,1)S(1)}, u32[]{:S(2)}, u32[]{:S(2)}) collective-permute-start(bf16[2,3,128,1024]{3,2,1,0:T(8,128)(2,1)S(1)} %pad_maximum_fusion.1), channel_id=1, source_target_pairs={{0,8},{1,9},{2,10},{3,11},{4,12},{5,13},{6,14},{7,15},{8,0},{9,1},... | collective-permute-start | bytes 4718600 | tf_op jit(solution)/shard_map/ppermute | solution.py:650
  101.9 53.7 %collective-permute-start.28 = (bf16[288,1024]{1,0:T(8,128)(2,1)S(1)}, bf16[288,1024]{1,0:T(8,128)(2,1)S(1)}, u32[]{:S(2)}, u32[]{:S(2)}) collective-permute-start(bf16[288,1024]{1,0:T(8,128)(2,1)S(1)} %collective-permute-done.12.refs_2_), channel_id=1, source_target_pairs={{0,16},{1,17},{2,18},{3,19},{4,20},{5,21},{6,22},{7,23},{8,24},{9,... | collective-permute-start | bytes 1769480 | tf_op jit(solution)/shard_map/ppermute | solution.py:650
  103.2 52.5 %collective-permute-start.30 = (bf16[288,1024]{1,0:T(8,128)(2,1)S(1)}, bf16[288,1024]{1,0:T(8,128)(2,1)S(1)}, u32[]{:S(2)}, u32[]{:S(2)}) collective-permute-start(bf16[288,1024]{1,0:T(8,128)(2,1)S(1)} %collective-permute-done.14.refs_4_), channel_id=1, source_target_pairs={{0,16},{1,17},{2,18},{3,19},{4,20},{5,21},{6,22},{7,23},{8,24},{9,... | collective-permute-start | bytes 1769480 | tf_op jit(solution)/shard_map/ppermute | solution.py:650
  103.4 52.7 %collective-permute-start.32 = (bf16[288,1024]{1,0:T(8,128)(2,1)S(1)}, bf16[288,1024]{1,0:T(8,128)(2,1)S(1)}, u32[]{:S(2)}, u32[]{:S(2)}) collective-permute-start(bf16[288,1024]{1,0:T(8,128)(2,1)S(1)} %collective-permute-done.16.refs_6_), channel_id=1, source_target_pairs={{0,16},{1,17},{2,18},{3,19},{4,20},{5,21},{6,22},{7,23},{8,24},{9,... | collective-permute-start | bytes 1769480 | tf_op jit(solution)/shard_map/ppermute | solution.py:650
  110.0 44.8 %collective-permute-start.27 = (bf16[288,1024]{1,0:T(8,128)(2,1)S(1)}, bf16[288,1024]{1,0:T(8,128)(2,1)S(1)}, u32[]{:S(2)}, u32[]{:S(2)}) collective-permute-start(bf16[288,1024]{1,0:T(8,128)(2,1)S(1)} %collective-permute-done.11.refs_1_), channel_id=1, source_target_pairs={{0,16},{1,17},{2,18},{3,19},{4,20},{5,21},{6,22},{7,23},{8,24},{9,... | collective-permute-start | bytes 1769480 | tf_op jit(solution)/shard_map/ppermute | solution.py:650
  157.2 18.5 %collective-permute-start.34 = (bf16[288,1024]{1,0:T(8,128)(2,1)}, bf16[288,1024]{1,0:T(8,128)(2,1)}, u32[]{:S(2)}, u32[]{:S(2)}) collective-permute-start(bf16[288,1024]{1,0:T(8,128)(2,1)} %collective-permute-done.26.refs_16_), channel_id=1, source_target_pairs={{0,8},{1,9},{2,10},{3,11},{4,12},{5,13},{6,14},{7,15},{8,0},{9,1},... | collective-permute-start | bytes 1769480 | tf_op jit(solution)/shard_map/ppermute | solution.py:650
  158.1 18.4 %collective-permute-start.29 = (bf16[288,1024]{1,0:T(8,128)(2,1)}, bf16[288,1024]{1,0:T(8,128)(2,1)}, u32[]{:S(2)}, u32[]{:S(2)}) collective-permute-start(bf16[288,1024]{1,0:T(8,128)(2,1)} %collective-permute-done.13.refs_3_), channel_id=1, source_target_pairs={{0,16},{1,17},{2,18},{3,19},{4,20},{5,21},{6,22},{7,23},{8,24},{9,... | collective-permute-start | bytes 1769480 | tf_op jit(solution)/shard_map/ppermute | solution.py:650
  159.3 40.1 %collective-permute-start.21 = (bf16[288,1024]{1,0:T(8,128)(2,1)}, bf16[288,1024]{1,0:T(8,128)(2,1)}, u32[]{:S(2)}, u32[]{:S(2)}) collective-permute-start(bf16[288,1024]{1,0:T(8,128)(2,1)} %collective-permute-done.13.refs_3_), channel_id=1, source_target_pairs={{0,8},{1,9},{2,10},{3,11},{4,12},{5,13},{6,14},{7,15},{8,0},{9,1},... | collective-permute-start | bytes 1769480 | tf_op jit(solution)/shard_map/ppermute | solution.py:650
  160.6 25.0 %collective-permute-start.31 = (bf16[288,1024]{1,0:T(8,128)(2,1)}, bf16[288,1024]{1,0:T(8,128)(2,1)}, u32[]{:S(2)}, u32[]{:S(2)}) collective-permute-start(bf16[288,1024]{1,0:T(8,128)(2,1)} %collective-permute-done.15.refs_5_), channel_id=1, source_target_pairs={{0,16},{1,17},{2,18},{3,19},{4,20},{5,21},{6,22},{7,23},{8,24},{9,... | collective-permute-start | bytes 1769480 | tf_op jit(solution)/shard_map/ppermute | solution.py:650
  161.8 36.4 %collective-permute-start.33 = (bf16[288,1024]{1,0:T(8,128)(2,1)}, bf16[288,1024]{1,0:T(8,128)(2,1)}, u32[]{:S(2)}, u32[]{:S(2)}) collective-permute-start(bf16[288,1024]{1,0:T(8,128)(2,1)} %collective-permute-done.17.refs_7_), channel_id=1, source_target_pairs={{0,16},{1,17},{2,18},{3,19},{4,20},{5,21},{6,22},{7,23},{8,24},{9,... | collective-permute-start | bytes 1769480 | tf_op jit(solution)/shard_map/ppermute | solution.py:650
  175.8 40.4 %collective-permute-start.23 = (bf16[288,1024]{1,0:T(8,128)(2,1)}, bf16[288,1024]{1,0:T(8,128)(2,1)S(1)}, u32[]{:S(2)}, u32[]{:S(2)}) collective-permute-start(bf16[288,1024]{1,0:T(8,128)(2,1)} %collective-permute-done.15.refs_5_), channel_id=1, source_target_pairs={{0,8},{1,9},{2,10},{3,11},{4,12},{5,13},{6,14},{7,15},{8,0},{9,1},... | collective-permute-start | bytes 1769480 | tf_op jit(solution)/shard_map/ppermute | solution.py:650
  176.5 40.3 %collective-permute-start.25 = (bf16[288,1024]{1,0:T(8,128)(2,1)}, bf16[288,1024]{1,0:T(8,128)(2,1)S(1)}, u32[]{:S(2)}, u32[]{:S(2)}) collective-permute-start(bf16[288,1024]{1,0:T(8,128)(2,1)} %collective-permute-done.17.refs_7_), channel_id=1, source_target_pairs={{0,8},{1,9},{2,10},{3,11},{4,12},{5,13},{6,14},{7,15},{8,0},{9,1},... | collective-permute-start | bytes 1769480 | tf_op jit(solution)/shard_map/ppermute | solution.py:650
  185.6 31.4 %collective-permute-start.35 = (bf16[288,1024]{1,0:T(8,128)(2,1)}, bf16[288,1024]{1,0:T(8,128)(2,1)S(1)}, u32[]{:S(2)}, u32[]{:S(2)}) collective-permute-start(bf16[288,1024]{1,0:T(8,128)(2,1)} %copy-done.50), channel_id=1, source_target_pairs={{0,8},{1,9},{2,10},{3,11},{4,12},{5,13},{6,14},{7,15},{8,0},{9,1},... | collective-permute-start | bytes 1769480 | tf_op jit(solution)/shard_map/ppermute | solution.py:650
  198.2 19.2 %collective-permute-start.36 = (bf16[288,1024]{1,0:T(8,128)(2,1)}, bf16[288,1024]{1,0:T(8,128)(2,1)S(1)}, u32[]{:S(2)}, u32[]{:S(2)}) collective-permute-start(bf16[288,1024]{1,0:T(8,128)(2,1)} %copy-done.46), channel_id=1, source_target_pairs={{0,8},{1,9},{2,10},{3,11},{4,12},{5,13},{6,14},{7,15},{8,0},{9,1},... | collective-permute-start | bytes 1769480 | tf_op jit(solution)/shard_map/ppermute | solution.py:650
  199.4 18.1 %collective-permute-start.38 = (bf16[288,1024]{1,0:T(8,128)(2,1)}, bf16[288,1024]{1,0:T(8,128)(2,1)S(1)}, u32[]{:S(2)}, u32[]{:S(2)}) collective-permute-start(bf16[288,1024]{1,0:T(8,128)(2,1)} %copy-done.47), channel_id=1, source_target_pairs={{0,8},{1,9},{2,10},{3,11},{4,12},{5,13},{6,14},{7,15},{8,0},{9,1},... | collective-permute-start | bytes 1769480 | tf_op jit(solution)/shard_map/ppermute | solution.py:650
  277.3 35.8 %collective-permute-start.43 = (bf16[768,512]{1,0:T(8,128)(2,1)}, bf16[768,512]{1,0:T(8,128)(2,1)}, u32[]{:S(2)}, u32[]{:S(2)}) collective-permute-start(bf16[768,512]{1,0:T(8,128)(2,1)} %get-tuple-element.59), channel_id=1, source_target_pairs={{0,8},{1,9},{2,10},{3,11},{4,12},{5,13},{6,14},{7,15},{8,0},{9,1},... | collective-permute-start | bytes 2359304 | tf_op jit(solution)/shard_map/ppermute | solution.py:650
  291.6 155.2 %collective-permute-start.82 = (bf16[2,2,4,128,1024]{4,3,2,1,0:T(8,128)(2,1)}, bf16[2,2,4,128,1024]{4,3,2,1,0:T(8,128)(2,1)}, u32[]{:S(2)}, u32[]{:S(2)}) collective-permute-start(bf16[2,2,4,128,1024]{4,3,2,1,0:T(8,128)(2,1)} %get-tuple-element.77), channel_id=1, source_target_pairs={{0,8},{1,9},{2,10},{3,11},{4,12},{5,13},{6,14},{7,15},{8,0},{9,1},... | collective-permute-start | bytes 12582920 | tf_op jit(solution)/shard_map/ppermute | solution.py:650
  304.7 147.1 %collective-permute-start.73 = (bf16[2,2,4,128,1024]{4,3,2,1,0:T(8,128)(2,1)}, bf16[2,2,4,128,1024]{4,3,2,1,0:T(8,128)(2,1)S(1)}, u32[]{:S(2)}, u32[]{:S(2)}) collective-permute-start(bf16[2,2,4,128,1024]{4,3,2,1,0:T(8,128)(2,1)} %get-tuple-element.73), channel_id=1, source_target_pairs={{0,8},{1,9},{2,10},{3,11},{4,12},{5,13},{6,14},{7,15},{8,0},{9,1},... | collective-permute-start | bytes 12582920 | tf_op jit(solution)/shard_map/ppermute | solution.py:650
  310.2 78.7 %collective-permute-start.64 = (bf16[2,2,4,32,1024]{4,3,2,1,0:T(8,128)(2,1)}, bf16[2,2,4,32,1024]{4,3,2,1,0:T(8,128)(2,1)}, u32[]{:S(2)}, u32[]{:S(2)}) collective-permute-start(bf16[2,2,4,32,1024]{4,3,2,1,0:T(8,128)(2,1)} %get-tuple-element.69), channel_id=1, source_target_pairs={{0,8},{1,9},{2,10},{3,11},{4,12},{5,13},{6,14},{7,15},{8,0},{9,1},... | collective-permute-start | bytes 3145736 | tf_op jit(solution)/shard_map/ppermute | solution.py:650
  311.8 46.0 %collective-permute-start.42 = (bf16[3,128,1024]{2,1,0:T(8,128)(2,1)S(1)}, bf16[3,128,1024]{2,1,0:T(8,128)(2,1)}, u32[]{:S(2)}, u32[]{:S(2)}) collective-permute-start(bf16[3,128,1024]{2,1,0:T(8,128)(2,1)S(1)} %bitcast.321), channel_id=1, source_target_pairs={{0,16},{1,17},{2,18},{3,19},{4,20},{5,21},{6,22},{7,23},{8,24},{9,... | collective-permute-start | bytes 2359304 | tf_op jit(solution)/shard_map/ppermute | solution.py:650
  349.3 12.7 %collective-permute-start.91 = (f32[16,1024]{1,0:T(8,128)S(1)}, f32[16,1024]{1,0:T(8,128)S(1)}, u32[]{:S(2)}, u32[]{:S(2)}) collective-permute-start(f32[16,1024]{1,0:T(8,128)S(1)} %maximum_add_fusion), channel_id=1, source_target_pairs={{0,8},{1,9},{2,10},{3,11},{4,12},{5,13},{6,14},{7,15},{8,0},{9,1},... | collective-permute-start | bytes 196616 | tf_op jit(solution)/shard_map/ppermute | solution.py:650
  357.8 36.9 %collective-permute-start.58 = (bf16[4,128,512]{2,1,0:T(8,128)(2,1)}, bf16[4,128,512]{2,1,0:T(8,128)(2,1)}, u32[]{:S(2)}, u32[]{:S(2)}) collective-permute-start(bf16[4,128,512]{2,1,0:T(8,128)(2,1)} %slice_bitcast_fusion.4), channel_id=1, source_target_pairs={{0,1},{1,0},{2,3},{3,2},{4,5},{5,4},{6,7},{7,6},{8,9},{9,8},{10,11... | collective-permute-start | bytes 1572872 | tf_op jit(solution)/shard_map/ppermute | solution.py:650
  387.6 11.7 %collective-permute-start.52 = (bf16[4,128,512]{2,1,0:T(8,128)(2,1)S(1)}, bf16[4,128,512]{2,1,0:T(8,128)(2,1)S(1)}, u32[]{:S(2)}, u32[]{:S(2)}) collective-permute-start(bf16[4,128,512]{2,1,0:T(8,128)(2,1)S(1)} %copy-done.20), channel_id=1, source_target_pairs={{0,1},{1,0},{2,3},{3,2},{4,5},{5,4},{6,7},{7,6},{8,9},{9,8},{10,11... | collective-permute-start | bytes 1572872 | tf_op jit(solution)/shard_map/ppermute | solution.py:650
  393.2 17.3 %collective-permute-start.46 = (bf16[4,128,512]{2,1,0:T(8,128)(2,1)S(1)}, bf16[4,128,512]{2,1,0:T(8,128)(2,1)S(1)}, u32[]{:S(2)}, u32[]{:S(2)}) collective-permute-start(bf16[4,128,512]{2,1,0:T(8,128)(2,1)S(1)} %copy-done.19), channel_id=1, source_target_pairs={{0,1},{1,0},{2,3},{3,2},{4,5},{5,4},{6,7},{7,6},{8,9},{9,8},{10,11... | collective-permute-start | bytes 1572872 | tf_op jit(solution)/shard_map/ppermute | solution.py:650
  396.0 16.7 %collective-permute-start.59 = (bf16[128,512]{1,0:T(8,128)(2,1)S(1)}, bf16[128,512]{1,0:T(8,128)(2,1)S(1)}, u32[]{:S(2)}, u32[]{:S(2)}) collective-permute-start(bf16[128,512]{1,0:T(8,128)(2,1)S(1)} %get-tuple-element.116), channel_id=1, source_target_pairs={{0,2},{1,3},{2,0},{3,1},{4,6},{5,7},{6,4},{7,5},{8,10},{9,11},{10,... | collective-permute-start | bytes 393224 | tf_op jit(solution)/shard_map/ppermute | solution.py:650
  399.3 13.7 %collective-permute-start.60 = (bf16[128,512]{1,0:T(8,128)(2,1)S(1)}, bf16[128,512]{1,0:T(8,128)(2,1)S(1)}, u32[]{:S(2)}, u32[]{:S(2)}) collective-permute-start(bf16[128,512]{1,0:T(8,128)(2,1)S(1)} %get-tuple-element.118), channel_id=1, source_target_pairs={{0,4},{1,5},{2,6},{3,7},{4,0},{5,1},{6,2},{7,3},{8,12},{9,13},{10,... | collective-permute-start | bytes 393224 | tf_op jit(solution)/shard_map/ppermute | solution.py:650
  416.3 26.7 %collective-permute-start.65 = (bf16[2,4,32,1024]{3,2,1,0:T(8,128)(2,1)S(1)}, bf16[2,4,32,1024]{3,2,1,0:T(8,128)(2,1)S(1)}, u32[]{:S(2)}, u32[]{:S(2)}) collective-permute-start(bf16[2,4,32,1024]{3,2,1,0:T(8,128)(2,1)S(1)} %get-tuple-element.115), channel_id=1, source_target_pairs={{0,16},{1,17},{2,18},{3,19},{4,20},{5,21},{6,22},{7,23},{8,24},{9,... | collective-permute-start | bytes 1572872 | tf_op jit(solution)/shard_map/ppermute | solution.py:650
  429.7 13.2 %collective-permute-start.49 = (bf16[128,512]{1,0:T(8,128)(2,1)S(1)}, bf16[128,512]{1,0:T(8,128)(2,1)S(1)}, u32[]{:S(2)}, u32[]{:S(2)}) collective-permute-start(bf16[128,512]{1,0:T(8,128)(2,1)S(1)} %get-tuple-element.123), channel_id=1, source_target_pairs={{0,6},{1,7},{2,4},{3,5},{4,2},{5,3},{6,0},{7,1},{8,14},{9,15},{10,... | collective-permute-start | bytes 393224 | tf_op jit(solution)/shard_map/ppermute | solution.py:650
  432.5 118.5 %collective-permute-start.44 = (f32[768,1024]{1,0:T(8,128)S(1)}, f32[768,1024]{1,0:T(8,128)S(1)}, u32[]{:S(2)}, u32[]{:S(2)}) collective-permute-start(f32[768,1024]{1,0:T(8,128)S(1)} %copy-done.9), channel_id=1, source_target_pairs={{0,8},{1,9},{2,10},{3,11},{4,12},{5,13},{6,14},{7,15},{8,0},{9,1},... | collective-permute-start | bytes 9437192 | tf_op jit(solution)/shard_map/ppermute | solution.py:650
  443.0 12.5 %collective-permute-start.56 = (bf16[128,512]{1,0:T(8,128)(2,1)S(1)}, bf16[128,512]{1,0:T(8,128)(2,1)S(1)}, u32[]{:S(2)}, u32[]{:S(2)}) collective-permute-start(bf16[128,512]{1,0:T(8,128)(2,1)S(1)} %add_convert_fusion.9), channel_id=1, source_target_pairs={{0,16},{1,17},{2,18},{3,19},{4,20},{5,21},{6,22},{7,23},{8,24},{9,... | collective-permute-start | bytes 393224 | tf_op jit(solution)/shard_map/ppermute | solution.py:650
  446.8 18.2 %collective-permute-start.66 = (bf16[4,32,1024]{2,1,0:T(8,128)(2,1)S(1)}, bf16[4,32,1024]{2,1,0:T(8,128)(2,1)S(1)}, u32[]{:S(2)}, u32[]{:S(2)}) collective-permute-start(bf16[4,32,1024]{2,1,0:T(8,128)(2,1)S(1)} %get-tuple-element.142), channel_id=1, source_target_pairs={{0,1},{1,0},{2,3},{3,2},{4,5},{5,4},{6,7},{7,6},{8,9},{9,8},{10,11... | collective-permute-start | bytes 786440 | tf_op jit(solution)/shard_map/ppermute | solution.py:650
  451.8 95.5 %collective-permute-start.83 = (bf16[2,4,128,1024]{3,2,1,0:T(8,128)(2,1)S(1)}, bf16[2,4,128,1024]{3,2,1,0:T(8,128)(2,1)S(1)}, u32[]{:S(2)}, u32[]{:S(2)}) collective-permute-start(bf16[2,4,128,1024]{3,2,1,0:T(8,128)(2,1)S(1)} %get-tuple-element.94), channel_id=1, source_target_pairs={{0,16},{1,17},{2,18},{3,19},{4,20},{5,21},{6,22},{7,23},{8,24},{9,... | collective-permute-start | bytes 6291464 | tf_op jit(solution)/shard_map/ppermute | solution.py:650
  455.6 93.4 %collective-permute-start.74 = (bf16[2,4,128,1024]{3,2,1,0:T(8,128)(2,1)S(1)}, bf16[2,4,128,1024]{3,2,1,0:T(8,128)(2,1)S(1)}, u32[]{:S(2)}, u32[]{:S(2)}) collective-permute-start(bf16[2,4,128,1024]{3,2,1,0:T(8,128)(2,1)S(1)} %get-tuple-element.96), channel_id=1, source_target_pairs={{0,16},{1,17},{2,18},{3,19},{4,20},{5,21},{6,22},{7,23},{8,24},{9,... | collective-permute-start | bytes 6291464 | tf_op jit(solution)/shard_map/ppermute | solution.py:650
  473.6 68.9 %collective-permute-start.71 = (bf16[32,1024]{1,0:T(8,128)(2,1)S(1)}, bf16[32,1024]{1,0:T(8,128)(2,1)S(1)}, u32[]{:S(2)}, u32[]{:S(2)}) collective-permute-start(bf16[32,1024]{1,0:T(8,128)(2,1)S(1)} %fusion.51), channel_id=1, source_target_pairs={{0,16},{1,17},{2,18},{3,19},{4,20},{5,21},{6,22},{7,23},{8,24},{9,... | collective-permute-start | bytes 196616 | tf_op jit(solution)/shard_map/ppermute | solution.py:650
  476.2 74.8 %collective-permute-start.70 = (bf16[32,1024]{1,0:T(8,128)(2,1)S(1)}, bf16[32,1024]{1,0:T(8,128)(2,1)S(1)}, u32[]{:S(2)}, u32[]{:S(2)}) collective-permute-start(bf16[32,1024]{1,0:T(8,128)(2,1)S(1)} %fusion.51), channel_id=1, source_target_pairs={{0,8},{1,9},{2,10},{3,11},{4,12},{5,13},{6,14},{7,15},{8,0},{9,1},... | collective-permute-start | bytes 196616 | tf_op jit(solution)/shard_map/ppermute | solution.py:650
  548.3 24.9 %collective-permute-start.84 = (bf16[4,128,1024]{2,1,0:T(8,128)(2,1)S(1)}, bf16[4,128,1024]{2,1,0:T(8,128)(2,1)S(1)}, u32[]{:S(2)}, u32[]{:S(2)}) collective-permute-start(bf16[4,128,1024]{2,1,0:T(8,128)(2,1)S(1)} %get-tuple-element.98), channel_id=1, source_target_pairs={{0,1},{1,0},{2,3},{3,2},{4,5},{5,4},{6,7},{7,6},{8,9},{9,8},{10,11... | collective-permute-start | bytes 3145736 | tf_op jit(solution)/shard_map/ppermute | solution.py:650
  550.0 45.6 %collective-permute-start.75 = (bf16[4,128,1024]{2,1,0:T(8,128)(2,1)S(1)}, bf16[4,128,1024]{2,1,0:T(8,128)(2,1)S(1)}, u32[]{:S(2)}, u32[]{:S(2)}) collective-permute-start(bf16[4,128,1024]{2,1,0:T(8,128)(2,1)S(1)} %get-tuple-element.100), channel_id=1, source_target_pairs={{0,1},{1,0},{2,3},{3,2},{4,5},{5,4},{6,7},{7,6},{8,9},{9,8},{10,11... | collective-permute-start | bytes 3145736 | tf_op jit(solution)/shard_map/ppermute | solution.py:650
  553.3 66.6 %collective-permute-start.45 = (bf16[3,128,1024]{2,1,0:T(8,128)(2,1)S(1)}, bf16[3,128,1024]{2,1,0:T(8,128)(2,1)S(1)}, u32[]{:S(2)}, u32[]{:S(2)}) collective-permute-start(bf16[3,128,1024]{2,1,0:T(8,128)(2,1)S(1)} %bitcast.318), channel_id=1, source_target_pairs={{0,16},{1,17},{2,18},{3,19},{4,20},{5,21},{6,22},{7,23},{8,24},{9,... | collective-permute-start | bytes 2359304 | tf_op jit(solution)/shard_map/ppermute | solution.py:650
  573.4 22.8 %collective-permute-start.85 = (bf16[128,1024]{1,0:T(8,128)(2,1)S(1)}, bf16[128,1024]{1,0:T(8,128)(2,1)S(1)}, u32[]{:S(2)}, u32[]{:S(2)}) collective-permute-start(bf16[128,1024]{1,0:T(8,128)(2,1)S(1)} %get-tuple-element.108), channel_id=1, source_target_pairs={{0,2},{1,3},{2,0},{3,1},{4,6},{5,7},{6,4},{7,5},{8,10},{9,11},{10,... | collective-permute-start | bytes 786440 | tf_op jit(solution)/shard_map/ppermute | solution.py:650
  573.7 23.2 %collective-permute-start.86 = (bf16[128,1024]{1,0:T(8,128)(2,1)S(1)}, bf16[128,1024]{1,0:T(8,128)(2,1)S(1)}, u32[]{:S(2)}, u32[]{:S(2)}) collective-permute-start(bf16[128,1024]{1,0:T(8,128)(2,1)S(1)} %get-tuple-element.110), channel_id=1, source_target_pairs={{0,4},{1,5},{2,6},{3,7},{4,0},{5,1},{6,2},{7,3},{8,12},{9,13},{10,... | collective-permute-start | bytes 786440 | tf_op jit(solution)/shard_map/ppermute | solution.py:650
  574.5 25.1 %collective-permute-start.87 = (bf16[128,1024]{1,0:T(8,128)(2,1)S(1)}, bf16[128,1024]{1,0:T(8,128)(2,1)S(1)}, u32[]{:S(2)}, u32[]{:S(2)}) collective-permute-start(bf16[128,1024]{1,0:T(8,128)(2,1)S(1)} %get-tuple-element.109), channel_id=1, source_target_pairs={{0,6},{1,7},{2,4},{3,5},{4,2},{5,3},{6,0},{7,1},{8,14},{9,15},{10,... | collective-permute-start | bytes 786440 | tf_op jit(solution)/shard_map/ppermute | solution.py:650
  595.9 11.7 %collective-permute-start.76 = (bf16[128,1024]{1,0:T(8,128)(2,1)S(1)}, bf16[128,1024]{1,0:T(8,128)(2,1)S(1)}, u32[]{:S(2)}, u32[]{:S(2)}) collective-permute-start(bf16[128,1024]{1,0:T(8,128)(2,1)S(1)} %get-tuple-element.111), channel_id=1, source_target_pairs={{0,2},{1,3},{2,0},{3,1},{4,6},{5,7},{6,4},{7,5},{8,10},{9,11},{10,... | collective-permute-start | bytes 786440 | tf_op jit(solution)/shard_map/ppermute | solution.py:650
  596.2 13.1 %collective-permute-start.77 = (bf16[128,1024]{1,0:T(8,128)(2,1)S(1)}, bf16[128,1024]{1,0:T(8,128)(2,1)S(1)}, u32[]{:S(2)}, u32[]{:S(2)}) collective-permute-start(bf16[128,1024]{1,0:T(8,128)(2,1)S(1)} %get-tuple-element.113), channel_id=1, source_target_pairs={{0,4},{1,5},{2,6},{3,7},{4,0},{5,1},{6,2},{7,3},{8,12},{9,13},{10,... | collective-permute-start | bytes 786440 | tf_op jit(solution)/shard_map/ppermute | solution.py:650
  597.0 18.0 %collective-permute-start.78 = (bf16[128,1024]{1,0:T(8,128)(2,1)S(1)}, bf16[128,1024]{1,0:T(8,128)(2,1)S(1)}, u32[]{:S(2)}, u32[]{:S(2)}) collective-permute-start(bf16[128,1024]{1,0:T(8,128)(2,1)S(1)} %get-tuple-element.112), channel_id=1, source_target_pairs={{0,6},{1,7},{2,4},{3,5},{4,2},{5,3},{6,0},{7,1},{8,14},{9,15},{10,... | collective-permute-start | bytes 786440 | tf_op jit(solution)/shard_map/ppermute | solution.py:650
  599.8 16.3 %collective-permute-start.89 = (bf16[128,1024]{1,0:T(8,128)(2,1)S(1)}, bf16[128,1024]{1,0:T(8,128)(2,1)S(1)}, u32[]{:S(2)}, u32[]{:S(2)}) collective-permute-start(bf16[128,1024]{1,0:T(8,128)(2,1)S(1)} %fusion.14), channel_id=1, source_target_pairs={{0,16},{1,17},{2,18},{3,19},{4,20},{5,21},{6,22},{7,23},{8,24},{9,... | collective-permute-start | bytes 786440 | tf_op jit(solution)/shard_map/ppermute | solution.py:650
  607.6 17.7 %collective-permute-start.88 = (bf16[128,1024]{1,0:T(8,128)(2,1)S(1)}, bf16[128,1024]{1,0:T(8,128)(2,1)S(1)}, u32[]{:S(2)}, u32[]{:S(2)}) collective-permute-start(bf16[128,1024]{1,0:T(8,128)(2,1)S(1)} %fusion.14), channel_id=1, source_target_pairs={{0,8},{1,9},{2,10},{3,11},{4,12},{5,13},{6,14},{7,15},{8,0},{9,1},... | collective-permute-start | bytes 786440 | tf_op jit(solution)/shard_map/ppermute | solution.py:650
  (97 other events, 1554.9 us)

commit v2 on v1

--- a/solution.py
+++ b/solution.py
@@ -37,76 +37,346 @@
     return pl.CostEstimate(flops=int(flops), bytes_accessed=int(size), transcendentals=int(trans))
 
 
-def qkv_kernel(n, ids, xm, xs, vec, *refs):
-    pieces, (q, k, v, w), sem = refs[:n], refs[n : n + 4], refs[n + 4]
-    step = pl.program_id(0)
-    f = ids[1]
-    rs = w.shape[1] // n
-
-    def copies():
-        out = []
-        for i in range(n):
-            at = pl.multiple_of((f ^ i) * rs, rs)
-            for j in range(3):
-                out.append(
-                    pltpu.make_async_copy(
-                        pieces[i].at[pl.ds(j * rs, rs)], w.at[j, pl.ds(at, rs)], sem.at[i * 3 + j]
-                    )
-                )
-        return out
-
-    @pl.when(step == 0)
-    def _():
-        todo = copies()
-        for c in todo:
+MESH = pl.DeviceIdType.MESH
+PACK = 16
+
+
+def flip(v, mask):
+    out, bit = v, 1
+    while bit <= mask:
+        if mask & bit:
+            out = out + bit - 2 * bit * ((v // bit) % 2)
+        bit *= 2
+    return out
+
+
+def at(index, size):
+    return pl.ds(pl.multiple_of(index * size, size), size)
+
+
+def spread(read, n, rs):
+    per = max(128 // rs, 1)
+    tiles = []
+    for t in range(n // per):
+        tile = read(t * per)
+        for u in range(1, per):
+            tile = tile + pltpu.roll(read(t * per + u), u * rs, 1)
+        tiles.append(tile)
+    return jnp.concatenate(tiles, 1)
+
+
+def front_kernel(
+    n,
+    lens,
+    xin,
+    cin,
+    wq,
+    wk,
+    wv,
+    vecs,
+    wo_in,
+    wi_in,
+    wu_in,
+    xo,
+    co,
+    wqkvo,
+    wio,
+    wuo,
+    woo,
+    veco,
+    qo,
+    ko,
+    vo,
+    cxo,
+    cro,
+    lseo,
+    X,
+    W,
+    VEC,
+    Q,
+    K,
+    V,
+    CX,
+    LSE,
+    lsem,
+    ssem,
+    rsem,
+):
+    C, f = lax.axis_index("ctx"), lax.axis_index("fsdp")
+    x, core = C // 2, C % 2
+    A = n // 2
+    sh, part, width = X.shape[1:]
+    hw = W.shape[2]
+    ff = wio.shape[1]
+    rs, ro, cq = width // n, ff // n, ff // 4
+
+    partners = [(0, 2 * k) for k in range(1, A)] + [(0, 1), (2, 0), (1, 0)]
+
+    def device(dc, df):
+        return (flip(C, dc), flip(f, df))
+
+    barrier = pltpu.get_barrier_semaphore()
+    for p in partners:
+        pl.semaphore_signal(barrier, inc=1, device_id=device(*p), device_id_type=MESH)
+
+    local = []
+    used = iter(range(lsem.shape[0]))
+
+    def begin(source, target):
+        c = pltpu.make_async_copy(source, target, lsem.at[next(used)])
+        c.start()
+        return c
+
+    def keep(source, target):
+        local.append(begin(source, target))
+
+    x_here = begin(xin.at[pl.ds(x * sh, sh)], X.at[0])
+    w_here = [begin(w.at[:, at(core, hw)], W.at[j, at(f, rs)]) for j, w in enumerate((wq, wk, wv))]
+    w_here.append(begin(vecs, VEC.at[f]))
+
+    pl.semaphore_wait(barrier, len(partners))
+
+    def remote(source, target, sem, dev):
+        return pltpu.make_async_remote_copy(
+            src_ref=source,
+            dst_ref=target,
+            send_sem=ssem.at[sem],
+            recv_sem=rsem.at[sem],
+            device_id=device(*dev),
+            device_id_type=MESH,
+        )
+
+    sent = []
+
+    def send(*what):
+        c = remote(*what)
+        c.start()
+        sent.append(c)
+
+    seen = set()
+
+    def arrive(target, sem, dev):
+        if sem not in seen:
+            seen.add(sem)
+            remote(target, target, sem, dev).wait_recv()
+
+    base_x = 12 * n + 4 * n
+    X1, X2, X3, COT, CTX = (base_x + i for i in range(5))
+    send(xin.at[pl.ds((1 - x) * sh, sh)], X.at[1], X1, (2, 0))
+
+    def qkv_slot(i):
+        s = flip(f, i)
+        return [W.at[j, at(s, rs)] for j in range(3)] + [VEC.at[s]]
+
+    def qkv_sem(i):
+        return [12 * n + 4 * i + j for j in range(4)]
+
+    own_qkv = [w.at[:, at(core, hw)] for w in (wq, wk, wv)] + [vecs]
+
+    def qkv_give(tag, source_piece, source, dev):
+        place = qkv_slot(source_piece)
+        for j in range(4):
+            send(source[j], place[j], qkv_sem(tag)[j], dev)
+
+    def qkv_need(i):
+        dev = (0, i) if i % 2 == 0 else (0, 1)
+        place = qkv_slot(i)
+        for j in range(4):
+            arrive(place[j], qkv_sem(i)[j], dev)
+
+    for k in range(1, A):
+        qkv_give(2 * k, 0, own_qkv, (0, 2 * k))
+    qkv_give(1, 0, own_qkv, (0, 1))
+    x_here.wait()
+    send(X.at[0], X.at[2], X2, (1, 0))
+
+    def rest_slot(e, i):
+        qq, s = flip(C, e), flip(f, i)
+        return [
+            woo.at[pl.ds(pl.multiple_of(s * rs + qq * (rs // 4), rs // 4), rs // 4)],
+            wio.at[at(s, rs), at(qq, cq)],
+            wuo.at[pl.ds(pl.multiple_of(s * ro + qq * (ro // 4), ro // 4), ro // 4)],
+        ]
+
+    def rest_sem(e, i):
+        return [(e * n + i) * 3 + kind for kind in range(3)]
+
+    def route(e, i):
+        if e % 2:
+            return (1, 0), (e - 1, i)
+        if e:
+            return (2, 0), (0, i)
+        if i % 2:
+            return (0, 1), (0, i - 1)
+        return (0, i), (0, 0)
+
+    def rest_copies(e, i):
+        dev, (pe, pi) = route(e, i)
+        place = rest_slot(pe, pi)
+        source = [wo_in.at[at(C, rs // 4)], wi_in.at[:, at(C, cq)], wu_in.at[at(C, ro // 4)]]
+        source = source if pi == 0 else place
+        sems = rest_sem(e, i)
+        return [remote(source[kind], place[kind], sems[kind], dev) for kind in range(3)]
+
+    def rest_send(e, i):
+        for c in rest_copies(e, i):
             c.start()
-        for c in todo:
-            c.wait()
-
-    def do(x_ref):
-        x = x_ref[...]
-        q[0] = (dot(x, w[0]) + vec[0:1, :]).astype(BF)
-        k[0] = dot(x, w[1]).astype(BF)
-        v[0] = (dot(x, w[2]) + vec[1:2, :]).astype(BF)
-
-    half = pl.num_programs(0) // 2
-
-    @pl.when(step < half)
-    def _():
-        do(xm)
-
-    @pl.when(step >= half)
-    def _():
-        do(xs)
-
-
-def qkv_call(ids, xm, xs, vec, pieces):
-    rows, width = xm.shape
-    cols = pieces[0].shape[1]
-    n = len(pieces)
-    block = rows // 3
-    grid_spec = pltpu.PrefetchScalarGridSpec(
-        num_scalar_prefetch=1,
-        grid=(6,),
-        in_specs=[
-            pl.BlockSpec((block, width), lambda i, s: (jnp.minimum(i, 2), 0)),
-            pl.BlockSpec((block, width), lambda i, s: (jnp.maximum(i - 3, 0), 0)),
-            pl.BlockSpec((8, cols), lambda i, s: (0, s[0] % 2)),
-        ]
-        + [ANY] * n,
-        out_specs=[pl.BlockSpec((1, block, cols), lambda i, s: (i // 3, i % 3, 0))] * 3
-        + [pl.BlockSpec((3, width, cols), lambda i, s: (0, 0, 0))],
-        scratch_shapes=[pltpu.SemaphoreType.DMA((3 * n,))],
-    )
-    act = jax.ShapeDtypeStruct((2, rows, cols), BF)
+
+    def rest_need(e, i):
+        dev, _ = route(e, i)
+        place = rest_slot(e, i)
+        for kind in range(3):
+            arrive(place[kind], rest_sem(e, i)[kind], dev)
+
+    def rest_hand_on(e, i):
+        rest_need(e, i)
+        if e == 0 and i % 2 == 0:
+            rest_send(0, i + 1)
+        if e == 0:
+            rest_send(2, i)
+        if e % 2 == 0:
+            rest_send(e + 1, i)
+
+    for k in range(1, A):
+        qkv_need(2 * k)
+        qkv_give(2 * k + 1, 2 * k, qkv_slot(2 * k), (0, 1))
+    for k in range(1, A):
+        rest_send(0, 2 * k)
+    arrive(X.at[1], X1, (2, 0))
+    send(X.at[1], X.at[3], X3, (1, 0))
+    send(cin.at[pl.ds((1 - x) * sh, sh)], co.at[1], COT, (2, 0))
+    rest_send(0, 1)
+    keep(cin.at[pl.ds(x * sh, sh)], co.at[0])
+    keep(wo_in, woo.at[at(f, rs)])
+    keep(wi_in, wio.at[at(f, rs)])
+    keep(wu_in, wuo.at[at(f, ro)])
+    for c in w_here:
+        c.wait()
+    for i in range(1, n):
+        qkv_need(i)
+    arrive(X.at[2], X2, (1, 0))
+    arrive(X.at[3], X3, (1, 0))
+    keep(X, xo)
+    keep(W, wqkvo)
+    keep(VEC, veco)
+
+    jobs = [(0, 1)] + [(0, i) for i in range(2, n, 2)] + [(2, 1)]
+    jobs += [(0, i) for i in range(3, n, 2)] + [(2, i) for i in range(2, n)]
+    slots = X.shape[0]
+    pairs = hw // (2 * HD)
+    steps = slots + sh * pairs
+    plan = [jobs[len(jobs) * t // steps : len(jobs) * (t + 1) // steps] for t in range(steps)]
+
+    def serve(step, base, count):
+        for t in range(count):
+            if plan[base + t]:
+
+                @pl.when(step == t)
+                def _():
+                    for job in plan[base + t]:
+                        rest_hand_on(*job)
+
+    def bias(row):
+        read = lambda s: VEC[pl.ds(core * (n // 2) + s, 1), row : row + 1, :128].reshape(1, 128).astype(F32)
+        return spread(read, n // 2, rs)
+
+    bias_q, bias_v = bias(0), bias(1)
+
+    def project(slot, carry):
+        a = X[slot].reshape(sh * part, width)
+        shape = (sh, part, hw)
+        Q[slot] = (dot(a, W[0]) + bias_q).astype(BF).reshape(shape)
+        K[slot] = dot(a, W[1]).astype(BF).reshape(shape)
+        V[slot] = (dot(a, W[2]) + bias_v).astype(BF).reshape(shape)
+        serve(slot, 0, slots)
+        return carry
+
+    lax.fori_loop(0, slots, project, 0)
+    keep(Q, qo)
+    keep(K, ko)
+    keep(V, vo)
+
+    def attend(step, carry):
+        s, pair = step // pairs, step % pairs
+        cols = at(pair, 2 * HD)
+
+        def load(ref):
+            return ref[:, s, :, cols].reshape(slots * part, 2 * HD)
+
+        q, k, v = load(Q), load(K), load(V)
+        mask = key_mask(lens[x * sh + s], C, part)
+        o, lse = attend_pair(q, k, v, mask)
+        CX[:, s, :, cols] = o.reshape(slots, part, 2 * HD)
+        LSE[s, :, cols] = lse
+        serve(step, slots, sh * pairs)
+        return carry
+
+    lax.fori_loop(0, sh * pairs, attend, 0)
+    send(CX.at[pl.ds(2, 2)], cro, CTX, (1, 0))
+    keep(CX, cxo)
+    keep(LSE, lseo)
+    for e in range(4):
+        for i in range(1, n):
+            rest_need(e, i)
+            for c in rest_copies(e, i):
+                c.wait_send()
+    arrive(co.at[1], COT, (2, 0))
+    arrive(cro, CTX, (1, 0))
+    for c in sent:
+        c.wait_send()
+    for c in local:
+        c.wait()
+
+
+def front_call(lengths, xin, cin, wq, wk, wv, vecs, wo, wi, wu, n):
+    seqs, part, width = xin.shape
+    sh, ff, hw = seqs // 2, wi.shape[1], width // 2
+
+    def bf(*shape):
+        return jax.ShapeDtypeStruct(shape, BF)
+
+    def vm(*shape):
+        return pltpu.VMEM(shape, BF)
+
+    full = 4 * part
+    lse = (sh, full, hw)
+    four = (4, sh, part, hw)
+    sems = 16 * n + 5
     return pl.pallas_call(
-        functools.partial(qkv_kernel, n),
-        grid_spec=grid_spec,
-        out_shape=[act, act, act, jax.ShapeDtypeStruct((3, width, cols), BF)],
-        compiler_params=params(),
-        cost_estimate=cost(2 * 2 * rows * width * cols * 3, 4 * rows * width + 12 * rows * cols),
-        name="qkv",
-    )(ids, xm, xs, vec, *pieces)
+        functools.partial(front_kernel, n),
+        in_specs=[pl.BlockSpec(memory_space=pltpu.SMEM)] + [ANY] * 9,
+        out_specs=[ANY] * 13,
+        out_shape=[
+            bf(4, sh, part, width),
+            bf(2, sh, part, width),
+            bf(3, width, hw),
+            bf(width, ff),
+            bf(ff, width),
+            bf(width, width),
+            bf(n, PACK, hw),
+            bf(*four),
+            bf(*four),
+            bf(*four),
+            bf(*four),
+            bf(2, sh, part, hw),
+            jax.ShapeDtypeStruct(lse, F32),
+        ],
+        scratch_shapes=[
+            vm(4, sh, part, width),
+            vm(3, width, hw),
+            vm(n, PACK, hw),
+            vm(*four),
+            vm(*four),
+            vm(*four),
+            vm(*four),
+            pltpu.VMEM(lse, F32),
+            pltpu.SemaphoreType.DMA((24,)),
+            pltpu.SemaphoreType.DMA((sems,)),
+            pltpu.SemaphoreType.DMA((sems,)),
+        ],
+        compiler_params=params(collective_id=0, has_side_effects=True),
+        name="front",
+    )(lengths, xin, cin, wq, wk, wv, vecs, wo, wi, wu)
 
 
 def lanes_of(shape, head):
@@ -126,8 +396,16 @@
     return a.reshape(-1, a.shape[-1])
 
 
-def attend_kernel(q_ref, k_ref, v_ref, mask_ref, cm_ref, cs_ref, lse_ref):
-    q, k, v, mask = flat(q_ref), flat(k_ref), flat(v_ref), flat(mask_ref)
+def key_mask(length, C, part):
+    row = lax.broadcasted_iota(jnp.int32, (part, 2 * HD), 0)
+    out = []
+    for e in (0, 2, 1, 3):
+        inside = row + flip(C, e) * part < length
+        out.append(jnp.where(inside, 0.0, -1e30).astype(BF))
+    return jnp.concatenate(out, 0)
+
+
+def attend_pair(q, k, v, mask):
     out = []
     for head in range(2):
         lane, own, other = lanes_of(q.shape, head)
@@ -140,40 +418,17 @@
         o = dot(e.astype(BF), v) * (1.0 / total)
         out.append((o, top + jnp.log(total), own))
     (o0, l0, own), (o1, l1, _) = out
-    o = jnp.where(own, o0, o1).astype(BF)
-    half = o.shape[0] // 2
-    cm_ref[...] = o[:half].reshape(cm_ref.shape)
-    cs_ref[...] = o[half:].reshape(cs_ref.shape)
-    lse_ref[0] = jnp.where(own, l1, l0)
-
-
-def attend_call(q, k, v, mask):
-    slots, seqs, part, cols = q.shape
-    pair = 2 * HD
-    four = pl.BlockSpec((4, 1, part, pair), lambda s, h: (0, s, 0, h))
-    two = pl.BlockSpec((2, 1, part, pair), lambda s, h: (0, s, 0, h))
-    half = jax.ShapeDtypeStruct((2, seqs, part, cols), BF)
-    full = slots * part
-    return pl.pallas_call(
-        attend_kernel,
-        grid=(seqs, cols // pair),
-        in_specs=[four, four, four, pl.BlockSpec((4, 1, part, pair), lambda s, h: (0, s, 0, 0))],
-        out_specs=[two, two, pl.BlockSpec((1, full, pair), lambda s, h: (s, 0, h))],
-        out_shape=[half, half, jax.ShapeDtypeStruct((seqs, full, cols), F32)],
-        compiler_params=params(),
-        cost_estimate=cost(
-            4 * seqs * full * full * cols * 4, 14 * seqs * full * cols, seqs * full * full * cols // HD
-        ),
-        name="attend",
-    )(q, k, v, mask)
+    return jnp.where(own, o0, o1).astype(BF), jnp.where(own, l1, l0)
 
 
 def attend_back_kernel(
-    q_ref, k_ref, v_ref, mask_ref, lse_ref, cm_ref, cs_ref, gm_ref, gs_ref, dq_ref, dk_ref, dv_ref
+    ids, lens, q_ref, k_ref, v_ref, lse_ref, c_ref, gm_ref, gs_ref, dq_ref, dk_ref, dv_ref
 ):
-    q, k, v, mask = flat(q_ref), flat(k_ref), flat(v_ref), flat(mask_ref)
+    q, k, v, c = flat(q_ref), flat(k_ref), flat(v_ref), flat(c_ref)
+    mask = key_mask(
+        lens[(ids[0] // 2) * pl.num_programs(0) + pl.program_id(0)], ids[0], q_ref.shape[2]
+    )
     lse = lse_ref[0]
-    c = jnp.concatenate([flat(cm_ref), flat(cs_ref)], 0)
     g = jnp.concatenate([flat(gm_ref), flat(gs_ref)], 0)
     qs = q * BF(HD**-0.5)
     kt = k.T
@@ -213,35 +468,37 @@
     dq_ref[...] = dqt.T.astype(BF).reshape(dq_ref.shape)
 
 
-def attend_back_call(q, k, v, mask, lse, cm, cs, gm, gs):
+def attend_back_call(ids, lens, q, k, v, lse, c, gm, gs):
     slots, seqs, part, cols = q.shape
     pair = 2 * HD
-    four = pl.BlockSpec((4, 1, part, pair), lambda s, h: (0, s, 0, h))
-    two = pl.BlockSpec((2, 1, part, pair), lambda s, h: (0, s, 0, h))
+    four = pl.BlockSpec((4, 1, part, pair), lambda s, h, *_: (0, s, 0, h))
+    two = pl.BlockSpec((2, 1, part, pair), lambda s, h, *_: (0, s, 0, h))
     full = slots * part
     out = jax.ShapeDtypeStruct(q.shape, BF)
-    return pl.pallas_call(
-        attend_back_kernel,
+    grid_spec = pltpu.PrefetchScalarGridSpec(
+        num_scalar_prefetch=2,
         grid=(seqs, cols // pair),
         in_specs=[
             four,
             four,
             four,
-            pl.BlockSpec((4, 1, part, pair), lambda s, h: (0, s, 0, 0)),
-            pl.BlockSpec((1, full, pair), lambda s, h: (s, 0, h)),
-            two,
-            two,
+            pl.BlockSpec((1, full, pair), lambda s, h, *_: (s, 0, h)),
+            four,
             two,
             two,
         ],
         out_specs=[four] * 3,
+    )
+    return pl.pallas_call(
+        attend_back_kernel,
+        grid_spec=grid_spec,
         out_shape=[out] * 3,
         compiler_params=params(),
         cost_estimate=cost(
             10 * seqs * full * full * cols * 4, 20 * seqs * full * cols, seqs * full * full * cols // HD
         ),
         name="attend_back",
-    )(q, k, v, mask, lse, cm, cs, gm, gs)
+    )(ids, lens, q, k, v, lse, c, gm, gs)
 
 
 def gelu_pair(u):
@@ -273,61 +530,51 @@
     )
 
 
-def ffn_kernel(n, ids, cm, cr, xm, cot, valid, vec, ib, *refs):
-    pieces = refs[: 4 * n]
-    lo, act, dout, dinn, nrm, dattn, dfirst, dco, dcs, acc = refs[4 * n : 4 * n + 10]
-    wo, wi, wu, gp, sem = refs[4 * n + 10 :]
+def ffn_kernel(n, sh, part, ids, lens, cm, cr, xm, cot, vecs, wo_in, wi_in, wu_in, *refs):
+    lo, act, dout, dinn, nrm, dattn, dfirst, dco, dcs, acc = refs[:10]
+    wo, wi, wu, gp, vec, ib, sem = refs[10:]
     width, ff = wi.shape
-    core, f = ids[0] % 2, ids[1]
+    core = ids[0] % 2
     step = pl.program_id(0)
     rs, ro = width // n, ff // n
-    cq = ff // 4
-    q_i, q_u, q_o = rs, ro // 4, rs // 4
-
-    def copies(kind):
-        out = []
-        for e in range(4):
-            qq = ids[0] ^ e
-            for i in range(n):
-                s = f ^ i
-                ref = pieces[e * n + i]
-                at = (kind * 4 + e) * n + i
-                if kind == 0:
-                    half = (s // (n // 2)) ^ core
-                    to = half * (width // 2) + (s % (n // 2)) * rs + qq * q_o
-                    src = ref.at[pl.ds(q_i + q_u, q_o)]
-                    dst = wo.at[pl.ds(pl.multiple_of(to, q_o), q_o)]
-                elif kind == 1:
-                    src = ref.at[pl.ds(0, q_i)]
-                    dst = wi.at[
-                        pl.ds(pl.multiple_of(s * rs, rs), rs), pl.ds(pl.multiple_of(qq * cq, cq), cq)
-                    ]
-                else:
-                    src = ref.at[pl.ds(q_i, q_u)]
-                    dst = wu.at[pl.ds(pl.multiple_of(s * ro + qq * q_u, q_u), q_u)]
-                out.append(pltpu.make_async_copy(src, dst, sem.at[at]))
-        return out
+    cq, hw = ff // 4, width // 2
+
+    pairs = ((wo_in, wo), (wi_in, wi), (wu_in, wu))
+
+    def copy(kind):
+        return pltpu.make_async_copy(*pairs[kind], sem.at[kind])
 
     @pl.when(step == 0)
     def _():
         for kind in range(3):
-            for c in copies(kind):
-                c.start()
+            copy(kind).start()
         acc[...] = jnp.zeros_like(acc)
+        vec[...] = spread(lambda s: vecs[s, :8, :128].astype(F32), n, rs)
+        for s in range(n):
+            ib[:, s * ro : (s + 1) * ro] = vecs[s, 8:9, :ro].astype(F32)
 
     def arrived(kind):
         @pl.when(step == 0)
         def _():
-            for c in copies(kind):
-                c.wait()
+            copy(kind).wait()
+
+    count = xm.shape[0] // part
+    inside = []
+    for u in range(count):
+        slot = step * count + u
+        ex, s = slot // sh, slot % sh
+        first = (ids[0] ^ (2 * ex)) * part
+        row = lax.broadcasted_iota(jnp.int32, (part, 1), 0) + first
+        inside.append(jnp.where(row < lens[(ids[0] // 2) * sh + s], 1.0, 0.0))
+    valid = jnp.concatenate(inside, 0)
+    own, other = at(core, hw), at(1 - core, hw)
 
     def add(row, value):
         acc[row : row + 1, :] += jnp.sum(value, 0, keepdims=True)
 
     arrived(0)
-    hw = width // 2
     first = (
-        xm[...].astype(F32) + (dot(cm[...], wo[:hw]) + dot(cr[...], wo[hw:])) + vec[2:3, :]
+        xm[...].astype(F32) + (dot(cm[...], wo[own]) + dot(cr[...], wo[other])) + vec[2:3, :]
     )
     hat1, r1 = normalise(first)
     normed = hat1 * vec[4:5, :] + vec[5:6, :]
@@ -343,7 +590,7 @@
     second = normed + (dot(act[...], wu[...]) + vec[3:4, :])
     hat2, r2 = normalise(second)
     lo[...] = (hat2 * vec[6:7, :] + vec[7:8, :]).astype(BF)
-    og = cot[...].astype(F32) * valid[...]
+    og = cot[...].astype(F32) * valid
     add(6, og * hat2)
     add(7, og)
     d2 = normalise_back(og * vec[6:7, :], hat2, r2)
@@ -363,29 +610,26 @@
     d1low = d1.astype(BF)
     dattn[...] = d1low
     add(2, d1low.astype(F32))
-    dc = dot_nt(d1low, wo[...]).astype(BF)
-    dco[...] = dc[:, :hw]
-    dcs[...] = dc[:, hw:]
-
-
-def ffn_call(ids, cm, cr, xm, cot, valid, vec, ib, pieces):
-    rows, width = xm.shape
-    ff = ib.shape[1]
-    n = len(pieces) // 4
+    dco[...] = dot_nt(d1low, wo[own]).astype(BF)
+    dcs[...] = dot_nt(d1low, wo[other]).astype(BF)
+
+
+def ffn_call(ids, lens, sh, c, cr, xall, cot, vecs, wo, wi, wu):
+    width, ff = wi.shape
+    n, rows = vecs.shape[0], cot.shape[0]
     block = rows // 3
     hw = width // 2
 
     def by(cols):
-        return pl.BlockSpec((block, cols), lambda i, s: (i, 0))
-
-    def whole(a, b):
-        return pl.BlockSpec((a, b), lambda i, s: (0, 0))
+        return pl.BlockSpec((block, cols), lambda i, *_: (i, 0))
+
+    def whole(*shape):
+        return pl.BlockSpec(shape, lambda i, *_: (0,) * len(shape))
 
     grid_spec = pltpu.PrefetchScalarGridSpec(
-        num_scalar_prefetch=1,
+        num_scalar_prefetch=2,
         grid=(3,),
-        in_specs=[by(hw), by(hw), by(width), by(width), by(1), whole(8, width), whole(1, ff)]
-        + [ANY] * (4 * n),
+        in_specs=[by(hw), by(hw), by(width), by(width), whole(*vecs.shape), ANY, ANY, ANY],
         out_specs=[
             by(width),
             by(ff),
@@ -403,7 +647,9 @@
             pltpu.VMEM((width, ff), BF),
             pltpu.VMEM((ff, width), BF),
             pltpu.VMEM((block, ff), F32),
-            pltpu.SemaphoreType.DMA((12 * n,)),
+            pltpu.VMEM((8, width), F32),
+            pltpu.VMEM((1, ff), F32),
+            pltpu.SemaphoreType.DMA((3,)),
         ],
     )
 
@@ -411,7 +657,7 @@
         return jax.ShapeDtypeStruct((rows, cols), dtype)
 
     return pl.pallas_call(
-        functools.partial(ffn_kernel, n),
+        functools.partial(ffn_kernel, n, sh, rows // (2 * sh)),
         grid_spec=grid_spec,
         out_shape=[
             shape(width),
@@ -430,7 +676,7 @@
             2 * rows * width * (2 * width + 4 * ff), 30 * rows * width + 2 * width * (2 * ff + width)
         ),
         name="ffn",
-    )(ids, cm, cr, xm, cot, valid, vec, ib, *pieces)
+    )(ids, lens, c, cr, xall, cot, vecs, wo, wi, wu)
 
 
 def outer_grad_kernel(ids, act, dout, keep, send, tmp):
@@ -438,8 +684,7 @@
     size = keep.shape[3]
     for ec, ref in ((0, keep), (1, send)):
         for ex in range(2):
-            at = pl.multiple_of((ids[0] ^ (2 * ex + ec)) * size, size)
-            ref[ex, 0, 0] = tmp[pl.ds(at, size), :].astype(BF)
+            ref[ex, 0, 0] = tmp[at(ids[0] ^ (2 * ex + ec), size), :].astype(BF)
 
 
 def outer_grad_call(ids, act, dout, n):
@@ -474,8 +719,7 @@
 
     def put(ref):
         for i in range(n):
-            at = pl.multiple_of((ids[1] ^ i) * rs, rs)
-            ref[0, i % 2, i // 2] = tmp[pl.ds(at, rs), :].astype(BF)
+            ref[0, i % 2, i // 2] = tmp[at(ids[1] ^ i, rs), :].astype(BF)
 
     @pl.when(pl.program_id(0) == 0)
     def _():
@@ -520,31 +764,37 @@
     hw, rs = width // 2, width // n
     size = rs // 4
     g = dattn[...]
-    tmp[:hw, :] = dot_tn(cm[...], g)
-    tmp[hw:, :] = dot_tn(cr[...], g)
+    core = ids[0] % 2
+    tmp[at(core, hw), :] = dot_tn(cm[...], g)
+    tmp[at(1 - core, hw), :] = dot_tn(cr[...], g)
     for ec, ref in ((0, keep), (1, send)):
         for ex in range(2):
             for i in range(n):
-                s = ids[1] ^ i
-                half = (s // (n // 2)) ^ (ids[0] % 2)
-                at = half * hw + (s % (n // 2)) * rs + (ids[0] ^ (2 * ex + ec)) * size
-                ref[ex, i % 2, i // 2] = tmp[pl.ds(pl.multiple_of(at, size), size), :].astype(BF)
-
-
-def out_grad_call(ids, cm, cr, dattn, n):
+                first = (ids[1] ^ i) * rs + (ids[0] ^ (2 * ex + ec)) * size
+                ref[ex, i % 2, i // 2] = tmp[pl.ds(pl.multiple_of(first, size), size), :].astype(BF)
+
+
+def out_grad_call(ids, ctx, cr, dattn, n):
     rows, width = dattn.shape
     shape = jax.ShapeDtypeStruct((2, 2, n // 2, width // n // 4, width), BF)
-    vm = pl.BlockSpec(memory_space=pltpu.VMEM)
     return pl.pallas_call(
         functools.partial(out_grad_kernel, n),
-        in_specs=[pl.BlockSpec(memory_space=pltpu.SMEM), vm, vm, vm],
-        out_specs=[vm, vm],
+        grid_spec=pltpu.PrefetchScalarGridSpec(
+            num_scalar_prefetch=1,
+            grid=(1,),
+            in_specs=[
+                pl.BlockSpec((rows, width // 2), lambda i, s: (0, 0)),
+                pl.BlockSpec((rows, width // 2), lambda i, s: (0, 0)),
+                pl.BlockSpec((rows, width), lambda i, s: (0, 0)),
+            ],
+            out_specs=[pl.BlockSpec(shape.shape, lambda i, s: (0, 0, 0, 0, 0))] * 2,
+            scratch_shapes=[pltpu.VMEM((width, width), F32)],
+        ),
         out_shape=[shape, shape],
-        scratch_shapes=[pltpu.VMEM((width, width), F32)],
         compiler_params=params(),
         cost_estimate=cost(2 * rows * width * width, 4 * rows * width + 2 * width * width),
         name="out_grad",
-    )(ids, cm, cr, dattn)
+    )(ids, ctx, cr, dattn)
 
 
 def qkv_grad_kernel(n, ids, xm, xs, dm, ds, out, bias, tmp):
@@ -555,21 +805,19 @@
     )
     rs = tmp.shape[0] // n
     for i in range(n):
-        at = pl.multiple_of((ids[1] ^ i) * rs, rs)
-        out[i % 2, i // 2] = tmp[pl.ds(at, rs), :].astype(BF)
-
-
-def qkv_grad_call(ids, xm, xs, d, n):
-    rows, width = xm.shape
+        out[i % 2, i // 2] = tmp[at(ids[1] ^ i, rs), :].astype(BF)
+
+
+def qkv_grad_call(ids, xall, d, n):
+    rows, width = xall.shape[0] // 2, xall.shape[1]
     cols = d.shape[2]
-    vm = pl.BlockSpec((rows, width), lambda i, s: (0, 0))
     shape = (2, n // 2, width // n, cols)
     grid_spec = pltpu.PrefetchScalarGridSpec(
         num_scalar_prefetch=1,
         grid=(1,),
         in_specs=[
-            vm,
-            vm,
+            pl.BlockSpec((rows, width), lambda i, s: (0, 0)),
+            pl.BlockSpec((rows, width), lambda i, s: (1, 0)),
             pl.BlockSpec((1, rows, cols), lambda i, s: (0, 0, 0)),
             pl.BlockSpec((1, rows, cols), lambda i, s: (1, 0, 0)),
         ],
@@ -586,7 +834,7 @@
         compiler_params=params(),
         cost_estimate=cost(4 * rows * width * cols, 4 * rows * width + 4 * rows * cols),
         name="qkv_grad",
-    )(ids, xm, xs, d, d)
+    )(ids, xall, xall, d, d)
 
 
 def back_project_kernel(dq, dk, dv, w, out):
@@ -649,9 +897,6 @@
         ]
         return lax.ppermute(a, ("ctx", "fsdp"), pairs)
 
-    def half_seqs(a, which):
-        return lax.dynamic_slice_in_dim(a, which * sh, sh, 0)
-
     def pick(bit, a, b):
         return jnp.where(bit == 0, a, b), jnp.where(bit == 0, b, a)
 
@@ -665,9 +910,6 @@
             ]
             step *= 2
         return items
-
-    def columns(w):
-        return lax.dynamic_slice_in_dim(w, core * hw, hw, 1)
 
     def row_of(v):
         return jnp.pad(v.reshape(1, -1), ((0, 0), (0, hw - v.shape[0])))
@@ -683,66 +925,27 @@
         second_shift,
         inner_bias,
     ]
-    pack = jnp.concatenate(
-        [columns(query_weight), columns(key_weight), columns(value_weight)]
-        + [row_of(v) for v in vectors]
-        + [jnp.zeros((16 - len(vectors), hw), BF)],
-        0,
-    )
-    got = {0: pack, 1: swap(pack, 0, 1)}
-    for k in range(1, A):
-        got[2 * k] = swap(pack, 0, 2 * k)
-    for k in range(1, A):
-        got[2 * k + 1] = swap(got[2 * k], 0, 1)
-    qkv_pieces = [got[i] for i in range(n)]
-
-    x_mine, x_other = half_seqs(inputs, x), half_seqs(inputs, 1 - x)
-    x_m = jnp.concatenate([x_mine[None], swap(x_other, 2, 0)[None]], 0)
-    x_s = swap(x_m, 1, 0)
-    xm, xs = x_m.reshape(rows, width), x_s.reshape(rows, width)
-
-    small = xor_order([p[3 * rs : 3 * rs + 16] for p in qkv_pieces], f)
-    vec = jnp.concatenate([p[:8, :rs] for p in small], 1).astype(F32)
-    ib = jnp.concatenate([p[8:9, :ro] for p in small], 1).astype(F32)
-
-    q, k, v, w_qkv = qkv_call(ids, xm, xs, vec, qkv_pieces)
-
-    quarter_i = lax.dynamic_slice_in_dim(inner_weight, C * (ff // 4), ff // 4, 1)
-    quarter_u = lax.dynamic_slice_in_dim(outer_weight, C * (ro // 4), ro // 4, 0)
-    quarter_o = lax.dynamic_slice_in_dim(out_weight, C * (rs // 4), rs // 4, 0)
-    ffn_pack = jnp.concatenate([quarter_i, quarter_u, quarter_o], 0)
-    ffn_pack = lax.optimization_barrier((ffn_pack, got[n - 2]))[0]
-    part0 = {0: ffn_pack, 1: swap(ffn_pack, 0, 1)}
-    for kk in range(1, A):
-        part0[2 * kk] = swap(ffn_pack, 0, 2 * kk)
-    for kk in range(1, A):
-        part0[2 * kk + 1] = swap(part0[2 * kk], 0, 1)
-    part2 = {i: swap(part0[i], 2, 0) for i in range(n)}
-    part1 = {i: swap(part0[i], 1, 0) for i in range(n)}
-    part3 = {i: swap(part2[i], 1, 0) for i in range(n)}
-    ffn_pieces = [p[i] for p in (part0, part1, part2, part3) for i in range(n)]
-
-    c_mine, c_other = half_seqs(cotangent, x), half_seqs(cotangent, 1 - x)
-    cot = jnp.concatenate([c_mine[None], swap(c_other, 2, 0)[None]], 0).reshape(rows, width)
-
-    lens = half_seqs(lengths, x)
-    order = jnp.stack([C ^ e for e in (0, 2, 1, 3)])
-    positions = order[:, None, None] * part + jnp.arange(part)[None, None, :]
-    inside = positions < lens[None, :, None]
-    valid = inside[:2].astype(F32).reshape(rows, 1)
-    mask = jnp.broadcast_to(
-        jnp.where(inside, 0.0, -1e30).astype(BF)[..., None], (4, sh, part, 2 * HD)
-    )
-
-    four = (4, sh, part, hw)
+    vecs = jnp.concatenate(
+        [row_of(v) for v in vectors] + [jnp.zeros((PACK - len(vectors), hw), BF)], 0
+    )
+    x4, cot, w_qkv, wi, wu, wo, vecs, q4, k4, v4, c4, c_r, lse = front_call(
+        lengths,
+        inputs,
+        cotangent,
+        query_weight,
+        key_weight,
+        value_weight,
+        vecs,
+        out_weight,
+        inner_weight,
+        outer_weight,
+        n,
+    )
+    xall = x4.reshape(2 * rows, width)
+    ctx, cr = c4.reshape(2 * rows, hw), c_r.reshape(rows, hw)
     two = (2, sh, part, hw)
-    q4, k4, v4 = q.reshape(four), k.reshape(four), v.reshape(four)
-    c_m, c_s, lse = attend_call(q4, k4, v4, mask)
-    c_r = swap(c_s, 1, 0)
-    cm, cr = c_m.reshape(rows, hw), c_r.reshape(rows, hw)
-
     lo, act, dout, dinn, nrm, dattn, dfirst, dco, dcs, acc = ffn_call(
-        ids, cm, cr, xm, cot, valid, vec, ib, ffn_pieces
+        ids, lengths, sh, ctx, cr, xall, cot.reshape(rows, width), vecs, wo, wi, wu
     )
 
     def give_back(a):
@@ -775,13 +978,13 @@
 
     ku, su = outer_grad_call(ids, act, dout, n)
     ki, si = inner_grad_call(ids, nrm, dinn, n)
-    ko, so = out_grad_call(ids, cm, cr, dattn, n)
+    ko, so = out_grad_call(ids, ctx, cr, dattn, n)
     grad_outer = jnp.concatenate(reduce_quarter(ku, su), 0)
     grad_inner = jnp.concatenate(reduce_quarter(ki, si), 1)
     grad_out = jnp.concatenate(reduce_quarter(ko, so), 0)
 
     dq, dk, dv = attend_back_call(
-        q4, k4, v4, mask, lse, c_m, c_s, dco.reshape(two), g_r.reshape(two)
+        ids, lengths, q4, k4, v4, lse, c4, dco.reshape(two), g_r.reshape(two)
     )
     flat3 = (2, rows, hw)
     dq, dk, dv = dq.reshape(flat3), dk.reshape(flat3), dv.reshape(flat3)
@@ -793,9 +996,9 @@
         mine = total(mine, swap(mine, 2, 0))
         return jnp.concatenate(pick(core, mine, swap(mine, 1, 0)), 1).astype(F32)
 
-    gq, bq = qkv_grad_call(ids, xm, xs, dq, n)
-    gk, _ = qkv_grad_call(ids, xm, xs, dk, n)
-    gv, bv = qkv_grad_call(ids, xm, xs, dv, n)
+    gq, bq = qkv_grad_call(ids, xall, dq, n)
+    gk, _ = qkv_grad_call(ids, xall, dk, n)
+    gv, bv = qkv_grad_call(ids, xall, dv, n)
     grad_query, grad_key, grad_value = reduce_half(gq), reduce_half(gk), reduce_half(gv)
 
     halves = jnp.concatenate([bq[:1], bv[:1], jnp.zeros((14, hw), F32)], 0)

time: 639 us -> 583 us (0.912)
  Pallas kernels: 169 us -> 302 us
  waiting for transfers between devices: 266 us -> 162 us
  starting transfers between devices: 127 us -> 71.1 us
  local copies, waits for them, and re-layouts: 31.7 us -> 14.2 us
    pallas_call x5 -> x4, Pallas kernels: 110 us -> 243 us  [the longest x1 160 us: front_call(): pl.pallas_call(functools.partial(front_kernel, n), in_specs=[pl.BlockSpec...]
    ppermute x96 -> x54, waiting for transfers between devices: 266 us -> 162 us  [swap(): return lax.ppermute(a, ('ctx', 'fsdp'), pairs)]
    ppermute x96 -> x54, starting transfers between devices: 127 us -> 71.1 us  [swap(): return lax.ppermute(a, ('ctx', 'fsdp'), pairs)]
  transfers between devices with their start and end apart: 96 -> 54, of which waited for: 38 -> 15; matrix products, arithmetic and copies ran while one was open for 8% -> 5% of each run, Pallas kernels for 18% -> 15%
where the time goes in v2:
time: 583 us; the launch traced here: 578 us
  Pallas kernels  302 us (52%)
  waiting for transfers between devices  162 us (28%)
  starting transfers between devices  71.1 us (12%)
  other arithmetic  27.8 us (5%)
  local copies, waits for them, and re-layouts  14.2 us (2%)
    ppermute x54, waiting for transfers between devices, swap(): return lax.ppermute(a, ('ctx', 'fsdp'), pairs)  162 us
    pallas_call x1, Pallas kernels, front_call(): pl.pallas_call(functools.partial(front_kernel, n), in_specs=[pl.BlockSpec...  160 us
    ppermute x54, starting transfers between devices, swap(): return lax.ppermute(a, ('ctx', 'fsdp'), pairs)  71.1 us
    pallas_call x1, Pallas kernels, ffn_call(): pl.pallas_call(functools.partial(ffn_kernel, n, sh, rows // (2 * sh)), gr...  53.4 us
    pallas_call x1, Pallas kernels, attend_back_call(): pl.pallas_call(attend_back_kernel, grid_spec=grid_spec, out_shape=[out] *...  23.9 us
    pallas_call x3, Pallas kernels, qkv_grad_call(): pl.pallas_call(functools.partial(qkv_grad_kernel, n), grid_spec=grid_spec...  17.9 us
    pallas_call x2, Pallas kernels, back_project_call(): pl.pallas_call(back_project_kernel, grid=(3,), in_specs=[one, one, one, p...  14 us
    convert_element_type x21, other arithmetic, total(): return out.astype(BF)  13.9 us
  transfers between devices with their start and end apart: 54, of which 15 were waited for; matrix products, arithmetic and copies ran while one was open for 5% of the time, Pallas kernels for 15%

profile of v2, /device:TPU:1, one launch (start us, length us, event | category | flops | bytes accessed | tf_op | source)
XLA Modules:
  0.0 578.5 jit_solution(1223979601519786329)
XLA Ops:
  7.2 1.3 concatenate.42.vecs
  8.5 160.1 %front.1 = (bf16[4,3,128,1024]{3,2,1,0:T(8,128)(2,1)}, bf16[2,3,128,1024]{3,2,1,0:T(8,128)(2,1)}, bf16[3,1024,512]{2,1,0:T(8,128)(2,1)}, bf16[1024,4096]{1,0:T(8...) custom-call(s32[6]{0:T(128)} %lens.5, ...), custom_call_target="tpu_custom_call" | custom-call | tf_op jit(solution)/shard_map/front/pallas_call | solution.py:345
  168.6 53.4 %ffn.1 = (bf16[768,1024]{1,0:T(8,128)(2,1)}, bf16[768,4096]{1,0:T(8,128)(2,1)}, bf16[768,1024]{1,0:T(8,128)(2,1)}, bf16[768,4096]{1,0:T(8,128)(2,1)}, bf16[768,1...) custom-call(s32[2]{0:T(128)} %pad_add_fusion.ids, ...), custom_call_target="tpu_custom_call" | custom-call | flops 28991029248 | bytes 42467328 | tf_op jit(solution)/shard_map/ffn/pallas_call | solution.py:659
  222.2 13.1 %inner_grad.1 = (bf16[2,2,4,128,1024]{4,3,2,1,0:T(8,128)(2,1)}, bf16[2,2,4,128,1024]{4,3,2,1,0:T(8,128)(2,1)}) custom-call(s32[2]{0:T(128)} %pad_add_fusion.ids, bf16[768,1024]{1,0:T(8,128)(2,1)} %get-tuple-element.80.nrm, bf16[768,4096]{1,0:T(8,128)(2,1)} %get-tuple-element.81.dinn), custom_call_target="tpu_custom_call" | custom-call | flops 6442450944 | bytes 16252928 | tf_op jit(solution)/shard_map/inner_grad/pallas_call | solution.py:752
  235.6 13.7 %outer_grad.1 = (bf16[2,2,4,128,1024]{4,3,2,1,0:T(8,128)(2,1)}, bf16[2,2,4,128,1024]{4,3,2,1,0:T(8,128)(2,1)}) custom-call(s32[2]{0:T(128)} %pad_add_fusion.ids, bf16[768,4096]{1,0:T(8,128)(2,1)} %get-tuple-element.84.act, bf16[768,1024]{1,0:T(8,128)(2,1)} %get-tuple-element.85.dout), custom_call_target="tpu_custom_call" | custom-call | flops 6442450944 | bytes 16252928 | tf_op jit(solution)/shard_map/outer_grad/pallas_call | solution.py:706
  249.5 5.9 %out_grad.1 = (bf16[2,2,4,32,1024]{4,3,2,1,0:T(8,128)(2,1)}, bf16[2,2,4,32,1024]{4,3,2,1,0:T(8,128)(2,1)}) custom-call(s32[2]{0:T(128)} %pad_add_fusion.ids, bf16[1536,512]{1,0:T(8,128)(2,1)} %bitcast.313, bf16[768,512]{1,0:T(8,128)(2,1)} %bitcast.317, bf16[768,1024]{1,0:T(8,128)(2,1)} %get-tuple-element.77.dattn), custom_call_target="tpu_custom_call" | custom-call | flops 1610612736 | bytes 5242880 | tf_op jit(solution)/shard_map/out_grad/pallas_call | solution.py:780
  258.6 23.9 %attend_back.1 = (bf16[4,3,128,512]{3,2,1,0:T(8,128)(2,1)}, bf16[4,3,128,512]{3,2,1,0:T(8,128)(2,1)}, bf16[4,3,128,512]{3,2,1,0:T(8,128)(2,1)}) custom-call(s32[2]{0:T(128)} %pad_add_fusion.ids, s32[6]{0:T(128)} %lens.5, bf16[4,3,128,512]{3,2,1,0:T(8,128)(2,1)} %get-tuple-element.64.q_ref, bf16[4,3,128,512]{3,2,1,0:T(8,128)(2,1)} %get-tuple-element.65.k_ref, ...), custom_call_target="tpu_custom_call" | custom-call | flops 16106127360 | bytes 15728640 | tf_op jit(solution)/shard_map/attend_back/pallas_call | solution.py:492
  282.5 5.9 %qkv_grad.5 = (bf16[2,4,128,512]{3,2,1,0:T(8,128)(2,1)}, f32[8,512]{1,0:T(8,128)}) custom-call(s32[2]{0:T(128)} %pad_add_fusion.ids, bf16[1536,1024]{1,0:T(8,128)(2,1)} %bitcast.282, bf16[1536,1024]{1,0:T(8,128)(2,1)} %bitcast.283, bf16[2,768,512]{2,1,0:T(8,128)(2,1)} %bitcast.296, bf16[2,768,512]{2,1,0:T(8,128)(2,1)} %bitcast.297), custom_call_target="tpu_custom_call" | custom-call | flops 1610612736 | bytes 4718592 | tf_op jit(solution)/shard_map/qkv_grad/pallas_call | solution.py:830
  289.1 6.0 %qkv_grad.3 = (bf16[2,4,128,512]{3,2,1,0:T(8,128)(2,1)}, f32[8,512]{1,0:T(8,128)}) custom-call(s32[2]{0:T(128)} %pad_add_fusion.ids, bf16[1536,1024]{1,0:T(8,128)(2,1)} %bitcast.284, bf16[1536,1024]{1,0:T(8,128)(2,1)} %bitcast.285, bf16[2,768,512]{2,1,0:T(8,128)(2,1)} %bitcast.288, bf16[2,768,512]{2,1,0:T(8,128)(2,1)} %bitcast.289), custom_call_target="tpu_custom_call" | custom-call | flops 1610612736 | bytes 4718592 | tf_op jit(solution)/shard_map/qkv_grad/pallas_call | solution.py:830
  296.4 5.9 %qkv_grad.4 = (bf16[2,4,128,512]{3,2,1,0:T(8,128)(2,1)}, f32[8,512]{1,0:T(8,128)}) custom-call(s32[2]{0:T(128)} %pad_add_fusion.ids, bf16[1536,1024]{1,0:T(8,128)(2,1)} %bitcast.286, bf16[1536,1024]{1,0:T(8,128)(2,1)} %bitcast.287, bf16[2,768,512]{2,1,0:T(8,128)(2,1)} %bitcast.292, bf16[2,768,512]{2,1,0:T(8,128)(2,1)} %bitcast.293), custom_call_target="tpu_custom_call" | custom-call | flops 1610612736 | bytes 4718592 | tf_op jit(solution)/shard_map/qkv_grad/pallas_call | solution.py:830
  302.4 1.2 slice_bitcast_fusion.5
  303.9 1.3 broadcast_select_fusion.1
  306.1 1.3 collective-permute-start.50
  307.4 7.2 %back_project.2 = f32[768,1024]{1,0:T(8,128)} custom-call(bf16[2,768,512]{2,1,0:T(8,128)(2,1)} %bitcast.290, bf16[2,768,512]{2,1,0:T(8,128)(2,1)} %bitcast.294, bf16[2,768,512]{2,1,0:T(8,128)(2,1)} %bitcast.298, bf16[3,1024,512]{2,1,0:T(8,128)(2,1)} %get-tuple-element.73.w), custom_call_target="tpu_custom_call" | custom-call | flops 2415919104 | bytes 8650752 | tf_op jit(solution)/shard_map/back_project/pallas_call | solution.py:849
  315.3 6.8 %back_project.3 = f32[768,1024]{1,0:T(8,128)} custom-call(bf16[2,768,512]{2,1,0:T(8,128)(2,1)} %bitcast.291, bf16[2,768,512]{2,1,0:T(8,128)(2,1)} %bitcast.295, bf16[2,768,512]{2,1,0:T(8,128)(2,1)} %bitcast.299, bf16[3,1024,512]{2,1,0:T(8,128)(2,1)} %get-tuple-element.73.w), custom_call_target="tpu_custom_call" | custom-call | flops 2415919104 | bytes 8650752 | tf_op jit(solution)/shard_map/back_project/pallas_call | solution.py:849
  322.6 1.3 pad_maximum_fusion.1
  323.9 1.4 collective-permute-done.52
  327.4 3.3 collective-permute-done.53
  332.9 1.3 fusion.40
  334.2 2.4 collective-permute-done.16
  336.6 1.3 collective-permute-start.12
  338.0 9.8 %collective-permute-done.4 = bf16[4,128,512]{2,1,0:T(8,128)(2,1)S(1)} collective-permute-done((bf16[4,128,512]{2,1,0:T(8,128)(2,1)S(1)}, bf16[4,128,512]{2,1,0:T(8,128)(2,1)S(1)}, u32[]{:S(2)}, u32[]{:S(2)}) %collective-permute-start.4) | collective-permute-done | bytes 524320 | tf_op jit(solution)/shard_map/ppermute | solution.py:898
  347.9 1.3 collective-permute-start.13
  349.6 2.0 collective-permute-start.18
  351.6 2.0 collective-permute-done.13
  353.6 1.4 collective-permute-start.19
  356.0 5.2 collective-permute-start.2
  361.3 4.7 collective-permute-start.5
  366.4 2.0 collective-permute-start.7
  368.3 3.7 add_convert_fusion.3
  372.0 1.2 collective-permute-start.23
  373.2 4.2 collective-permute-done.6
  377.4 1.5 collective-permute-start.32
  379.1 3.7 add_convert_fusion.1
  382.8 1.5 collective-permute-start.41
  385.2 1.4 collective-permute-start.8
  386.7 94.0 %collective-permute-done.8 = bf16[128,512]{1,0:T(8,128)(2,1)S(1)} collective-permute-done((bf16[128,512]{1,0:T(8,128)(2,1)S(1)}, bf16[128,512]{1,0:T(8,128)(2,1)S(1)}, u32[]{:S(2)}, u32[]{:S(2)}) %collective-permute-start.8) | collective-permute-done | bytes 131104 | tf_op jit(solution)/shard_map/ppermute | solution.py:898
  480.7 4.0 collective-permute-start.15
  484.9 1.3 collective-permute-done.9
  486.4 1.1 collective-permute-start.24
  488.6 1.1 collective-permute-start.33
  491.4 2.6 collective-permute-done.24
  494.5 1.2 collective-permute-start.26
  495.7 1.9 collective-permute-start.27
  497.6 1.0 fusion.3
  498.7 1.1 collective-permute-start.42
  500.7 1.1 collective-permute-start.29
  501.9 14.6 %collective-permute-done.33 = bf16[4,128,1024]{2,1,0:T(8,128)(2,1)S(1)} collective-permute-done((bf16[4,128,1024]{2,1,0:T(8,128)(2,1)S(1)}, bf16[4,128,1024]{2,1,0:T(8,128)(2,1)S(1)}, u32[]{:S(2)}, u32[]{:S(2)}) %collective-permute-start.33) | collective-permute-done | bytes 1048608 | tf_op jit(solution)/shard_map/ppermute | solution.py:898
  517.2 1.2 collective-permute-start.35
  518.5 1.9 collective-permute-start.36
  520.4 1.4 add_add_fusion
  521.9 17.0 %collective-permute-done.42 = bf16[4,128,1024]{2,1,0:T(8,128)(2,1)S(1)} collective-permute-done((bf16[4,128,1024]{2,1,0:T(8,128)(2,1)S(1)}, bf16[4,128,1024]{2,1,0:T(8,128)(2,1)S(1)}, u32[]{:S(2)}, u32[]{:S(2)}) %collective-permute-start.42) | collective-permute-done | bytes 1048608 | tf_op jit(solution)/shard_map/ppermute | solution.py:898
  538.9 1.2 collective-permute-start.3
  541.4 2.6 collective-permute-start.45
  544.2 2.4 collective-permute-start.28
  546.6 4.9 collective-permute-done.43
  551.5 2.3 collective-permute-start.30
  553.8 3.7 collective-permute-done.45
  559.7 7.1 %collective-permute-start.37 = (bf16[128,1024]{1,0:T(8,128)(2,1)S(1)}, bf16[128,1024]{1,0:T(8,128)(2,1)S(1)}, u32[]{:S(2)}, u32[]{:S(2)}) collective-permute-start(bf16[128,1024]{1,0:T(8,128)(2,1)S(1)} %fusion.21), channel_id=1, source_target_pairs={{0,8},{1,9},{2,10},{3,11},{4,12},{5,13},{6,14},{7,15},{8,0},{9,1},... | collective-permute-start | bytes 786440 | tf_op jit(solution)/shard_map/ppermute | solution.py:898
  566.9 2.9 collective-permute-start.39
  569.7 2.8 collective-permute-start.48
  573.0 2.0 pad_maximum_fusion
  575.2 1.6 maximum_convert_fusion.1
  576.8 1.5 maximum_convert_fusion
  (152 shorter events, 32.2 us)
Async XLA Ops:
  222.0 35.7 %collective-permute-start.1 = (bf16[768,512]{1,0:T(8,128)(2,1)}, bf16[768,512]{1,0:T(8,128)(2,1)S(1)}, u32[]{:S(2)}, u32[]{:S(2)}) collective-permute-start(bf16[768,512]{1,0:T(8,128)(2,1)} %get-tuple-element.69), channel_id=1, source_target_pairs={{0,8},{1,9},{2,10},{3,11},{4,12},{5,13},{6,14},{7,15},{8,0},{9,1},... | collective-permute-start | bytes 2359304 | tf_op jit(solution)/shard_map/ppermute | solution.py:898
  235.2 131.1 %collective-permute-start.31 = (bf16[2,2,4,128,1024]{4,3,2,1,0:T(8,128)(2,1)}, bf16[2,2,4,128,1024]{4,3,2,1,0:T(8,128)(2,1)}, u32[]{:S(2)}, u32[]{:S(2)}) collective-permute-start(bf16[2,2,4,128,1024]{4,3,2,1,0:T(8,128)(2,1)} %get-tuple-element.83), channel_id=1, source_target_pairs={{0,8},{1,9},{2,10},{3,11},{4,12},{5,13},{6,14},{7,15},{8,0},{9,1},... | collective-permute-start | bytes 12582920 | tf_op jit(solution)/shard_map/ppermute | solution.py:898
  249.4 129.6 %collective-permute-start.40 = (bf16[2,2,4,128,1024]{4,3,2,1,0:T(8,128)(2,1)}, bf16[2,2,4,128,1024]{4,3,2,1,0:T(8,128)(2,1)}, u32[]{:S(2)}, u32[]{:S(2)}) collective-permute-start(bf16[2,2,4,128,1024]{4,3,2,1,0:T(8,128)(2,1)} %get-tuple-element.87), channel_id=1, source_target_pairs={{0,8},{1,9},{2,10},{3,11},{4,12},{5,13},{6,14},{7,15},{8,0},{9,1},... | collective-permute-start | bytes 12582920 | tf_op jit(solution)/shard_map/ppermute | solution.py:898
  249.5 6.3 %copy-start.5 = (bf16[768,1024]{1,0:T(8,128)(2,1)S(1)}, bf16[768,1024]{1,0:T(8,128)(2,1)}, u32[]{:S(2)}) copy-start(bf16[768,1024]{1,0:T(8,128)(2,1)} %get-tuple-element.62) | copy-start | bytes 4718596
  255.4 70.7 %collective-permute-start.22 = (bf16[2,2,4,32,1024]{4,3,2,1,0:T(8,128)(2,1)}, bf16[2,2,4,32,1024]{4,3,2,1,0:T(8,128)(2,1)S(1)}, u32[]{:S(2)}, u32[]{:S(2)}) collective-permute-start(bf16[2,2,4,32,1024]{4,3,2,1,0:T(8,128)(2,1)} %get-tuple-element.79), channel_id=1, source_target_pairs={{0,8},{1,9},{2,10},{3,11},{4,12},{5,13},{6,14},{7,15},{8,0},{9,1},... | collective-permute-start | bytes 3145736 | tf_op jit(solution)/shard_map/ppermute | solution.py:898
  256.8 46.7 %collective-permute-start = (bf16[3,128,1024]{2,1,0:T(8,128)(2,1)}, bf16[3,128,1024]{2,1,0:T(8,128)(2,1)}, u32[]{:S(2)}, u32[]{:S(2)}) collective-permute-start(bf16[3,128,1024]{2,1,0:T(8,128)(2,1)} %bitcast.15), channel_id=1, source_target_pairs={{0,16},{1,17},{2,18},{3,19},{4,20},{5,21},{6,22},{7,23},{8,24},{9,... | collective-permute-start | bytes 2359304 | tf_op jit(solution)/shard_map/ppermute | solution.py:898
  289.1 6.8 %copy-start.11 = (f32[16,1024]{1,0:T(8,128)S(1)}, f32[16,1024]{1,0:T(8,128)}, u32[]{:S(2)}) copy-start(f32[16,1024]{1,0:T(8,128)} %get-tuple-element.88) | copy-start | bytes 196612
  296.0 10.1 %collective-permute-start.49 = (f32[16,1024]{1,0:T(8,128)S(1)}, f32[16,1024]{1,0:T(8,128)S(1)}, u32[]{:S(2)}, u32[]{:S(2)}) collective-permute-start(f32[16,1024]{1,0:T(8,128)S(1)} %maximum_add_fusion), channel_id=1, source_target_pairs={{0,8},{1,9},{2,10},{3,11},{4,12},{5,13},{6,14},{7,15},{8,0},{9,1},... | collective-permute-start | bytes 196616 | tf_op jit(solution)/shard_map/ppermute | solution.py:898
  303.5 29.3 %collective-permute-start.10 = (bf16[4,128,512]{2,1,0:T(8,128)(2,1)S(1)}, bf16[4,128,512]{2,1,0:T(8,128)(2,1)}, u32[]{:S(2)}, u32[]{:S(2)}) collective-permute-start(bf16[4,128,512]{2,1,0:T(8,128)(2,1)S(1)} %slice_bitcast_fusion.5), channel_id=1, source_target_pairs={{0,1},{1,0},{2,3},{3,2},{4,5},{5,4},{6,7},{7,6},{8,9},{9,8},{10,11... | collective-permute-start | bytes 1572872 | tf_op jit(solution)/shard_map/ppermute | solution.py:898
  306.1 8.4 %collective-permute-start.50 = (f32[16,1024]{1,0:T(8,128)S(1)}, f32[16,1024]{1,0:T(8,128)S(1)}, u32[]{:S(2)}, u32[]{:S(2)}) collective-permute-start(f32[16,1024]{1,0:T(8,128)S(1)} %add.317), channel_id=1, source_target_pairs={{0,16},{1,17},{2,18},{3,19},{4,20},{5,21},{6,22},{7,23},{8,24},{9,... | collective-permute-start | bytes 196616 | tf_op jit(solution)/shard_map/ppermute | solution.py:898
  314.6 7.6 %collective-permute-start.51 = (f32[16,1024]{1,0:T(8,128)S(1)}, f32[16,1024]{1,0:T(8,128)S(1)}, u32[]{:S(2)}, u32[]{:S(2)}) collective-permute-start(f32[16,1024]{1,0:T(8,128)S(1)} %add.318), channel_id=1, source_target_pairs={{0,1},{1,0},{2,3},{3,2},{4,5},{5,4},{6,7},{7,6},{8,9},{9,8},{10,11... | collective-permute-start | bytes 196616 | tf_op jit(solution)/shard_map/ppermute | solution.py:898
  322.1 3.2 copy-start.10
  322.1 4.8 copy-start.6
  322.2 3.2 collective-permute-start.52
  323.9 9.0 %copy-start.9 = (bf16[2,4,128,512]{3,2,1,0:T(8,128)(2,1)S(1)}, bf16[2,4,128,512]{3,2,1,0:T(8,128)(2,1)}, u32[]{:S(2)}) copy-start(bf16[2,4,128,512]{3,2,1,0:T(8,128)(2,1)} %get-tuple-element.75) | copy-start | bytes 3145732
  325.3 11.3 %collective-permute-start.16 = (bf16[4,128,512]{2,1,0:T(8,128)(2,1)S(1)}, bf16[4,128,512]{2,1,0:T(8,128)(2,1)S(1)}, u32[]{:S(2)}, u32[]{:S(2)}) collective-permute-start(bf16[4,128,512]{2,1,0:T(8,128)(2,1)S(1)} %copy-done.10), channel_id=1, source_target_pairs={{0,1},{1,0},{2,3},{3,2},{4,5},{5,4},{6,7},{7,6},{8,9},{9,8},{10,11... | collective-permute-start | bytes 1572872 | tf_op jit(solution)/shard_map/ppermute | solution.py:898
  326.1 4.5 collective-permute-start.53
  327.0 29.0 %copy-start.4 = (f32[768,1024]{1,0:T(8,128)S(1)}, f32[768,1024]{1,0:T(8,128)}, u32[]{:S(2)}) copy-start(f32[768,1024]{1,0:T(8,128)} %back_project.3) | copy-start | bytes 9437188
  330.6 17.2 %collective-permute-start.4 = (bf16[4,128,512]{2,1,0:T(8,128)(2,1)S(1)}, bf16[4,128,512]{2,1,0:T(8,128)(2,1)S(1)}, u32[]{:S(2)}, u32[]{:S(2)}) collective-permute-start(bf16[4,128,512]{2,1,0:T(8,128)(2,1)S(1)} %slice_bitcast_fusion.6), channel_id=1, source_target_pairs={{0,1},{1,0},{2,3},{3,2},{4,5},{5,4},{6,7},{7,6},{8,9},{9,8},{10,11... | collective-permute-start | bytes 1572872 | tf_op jit(solution)/shard_map/ppermute | solution.py:898
  332.9 35.4 %copy-start.2 = (bf16[2,2,4,128,1024]{4,3,2,1,0:T(8,128)(2,1)S(1)}, bf16[2,2,4,128,1024]{4,3,2,1,0:T(8,128)(2,1)}, u32[]{:S(2)}) copy-start(bf16[2,2,4,128,1024]{4,3,2,1,0:T(8,128)(2,1)} %get-tuple-element.82) | copy-start | bytes 12582916
  334.2 15.1 %collective-permute-start.11 = (bf16[128,512]{1,0:T(8,128)(2,1)S(1)}, bf16[128,512]{1,0:T(8,128)(2,1)S(1)}, u32[]{:S(2)}, u32[]{:S(2)}) collective-permute-start(bf16[128,512]{1,0:T(8,128)(2,1)S(1)} %get-tuple-element.112), channel_id=1, source_target_pairs={{0,2},{1,3},{2,0},{3,1},{4,6},{5,7},{6,4},{7,5},{8,10},{9,11},{10,... | collective-permute-start | bytes 393224 | tf_op jit(solution)/shard_map/ppermute | solution.py:898
  336.6 13.0 %collective-permute-start.12 = (bf16[128,512]{1,0:T(8,128)(2,1)S(1)}, bf16[128,512]{1,0:T(8,128)(2,1)S(1)}, u32[]{:S(2)}, u32[]{:S(2)}) collective-permute-start(bf16[128,512]{1,0:T(8,128)(2,1)S(1)} %get-tuple-element.114), channel_id=1, source_target_pairs={{0,4},{1,5},{2,6},{3,7},{4,0},{5,1},{6,2},{7,3},{8,12},{9,13},{10,... | collective-permute-start | bytes 393224 | tf_op jit(solution)/shard_map/ppermute | solution.py:898
  347.9 5.8 collective-permute-start.13
  349.3 6.7 %collective-permute-start.17 = (bf16[128,512]{1,0:T(8,128)(2,1)S(1)}, bf16[128,512]{1,0:T(8,128)(2,1)S(1)}, u32[]{:S(2)}, u32[]{:S(2)}) collective-permute-start(bf16[128,512]{1,0:T(8,128)(2,1)S(1)} %get-tuple-element.109), channel_id=1, source_target_pairs={{0,2},{1,3},{2,0},{3,1},{4,6},{5,7},{6,4},{7,5},{8,10},{9,11},{10,... | collective-permute-start | bytes 393224 | tf_op jit(solution)/shard_map/ppermute | solution.py:898
  349.6 11.6 %collective-permute-start.18 = (bf16[128,512]{1,0:T(8,128)(2,1)S(1)}, bf16[128,512]{1,0:T(8,128)(2,1)S(1)}, u32[]{:S(2)}, u32[]{:S(2)}) collective-permute-start(bf16[128,512]{1,0:T(8,128)(2,1)S(1)} %get-tuple-element.111), channel_id=1, source_target_pairs={{0,4},{1,5},{2,6},{3,7},{4,0},{5,1},{6,2},{7,3},{8,12},{9,13},{10,... | collective-permute-start | bytes 393224 | tf_op jit(solution)/shard_map/ppermute | solution.py:898
  353.6 12.3 %collective-permute-start.19 = (bf16[128,512]{1,0:T(8,128)(2,1)S(1)}, bf16[128,512]{1,0:T(8,128)(2,1)S(1)}, u32[]{:S(2)}, u32[]{:S(2)}) collective-permute-start(bf16[128,512]{1,0:T(8,128)(2,1)S(1)} %get-tuple-element.110), channel_id=1, source_target_pairs={{0,6},{1,7},{2,4},{3,5},{4,2},{5,3},{6,0},{7,1},{8,14},{9,15},{10,... | collective-permute-start | bytes 393224 | tf_op jit(solution)/shard_map/ppermute | solution.py:898
  356.0 162.4 %collective-permute-start.2 = (f32[768,1024]{1,0:T(8,128)S(1)}, f32[768,1024]{1,0:T(8,128)S(1)}, u32[]{:S(2)}, u32[]{:S(2)}) collective-permute-start(f32[768,1024]{1,0:T(8,128)S(1)} %copy-done.4), channel_id=1, source_target_pairs={{0,8},{1,9},{2,10},{3,11},{4,12},{5,13},{6,14},{7,15},{8,0},{9,1},... | collective-permute-start | bytes 9437192 | tf_op jit(solution)/shard_map/ppermute | solution.py:898
  361.3 10.7 %collective-permute-start.5 = (bf16[128,512]{1,0:T(8,128)(2,1)S(1)}, bf16[128,512]{1,0:T(8,128)(2,1)S(1)}, u32[]{:S(2)}, u32[]{:S(2)}) collective-permute-start(bf16[128,512]{1,0:T(8,128)(2,1)S(1)} %get-tuple-element.115), channel_id=1, source_target_pairs={{0,2},{1,3},{2,0},{3,1},{4,6},{5,7},{6,4},{7,5},{8,10},{9,11},{10,... | collective-permute-start | bytes 393224 | tf_op jit(solution)/shard_map/ppermute | solution.py:898
  365.9 11.5 %collective-permute-start.6 = (bf16[128,512]{1,0:T(8,128)(2,1)S(1)}, bf16[128,512]{1,0:T(8,128)(2,1)S(1)}, u32[]{:S(2)}, u32[]{:S(2)}) collective-permute-start(bf16[128,512]{1,0:T(8,128)(2,1)S(1)} %get-tuple-element.117), channel_id=1, source_target_pairs={{0,4},{1,5},{2,6},{3,7},{4,0},{5,1},{6,2},{7,3},{8,12},{9,13},{10,... | collective-permute-start | bytes 393224 | tf_op jit(solution)/shard_map/ppermute | solution.py:898
  366.4 11.1 %collective-permute-start.7 = (bf16[128,512]{1,0:T(8,128)(2,1)S(1)}, bf16[128,512]{1,0:T(8,128)(2,1)S(1)}, u32[]{:S(2)}, u32[]{:S(2)}) collective-permute-start(bf16[128,512]{1,0:T(8,128)(2,1)S(1)} %get-tuple-element.116), channel_id=1, source_target_pairs={{0,6},{1,7},{2,4},{3,5},{4,2},{5,3},{6,0},{7,1},{8,14},{9,15},{10,... | collective-permute-start | bytes 393224 | tf_op jit(solution)/shard_map/ppermute | solution.py:898
  368.3 10.8 %copy-start.1 = (bf16[2,2,4,128,1024]{4,3,2,1,0:T(8,128)(2,1)S(1)}, bf16[2,2,4,128,1024]{4,3,2,1,0:T(8,128)(2,1)}, u32[]{:S(2)}) copy-start(bf16[2,2,4,128,1024]{4,3,2,1,0:T(8,128)(2,1)} %get-tuple-element.86) | copy-start | bytes 12582916
  372.0 10.8 %collective-permute-start.23 = (bf16[2,4,32,1024]{3,2,1,0:T(8,128)(2,1)S(1)}, bf16[2,4,32,1024]{3,2,1,0:T(8,128)(2,1)S(1)}, u32[]{:S(2)}, u32[]{:S(2)}) collective-permute-start(bf16[2,4,32,1024]{3,2,1,0:T(8,128)(2,1)S(1)} %get-tuple-element.108), channel_id=1, source_target_pairs={{0,16},{1,17},{2,18},{3,19},{4,20},{5,21},{6,22},{7,23},{8,24},{9,... | collective-permute-start | bytes 1572872 | tf_op jit(solution)/shard_map/ppermute | solution.py:898
  377.4 7.8 %collective-permute-start.14 = (bf16[128,512]{1,0:T(8,128)(2,1)S(1)}, bf16[128,512]{1,0:T(8,128)(2,1)S(1)}, u32[]{:S(2)}, u32[]{:S(2)}) collective-permute-start(bf16[128,512]{1,0:T(8,128)(2,1)S(1)} %add_convert_fusion.9), channel_id=1, source_target_pairs={{0,16},{1,17},{2,18},{3,19},{4,20},{5,21},{6,22},{7,23},{8,24},{9,... | collective-permute-start | bytes 393224 | tf_op jit(solution)/shard_map/ppermute | solution.py:898
  377.4 110.2 %collective-permute-start.32 = (bf16[2,4,128,1024]{3,2,1,0:T(8,128)(2,1)S(1)}, bf16[2,4,128,1024]{3,2,1,0:T(8,128)(2,1)S(1)}, u32[]{:S(2)}, u32[]{:S(2)}) collective-permute-start(bf16[2,4,128,1024]{3,2,1,0:T(8,128)(2,1)S(1)} %get-tuple-element.94), channel_id=1, source_target_pairs={{0,16},{1,17},{2,18},{3,19},{4,20},{5,21},{6,22},{7,23},{8,24},{9,... | collective-permute-start | bytes 6291464 | tf_op jit(solution)/shard_map/ppermute | solution.py:898
  379.0 105.8 %collective-permute-start.20 = (bf16[128,512]{1,0:T(8,128)(2,1)S(1)}, bf16[128,512]{1,0:T(8,128)(2,1)S(1)}, u32[]{:S(2)}, u32[]{:S(2)}) collective-permute-start(bf16[128,512]{1,0:T(8,128)(2,1)S(1)} %add_convert_fusion.7), channel_id=1, source_target_pairs={{0,16},{1,17},{2,18},{3,19},{4,20},{5,21},{6,22},{7,23},{8,24},{9,... | collective-permute-start | bytes 393224 | tf_op jit(solution)/shard_map/ppermute | solution.py:898
  382.8 112.9 %collective-permute-start.41 = (bf16[2,4,128,1024]{3,2,1,0:T(8,128)(2,1)S(1)}, bf16[2,4,128,1024]{3,2,1,0:T(8,128)(2,1)S(1)}, u32[]{:S(2)}, u32[]{:S(2)}) collective-permute-start(bf16[2,4,128,1024]{3,2,1,0:T(8,128)(2,1)S(1)} %get-tuple-element.92), channel_id=1, source_target_pairs={{0,16},{1,17},{2,18},{3,19},{4,20},{5,21},{6,22},{7,23},{8,24},{9,... | collective-permute-start | bytes 6291464 | tf_op jit(solution)/shard_map/ppermute | solution.py:898
  385.2 95.5 %collective-permute-start.8 = (bf16[128,512]{1,0:T(8,128)(2,1)S(1)}, bf16[128,512]{1,0:T(8,128)(2,1)S(1)}, u32[]{:S(2)}, u32[]{:S(2)}) collective-permute-start(bf16[128,512]{1,0:T(8,128)(2,1)S(1)} %add_convert_fusion.11), channel_id=1, source_target_pairs={{0,16},{1,17},{2,18},{3,19},{4,20},{5,21},{6,22},{7,23},{8,24},{9,... | collective-permute-start | bytes 393224 | tf_op jit(solution)/shard_map/ppermute | solution.py:898
  480.7 5.6 collective-permute-start.15
  484.8 1.4 collective-permute-start.9
  486.2 1.3 collective-permute-start.21
  486.4 7.6 %collective-permute-start.24 = (bf16[4,32,1024]{2,1,0:T(8,128)(2,1)S(1)}, bf16[4,32,1024]{2,1,0:T(8,128)(2,1)S(1)}, u32[]{:S(2)}, u32[]{:S(2)}) collective-permute-start(bf16[4,32,1024]{2,1,0:T(8,128)(2,1)S(1)} %get-tuple-element.131), channel_id=1, source_target_pairs={{0,1},{1,0},{2,3},{3,2},{4,5},{5,4},{6,7},{7,6},{8,9},{9,8},{10,11... | collective-permute-start | bytes 786440 | tf_op jit(solution)/shard_map/ppermute | solution.py:898
  488.6 27.9 %collective-permute-start.33 = (bf16[4,128,1024]{2,1,0:T(8,128)(2,1)S(1)}, bf16[4,128,1024]{2,1,0:T(8,128)(2,1)S(1)}, u32[]{:S(2)}, u32[]{:S(2)}) collective-permute-start(bf16[4,128,1024]{2,1,0:T(8,128)(2,1)S(1)} %get-tuple-element.98), channel_id=1, source_target_pairs={{0,1},{1,0},{2,3},{3,2},{4,5},{5,4},{6,7},{7,6},{8,9},{9,8},{10,11... | collective-permute-start | bytes 3145736 | tf_op jit(solution)/shard_map/ppermute | solution.py:898
  494.0 4.7 collective-permute-start.25
  494.5 6.1 %collective-permute-start.26 = (bf16[32,1024]{1,0:T(8,128)(2,1)S(1)}, bf16[32,1024]{1,0:T(8,128)(2,1)S(1)}, u32[]{:S(2)}, u32[]{:S(2)}) collective-permute-start(bf16[32,1024]{1,0:T(8,128)(2,1)S(1)} %get-tuple-element.134), channel_id=1, source_target_pairs={{0,4},{1,5},{2,6},{3,7},{4,0},{5,1},{6,2},{7,3},{8,12},{9,13},{10,... | collective-permute-start | bytes 196616 | tf_op jit(solution)/shard_map/ppermute | solution.py:898
  495.7 4.9 collective-permute-start.27
  497.6 22.7 %copy-start.3 = (f32[768,1024]{1,0:T(8,128)S(1)}, f32[768,1024]{1,0:T(8,128)}, u32[]{:S(2)}) copy-start(f32[768,1024]{1,0:T(8,128)} %get-tuple-element.63) | copy-start | bytes 9437188
  498.7 21.7 %copy-start = (f32[768,1024]{1,0:T(8,128)S(1)}, f32[768,1024]{1,0:T(8,128)}, u32[]{:S(2)}) copy-start(f32[768,1024]{1,0:T(8,128)} %back_project.2) | copy-start | bytes 9437188
  498.7 40.2 %collective-permute-start.42 = (bf16[4,128,1024]{2,1,0:T(8,128)(2,1)S(1)}, bf16[4,128,1024]{2,1,0:T(8,128)(2,1)S(1)}, u32[]{:S(2)}, u32[]{:S(2)}) collective-permute-start(bf16[4,128,1024]{2,1,0:T(8,128)(2,1)S(1)} %get-tuple-element.96), channel_id=1, source_target_pairs={{0,1},{1,0},{2,3},{3,2},{4,5},{5,4},{6,7},{7,6},{8,9},{9,8},{10,11... | collective-permute-start | bytes 3145736 | tf_op jit(solution)/shard_map/ppermute | solution.py:898
  500.7 43.5 %collective-permute-start.29 = (bf16[32,1024]{1,0:T(8,128)(2,1)S(1)}, bf16[32,1024]{1,0:T(8,128)(2,1)S(1)}, u32[]{:S(2)}, u32[]{:S(2)}) collective-permute-start(bf16[32,1024]{1,0:T(8,128)(2,1)S(1)} %fusion.51), channel_id=1, source_target_pairs={{0,16},{1,17},{2,18},{3,19},{4,20},{5,21},{6,22},{7,23},{8,24},{9,... | collective-permute-start | bytes 196616 | tf_op jit(solution)/shard_map/ppermute | solution.py:898
  516.7 23.6 %collective-permute-start.34 = (bf16[128,1024]{1,0:T(8,128)(2,1)S(1)}, bf16[128,1024]{1,0:T(8,128)(2,1)S(1)}, u32[]{:S(2)}, u32[]{:S(2)}) collective-permute-start(bf16[128,1024]{1,0:T(8,128)(2,1)S(1)} %get-tuple-element.104), channel_id=1, source_target_pairs={{0,2},{1,3},{2,0},{3,1},{4,6},{5,7},{6,4},{7,5},{8,10},{9,11},{10,... | collective-permute-start | bytes 786440 | tf_op jit(solution)/shard_map/ppermute | solution.py:898
  517.2 23.2 %collective-permute-start.35 = (bf16[128,1024]{1,0:T(8,128)(2,1)S(1)}, bf16[128,1024]{1,0:T(8,128)(2,1)S(1)}, u32[]{:S(2)}, u32[]{:S(2)}) collective-permute-start(bf16[128,1024]{1,0:T(8,128)(2,1)S(1)} %get-tuple-element.106), channel_id=1, source_target_pairs={{0,4},{1,5},{2,6},{3,7},{4,0},{5,1},{6,2},{7,3},{8,12},{9,13},{10,... | collective-permute-start | bytes 786440 | tf_op jit(solution)/shard_map/ppermute | solution.py:898
  518.5 22.9 %collective-permute-start.36 = (bf16[128,1024]{1,0:T(8,128)(2,1)S(1)}, bf16[128,1024]{1,0:T(8,128)(2,1)S(1)}, u32[]{:S(2)}, u32[]{:S(2)}) collective-permute-start(bf16[128,1024]{1,0:T(8,128)(2,1)S(1)} %get-tuple-element.105), channel_id=1, source_target_pairs={{0,6},{1,7},{2,4},{3,5},{4,2},{5,3},{6,0},{7,1},{8,14},{9,15},{10,... | collective-permute-start | bytes 786440 | tf_op jit(solution)/shard_map/ppermute | solution.py:898
  538.9 33.6 %collective-permute-start.3 = (bf16[3,128,1024]{2,1,0:T(8,128)(2,1)S(1)}, bf16[3,128,1024]{2,1,0:T(8,128)(2,1)S(1)}, u32[]{:S(2)}, u32[]{:S(2)}) collective-permute-start(bf16[3,128,1024]{2,1,0:T(8,128)(2,1)S(1)} %bitcast.302), channel_id=1, source_target_pairs={{0,16},{1,17},{2,18},{3,19},{4,20},{5,21},{6,22},{7,23},{8,24},{9,... | collective-permute-start | bytes 2359304 | tf_op jit(solution)/shard_map/ppermute | solution.py:898
  540.4 11.1 %collective-permute-start.43 = (bf16[128,1024]{1,0:T(8,128)(2,1)S(1)}, bf16[128,1024]{1,0:T(8,128)(2,1)S(1)}, u32[]{:S(2)}, u32[]{:S(2)}) collective-permute-start(bf16[128,1024]{1,0:T(8,128)(2,1)S(1)} %get-tuple-element.101), channel_id=1, source_target_pairs={{0,2},{1,3},{2,0},{3,1},{4,6},{5,7},{6,4},{7,5},{8,10},{9,11},{10,... | collective-permute-start | bytes 786440 | tf_op jit(solution)/shard_map/ppermute | solution.py:898
  540.4 13.3 %collective-permute-start.44 = (bf16[128,1024]{1,0:T(8,128)(2,1)S(1)}, bf16[128,1024]{1,0:T(8,128)(2,1)S(1)}, u32[]{:S(2)}, u32[]{:S(2)}) collective-permute-start(bf16[128,1024]{1,0:T(8,128)(2,1)S(1)} %get-tuple-element.103), channel_id=1, source_target_pairs={{0,4},{1,5},{2,6},{3,7},{4,0},{5,1},{6,2},{7,3},{8,12},{9,13},{10,... | collective-permute-start | bytes 786440 | tf_op jit(solution)/shard_map/ppermute | solution.py:898
  541.4 16.1 %collective-permute-start.45 = (bf16[128,1024]{1,0:T(8,128)(2,1)S(1)}, bf16[128,1024]{1,0:T(8,128)(2,1)S(1)}, u32[]{:S(2)}, u32[]{:S(2)}) collective-permute-start(bf16[128,1024]{1,0:T(8,128)(2,1)S(1)} %get-tuple-element.102), channel_id=1, source_target_pairs={{0,6},{1,7},{2,4},{3,5},{4,2},{5,3},{6,0},{7,1},{8,14},{9,15},{10,... | collective-permute-start | bytes 786440 | tf_op jit(solution)/shard_map/ppermute | solution.py:898
  544.2 14.5 %collective-permute-start.28 = (bf16[32,1024]{1,0:T(8,128)(2,1)S(1)}, bf16[32,1024]{1,0:T(8,128)(2,1)S(1)}, u32[]{:S(2)}, u32[]{:S(2)}) collective-permute-start(bf16[32,1024]{1,0:T(8,128)(2,1)S(1)} %fusion.51), channel_id=1, source_target_pairs={{0,8},{1,9},{2,10},{3,11},{4,12},{5,13},{6,14},{7,15},{8,0},{9,1},... | collective-permute-start | bytes 196616 | tf_op jit(solution)/shard_map/ppermute | solution.py:898
  551.5 7.2 %collective-permute-start.30 = (bf16[32,1024]{1,0:T(8,128)(2,1)S(1)}, bf16[32,1024]{1,0:T(8,128)(2,1)S(1)}, u32[]{:S(2)}, u32[]{:S(2)}) collective-permute-start(bf16[32,1024]{1,0:T(8,128)(2,1)S(1)} %collective-permute-done.29), channel_id=1, source_target_pairs={{0,8},{1,9},{2,10},{3,11},{4,12},{5,13},{6,14},{7,15},{8,0},{9,1},... | collective-permute-start | bytes 196616 | tf_op jit(solution)/shard_map/ppermute | solution.py:898
  553.8 13.1 %collective-permute-start.38 = (bf16[128,1024]{1,0:T(8,128)(2,1)S(1)}, bf16[128,1024]{1,0:T(8,128)(2,1)S(1)}, u32[]{:S(2)}, u32[]{:S(2)}) collective-permute-start(bf16[128,1024]{1,0:T(8,128)(2,1)S(1)} %fusion.21), channel_id=1, source_target_pairs={{0,16},{1,17},{2,18},{3,19},{4,20},{5,21},{6,22},{7,23},{8,24},{9,... | collective-permute-start | bytes 786440 | tf_op jit(solution)/shard_map/ppermute | solution.py:898
  557.7 12.0 %collective-permute-start.47 = (bf16[128,1024]{1,0:T(8,128)(2,1)S(1)}, bf16[128,1024]{1,0:T(8,128)(2,1)S(1)}, u32[]{:S(2)}, u32[]{:S(2)}) collective-permute-start(bf16[128,1024]{1,0:T(8,128)(2,1)S(1)} %fusion.14), channel_id=1, source_target_pairs={{0,16},{1,17},{2,18},{3,19},{4,20},{5,21},{6,22},{7,23},{8,24},{9,... | collective-permute-start | bytes 786440 | tf_op jit(solution)/shard_map/ppermute | solution.py:898
  559.7 15.3 %collective-permute-start.37 = (bf16[128,1024]{1,0:T(8,128)(2,1)S(1)}, bf16[128,1024]{1,0:T(8,128)(2,1)S(1)}, u32[]{:S(2)}, u32[]{:S(2)}) collective-permute-start(bf16[128,1024]{1,0:T(8,128)(2,1)S(1)} %fusion.21), channel_id=1, source_target_pairs={{0,8},{1,9},{2,10},{3,11},{4,12},{5,13},{6,14},{7,15},{8,0},{9,1},... | collective-permute-start | bytes 786440 | tf_op jit(solution)/shard_map/ppermute | solution.py:898
  566.8 8.2 %collective-permute-start.46 = (bf16[128,1024]{1,0:T(8,128)(2,1)S(1)}, bf16[128,1024]{1,0:T(8,128)(2,1)S(1)}, u32[]{:S(2)}, u32[]{:S(2)}) collective-permute-start(bf16[128,1024]{1,0:T(8,128)(2,1)S(1)} %fusion.14), channel_id=1, source_target_pairs={{0,8},{1,9},{2,10},{3,11},{4,12},{5,13},{6,14},{7,15},{8,0},{9,1},... | collective-permute-start | bytes 786440 | tf_op jit(solution)/shard_map/ppermute | solution.py:898
  566.9 8.1 %collective-permute-start.39 = (bf16[128,1024]{1,0:T(8,128)(2,1)S(1)}, bf16[128,1024]{1,0:T(8,128)(2,1)S(1)}, u32[]{:S(2)}, u32[]{:S(2)}) collective-permute-start(bf16[128,1024]{1,0:T(8,128)(2,1)S(1)} %collective-permute-done.38), channel_id=1, source_target_pairs={{0,8},{1,9},{2,10},{3,11},{4,12},{5,13},{6,14},{7,15},{8,0},{9,1},... | collective-permute-start | bytes 786440 | tf_op jit(solution)/shard_map/ppermute | solution.py:898
  569.7 5.3 collective-permute-start.48
  (3 other events, 5.9 us)

commit v3 on v2

--- a/solution.py
+++ b/solution.py
@@ -15,6 +15,7 @@
 NT = (((1,), (1,)), ((), ()))
 TN = (((0,), (0,)), ((), ()))
 VMEM_LIMIT = 58 << 20
+BACK_LIMIT = 60 << 20
 
 
 def dot(a, b):
@@ -421,15 +422,7 @@
     return jnp.where(own, o0, o1).astype(BF), jnp.where(own, l1, l0)
 
 
-def attend_back_kernel(
-    ids, lens, q_ref, k_ref, v_ref, lse_ref, c_ref, gm_ref, gs_ref, dq_ref, dk_ref, dv_ref
-):
-    q, k, v, c = flat(q_ref), flat(k_ref), flat(v_ref), flat(c_ref)
-    mask = key_mask(
-        lens[(ids[0] // 2) * pl.num_programs(0) + pl.program_id(0)], ids[0], q_ref.shape[2]
-    )
-    lse = lse_ref[0]
-    g = jnp.concatenate([flat(gm_ref), flat(gs_ref)], 0)
+def attend_back_pair(q, k, v, mask, lse, c, g):
     qs = q * BF(HD**-0.5)
     kt = k.T
     prod = c.astype(F32) * g.astype(F32)
@@ -462,43 +455,8 @@
         dqt = dot(kt, ds)
         res.append((dv, dk, dqt, own))
     (dv0, dk0, dq0, own), (dv1, dk1, dq1, _) = res
-    dv_ref[...] = jnp.where(own, dv0, dv1).astype(BF).reshape(dv_ref.shape)
-    dk_ref[...] = jnp.where(own, dk0, dk1).astype(BF).reshape(dk_ref.shape)
     dqt = jnp.concatenate([dq0[:HD], dq1[HD:]], 0) * (HD**-0.5)
-    dq_ref[...] = dqt.T.astype(BF).reshape(dq_ref.shape)
-
-
-def attend_back_call(ids, lens, q, k, v, lse, c, gm, gs):
-    slots, seqs, part, cols = q.shape
-    pair = 2 * HD
-    four = pl.BlockSpec((4, 1, part, pair), lambda s, h, *_: (0, s, 0, h))
-    two = pl.BlockSpec((2, 1, part, pair), lambda s, h, *_: (0, s, 0, h))
-    full = slots * part
-    out = jax.ShapeDtypeStruct(q.shape, BF)
-    grid_spec = pltpu.PrefetchScalarGridSpec(
-        num_scalar_prefetch=2,
-        grid=(seqs, cols // pair),
-        in_specs=[
-            four,
-            four,
-            four,
-            pl.BlockSpec((1, full, pair), lambda s, h, *_: (s, 0, h)),
-            four,
-            two,
-            two,
-        ],
-        out_specs=[four] * 3,
-    )
-    return pl.pallas_call(
-        attend_back_kernel,
-        grid_spec=grid_spec,
-        out_shape=[out] * 3,
-        compiler_params=params(),
-        cost_estimate=cost(
-            10 * seqs * full * full * cols * 4, 20 * seqs * full * cols, seqs * full * full * cols // HD
-        ),
-        name="attend_back",
-    )(ids, lens, q, k, v, lse, c, gm, gs)
+    return dqt.T.astype(BF), jnp.where(own, dk0, dk1).astype(BF), jnp.where(own, dv0, dv1).astype(BF)
 
 
 def gelu_pair(u):
@@ -679,183 +637,715 @@
     )(ids, lens, c, cr, xall, cot, vecs, wo, wi, wu)
 
 
-def outer_grad_kernel(ids, act, dout, keep, send, tmp):
-    tmp[...] = dot_tn(act[...], dout[...])
-    size = keep.shape[3]
-    for ec, ref in ((0, keep), (1, send)):
+def xor(a, b, count):
+    out, bit = 0, 1
+    while bit < count:
+        out = out + bit * ((a // bit + b // bit) % 2)
+        bit *= 2
+    return out
+
+
+def plus(*items):
+    out = items[0].astype(F32)
+    for i in items[1:]:
+        out = out + i.astype(F32)
+    return out.astype(BF)
+
+
+class Plan:
+    def __init__(self):
+        self.jobs = []
+
+    def add(self, time, job):
+        self.jobs.append((time, len(self.jobs), job))
+        self.jobs.sort(key=lambda j: j[:2])
+
+    def due(self, time):
+        out = [j[2] for j in self.jobs if j[0] <= time]
+        self.jobs = [j for j in self.jobs if j[0] > time]
+        return out
+
+    def beside(self, step, times):
+        for t, time in enumerate(times):
+            jobs = self.due(time)
+            if jobs:
+
+                @pl.when(step == t)
+                def _():
+                    for job in jobs:
+                        job()
+
+
+def back_kernel(
+    n,
+    lens,
+    act,
+    dout,
+    nrm,
+    dinn,
+    dattn,
+    ctx,
+    ctx2,
+    cr,
+    xall,
+    q_in,
+    k_in,
+    v_in,
+    lse_in,
+    dco,
+    dcs,
+    dfirst,
+    w_in,
+    lo,
+    acc,
+    o_lo,
+    o_igl,
+    o_igr,
+    o_i,
+    o_u,
+    o_o,
+    o_q,
+    o_k,
+    o_v,
+    o_vec,
+    act_s,
+    ig_s,
+    Q,
+    K,
+    V,
+    CX,
+    G,
+    LSE,
+    L,
+    D,
+    DO,
+    DA,
+    CO,
+    W,
+    PI,
+    PU,
+    PO,
+    PQ,
+    RYI,
+    RZI,
+    MI,
+    RXI,
+    RXU,
+    RYU,
+    RZU,
+    MU,
+    RYO,
+    RZO,
+    MO,
+    RXO,
+    RYQ,
+    RZQ,
+    MQ,
+    RXQ,
+    VS,
+    VR,
+    SB,
+    IB,
+    XS,
+    lsem,
+    ssem,
+    rsem,
+):
+    C, f = lax.axis_index("ctx"), lax.axis_index("fsdp")
+    x, core = C // 2, C % 2
+    A = n // 2
+    slots, sh, part, hw = Q.shape
+    rows, width = nrm.shape
+    ff = act.shape[1]
+    rs, ro, cq, wq = width // n, ff // n, ff // 4, width // 4
+    half_rows = rows // 2
+    CORE, NEAR, Y = (1, 0), (2, 0), (0, 1)
+
+    def device(dc, df):
+        return (flip(C, dc), flip(f, df))
+
+    partners = [(0, 2 * k) for k in range(1, A)] + [Y, NEAR, CORE]
+    barrier = pltpu.get_barrier_semaphore()
+    for p in partners:
+        pl.semaphore_signal(barrier, inc=1, device_id=device(*p), device_id_type=MESH)
+
+    locals_free = iter(range(lsem.shape[0]))
+    remotes_free = iter(range(ssem.shape[0]))
+
+    def local(make):
+        sem = next(locals_free)
+        return lambda: pltpu.make_async_copy(*make(), lsem.at[sem])
+
+    def remote_at(dev, sem, make):
+        source, target = make()
+        return pltpu.make_async_remote_copy(
+            src_ref=source,
+            dst_ref=target,
+            send_sem=ssem.at[sem],
+            recv_sem=rsem.at[sem],
+            device_id=device(*dev),
+            device_id_type=MESH,
+        )
+
+    def remote(dev, make):
+        sem = next(remotes_free)
+        return lambda: remote_at(dev, sem, make)
+
+    ends = []
+
+    def go(build):
+        build().start()
+        ends.append(lambda: build().wait_send())
+
+    def go_local(make):
+        build = local(make)
+        build().start()
+        ends.append(lambda: build().wait())
+
+    loads = {}
+
+    def load(name, make):
+        loads[name] = local(make)
+        loads[name]().start()
+
+    def need(*names):
+        for name in names:
+            loads.pop(name)().wait()
+
+    load("q", lambda: (q_in, Q))
+    load("k", lambda: (k_in, K))
+    load("v", lambda: (v_in, V))
+    load("c", lambda: (ctx, CX))
+    load("g", lambda: (dco, G.at[pl.ds(0, 2)]))
+    for s in range(2):
+        load(("lse", s), lambda s=s: (lse_in.at[s], LSE.at[s]))
+    load("nrm", lambda: (nrm, L.at[0]))
+    load("vec", lambda: (acc, VS.at[0]))
+
+    def quarters(ref, size, ex, ec):
+        return ref.at[:, at(flip(C, 2 * ex + ec), size)]
+
+    for ex in range(2):
+        load(("dinn", ex), lambda ex=ex: (quarters(dinn, cq, ex, 0), D.at[ex, 0]))
+
+    pl.semaphore_wait(barrier, len(partners))
+
+    g_swap = remote(CORE, lambda: (dcs, G.at[pl.ds(2, 2)]))
+    go(g_swap)
+    lo_swap = remote(NEAR, lambda: (lo.at[1], o_lo.at[pl.ds(x * sh, sh)]))
+    go(lo_swap)
+    go_local(lambda: (lo.at[0], o_lo.at[pl.ds(x * sh, sh)]))
+    nrm_swap = remote(CORE, lambda: (nrm, L.at[1]))
+    go(nrm_swap)
+    dinn_swap = [
+        remote(CORE, lambda ex=ex: (quarters(dinn, cq, ex, 1), D.at[ex, 1])) for ex in range(2)
+    ]
+    go(dinn_swap[0])
+    go(dinn_swap[1])
+
+    for ex in range(2):
+        load(
+            ("dout", ex),
+            lambda ex=ex: (quarters(dout, wq, ex, 0), DO.at[0, :, pl.ds(ex * wq, wq)]),
+        )
+        load(
+            ("dattn", ex),
+            lambda ex=ex: (quarters(dattn, wq, ex, 0), DA.at[0, :, pl.ds(ex * wq, wq)]),
+        )
+    load("co", lambda: (cr, CO.at[0]))
+    load("w", lambda: (w_in, W))
+
+    chunks = ff // 1024
+    per = 1024 // ro
+
+    def act_cols(t):
+        return at(xor(f // per, t, chunks), 1024)
+
+    dout_swap = [
+        remote(
+            CORE, lambda ex=ex: (quarters(dout, wq, ex, 1), DO.at[1, :, pl.ds(ex * wq, wq)])
+        )
+        for ex in range(2)
+    ]
+    act_swap = [
+        remote(CORE, lambda t=t: (act.at[:, act_cols(t)], act_s.at[:, act_cols(t)]))
+        for t in range(chunks)
+    ]
+    ctx_swap = remote(CORE, lambda: (ctx2.at[pl.ds(0, rows)], CO.at[1]))
+    dattn_swap = [
+        remote(
+            CORE, lambda ex=ex: (quarters(dattn, wq, ex, 1), DA.at[1, :, pl.ds(ex * wq, wq)])
+        )
+        for ex in range(2)
+    ]
+    need("q", "k", "v", "c", "g")
+    g_swap().wait_recv()
+    for build in dout_swap + act_swap + [ctx_swap] + dattn_swap:
+        go(build)
+
+    class Unit:
+        def __init__(self, P, RY, RZ, M):
+            self.P, self.RY, self.RZ, self.M = P, RY, RZ, M
+            self.y = [
+                remote(Y, lambda a=a: (P.at[1, a], RY.at[a])) for a in range(A)
+            ]
+            self.z = [None] + [
+                remote((0, 2 * a), lambda a=a: (P.at[0, a], RZ.at[a - 1])) for a in range(1, A)
+            ]
+
+        def start_y(self, a=None):
+            for i in order if a is None else [a]:
+                go(self.y[i])
+
+        def fold_y(self, a):
+            self.y[a]().wait_recv()
+            self.P[0, a] = plus(self.P[0, a], self.RY[a])
+            if a:
+                go(self.z[a])
+
+        def fold_z(self):
+            for a in range(1, A):
+                self.z[a]().wait_recv()
+            self.M[...] = plus(self.P[0, 0], *[self.RZ[a - 1] for a in range(1, A)])
+
+    order = list(range(1, A)) + [0]
+    UI = [Unit(PI.at[ex], RYI.at[ex], RZI.at[ex], MI.at[ex]) for ex in range(2)]
+    UU = Unit(PU.at[0], RYU, RZU, MU)
+    UO = Unit(PO, RYO, RZO, MO)
+    UQ = [Unit(PQ.at[j], RYQ.at[j], RZQ.at[j], MQ.at[j]) for j in range(3)]
+    plan = Plan()
+
+    xi = [remote(NEAR, lambda ex=ex: (MI.at[ex], RXI.at[ex])) for ex in range(2)]
+
+    def inner_z(ex):
+        UI[ex].fold_z()
+        go(xi[ex])
+
+    def cols_of(ref, e, size):
+        return ref.at[:, at(flip(C, e), size)]
+
+    i_core = [
+        remote(CORE, lambda ex=ex: (RXI.at[1 - ex], cols_of(o_i, 2 * ex, cq))) for ex in range(2)
+    ]
+
+    def inner_x():
         for ex in range(2):
-            ref[ex, 0, 0] = tmp[at(ids[0] ^ (2 * ex + ec), size), :].astype(BF)
-
-
-def outer_grad_call(ids, act, dout, n):
-    rows, ff = act.shape
-    width = dout.shape[1]
-    ro = ff // n
-    out = pl.BlockSpec((2, 1, 1, ro // 4, width), lambda i, s: (0, i % 2, i // 2, 0, 0))
-    grid_spec = pltpu.PrefetchScalarGridSpec(
-        num_scalar_prefetch=1,
-        grid=(n,),
-        in_specs=[
-            pl.BlockSpec((rows, ro), lambda i, s: (0, s[1] ^ i)),
-            pl.BlockSpec((rows, width), lambda i, s: (0, 0)),
+            xi[1 - ex]().wait_recv()
+            RXI[1 - ex] = plus(MI[ex], RXI[1 - ex])
+            go(i_core[ex])
+            go_local(lambda ex=ex: (RXI.at[1 - ex], cols_of(o_i, 2 * ex, cq)))
+
+    x_base = [next(remotes_free) for _ in range(n)][0]
+
+    def outer_copy(i):
+        return remote_at(NEAR, x_base + i, lambda: (PU.at[1, i % 2, i // 2], RXU.at[i % 2, i // 2]))
+
+    def outer_x(i):
+        outer_copy(i).wait_recv()
+        PU[0, i % 2, i // 2] = plus(PU[0, i % 2, i // 2], RXU[i % 2, i // 2])
+        if i % 2:
+            UU.start_y(i // 2)
+
+    u_near = remote(NEAR, lambda: (MU, cols_of(o_u, 0, wq)))
+    u_core = remote(CORE, lambda: (MU, cols_of(o_u, 0, wq)))
+    u_core2 = remote(CORE, lambda: (cols_of(o_u, 2, wq), cols_of(o_u, 2, wq)))
+
+    def outer_z():
+        UU.fold_z()
+        go(u_near)
+        go(u_core)
+        go_local(lambda: (MU, cols_of(o_u, 0, wq)))
+
+    def outer_end():
+        u_near().wait_recv()
+        go(u_core2)
+
+    xo = remote(NEAR, lambda: (MO, RXO))
+    o_core = [
+        remote(
+            CORE, lambda ex=ex: (RXO.at[pl.ds((1 - ex) * rs, rs)], cols_of(o_o, 2 * ex, wq))
+        )
+        for ex in range(2)
+    ]
+
+    def out_z():
+        UO.fold_z()
+        go(xo)
+
+    def out_x():
+        xo().wait_recv()
+        for ex in range(2):
+            mine, theirs = pl.ds(ex * rs, rs), pl.ds((1 - ex) * rs, rs)
+            RXO[theirs] = plus(MO[mine], RXO[theirs])
+            go(o_core[ex])
+            go_local(
+                lambda ex=ex: (RXO.at[pl.ds((1 - ex) * rs, rs)], cols_of(o_o, 2 * ex, wq))
+            )
+
+    outs = (o_q, o_k, o_v)
+    xq = [remote(NEAR, lambda j=j: (MQ.at[j], RXQ.at[j])) for j in range(3)]
+    q_core = [
+        remote(CORE, lambda j=j: (RXQ.at[j], outs[j].at[:, at(core, hw)])) for j in range(3)
+    ]
+
+    def proj_z(j):
+        UQ[j].fold_z()
+        go(xq[j])
+
+    def proj_x(j):
+        xq[j]().wait_recv()
+        RXQ[j] = plus(MQ[j], RXQ[j])
+        go(q_core[j])
+        go_local(lambda: (RXQ.at[j], outs[j].at[:, at(core, hw)]))
+
+    hops = [CORE, NEAR] + [(0, 1 << b) for b in range(n.bit_length() - 1)]
+    hop_copies = [
+        remote(dev, lambda t=t: (VS.at[t], VR.at[t])) for t, dev in enumerate(hops)
+    ]
+
+    def vector_hop(t):
+        if t:
+            hop_copies[t - 1]().wait_recv()
+            VS[t] = VS[t - 1] + VR[t - 1]
+        if t < len(hops):
+            go(hop_copies[t])
+        else:
+            go_local(lambda: (VS.at[t], o_vec))
+
+    pairs = hw // (2 * HD)
+
+    def attention(s, times):
+        need(("lse", s))
+
+        def body(step, carry):
+            cols = at(step, 2 * HD)
+
+            def get(ref):
+                return ref[:, s, :, cols].reshape(slots * part, 2 * HD)
+
+            mask = key_mask(lens[x * sh + s], C, part)
+            dq, dk, dv = attend_back_pair(
+                get(Q), get(K), get(V), mask, LSE[s % 2, :, cols], get(CX), get(G)
+            )
+            for ref, value in ((Q, dq), (K, dk), (V, dv)):
+                ref[:, s, :, cols] = value.reshape(slots, part, 2 * HD)
+            plan.beside(step, times)
+            return carry
+
+        lax.fori_loop(0, pairs, body, 0)
+        if s + 2 < sh:
+            load(("lse", s + 2), lambda: (lse_in.at[s + 2], LSE.at[s % 2]))
+
+    groups = width // 256
+    gsz = 256 // rs
+
+    def weight_grad(get, P, times):
+        def body(a, carry):
+            cols = at(xor(f // gsz, a, groups), 256)
+            r = (dot_tn(L[0, :, cols], get(0)) + dot_tn(L[1, :, cols], get(1))).astype(BF)
+            for u in range(gsz):
+                i = a * gsz + flip(f % gsz, u) if gsz > 1 else a
+                P[i % 2, i // 2] = r[u * rs : (u + 1) * rs]
+            plan.beside(a, times)
+            return carry
+
+        lax.fori_loop(0, groups, body, 0)
+
+    def spaced(first, last, count):
+        return [first + (last - first) * (t + 1) / count for t in range(count)]
+
+    for k, a in enumerate(order):
+        plan.add(27 + 6 * k, lambda a=a: UI[0].fold_y(a))
+        plan.add(51 + 6 * k, lambda a=a: UI[1].fold_y(a))
+        plan.add(78 + 3 * k, lambda a=a: UU.fold_y(a))
+        plan.add(80 + 2 * k, lambda a=a: UO.fold_y(a))
+        for j in range(3):
+            plan.add(92 + 10 * j + 3 * k, lambda a=a, j=j: UQ[j].fold_y(a))
+    xs_order = [t * per + il for t in range(chunks) for il in reversed(range(per))]
+    for k, i in enumerate(xs_order):
+        plan.add(30 + 6 * k, lambda i=i: outer_x(i))
+    plan.add(72, lambda: inner_z(0))
+    plan.add(88, lambda: inner_z(1))
+    plan.add(98, inner_x)
+    plan.add(104, outer_z)
+    plan.add(112, outer_end)
+    plan.add(106, out_z)
+    plan.add(114, out_x)
+    for j in range(3):
+        plan.add(115 + 6 * j, lambda j=j: proj_z(j))
+        plan.add(120 + 6 * j, lambda j=j: proj_x(j))
+    for t in range(len(hops) + 1):
+        plan.add(74 + 4 * t, lambda t=t: vector_hop(t))
+
+    attention(0, spaced(5, 13, pairs))
+    need("nrm", ("dinn", 0))
+    nrm_swap().wait_recv()
+    dinn_swap[0]().wait_recv()
+    weight_grad(lambda m: D[0, m], PI.at[0], spaced(13, 17, groups))
+    UI[0].start_y()
+
+    def act_load(t):
+        slot = t % 2
+        return [
+            pltpu.make_async_copy(act.at[:, act_cols(t)], D.at[slot, 0], lsem.at[act_sem + 2 * slot]),
+            pltpu.make_async_copy(
+                act_s.at[:, act_cols(t)], D.at[slot, 1], lsem.at[act_sem + 2 * slot + 1]
+            ),
+        ]
+
+    act_sem = [next(locals_free) for _ in range(4)][0]
+
+    def begin_act(t):
+        for c in act_load(t):
+            c.start()
+
+    act_swap[0]().wait_recv()
+    begin_act(0)
+    need(("dinn", 1))
+    dinn_swap[1]().wait_recv()
+    weight_grad(lambda m: D[1, m], PI.at[1], spaced(17, 20, groups))
+    UI[1].start_y()
+    for t in range(1, chunks):
+        act_swap[t]().wait_recv()
+    if chunks > 1:
+        begin_act(1)
+    load("x0", lambda: (xall.at[pl.ds(0, rows)], L.at[0]))
+    load("x1", lambda: (xall.at[pl.ds(rows, rows)], L.at[1]))
+    need(("dout", 0), ("dout", 1))
+    dout_swap[0]().wait_recv()
+    dout_swap[1]().wait_recv()
+
+    outer_times = spaced(20, 34, n)
+
+    def outer_body(u, carry):
+        t, il = u // per, per - 1 - u % per
+        slot = t % 2
+
+        @pl.when(u % per == 0)
+        def _():
+            for c in act_load(t):
+                c.wait()
+
+        cols = at(xor(f % per, il, per), ro)
+        r = dot_tn(D[slot, 0, :, cols], DO[0]) + dot_tn(D[slot, 1, :, cols], DO[1])
+        r = r.astype(BF)
+        i = t * per + il
+        for ex in range(2):
+            PU[ex, i % 2, i // 2] = r[:, ex * wq : (ex + 1) * wq]
+        outer_copy(i).start()
+
+        @pl.when((u % per == per - 1) & (t + 2 < chunks))
+        def _():
+            begin_act(t + 2)
+
+        plan.beside(u, outer_times)
+        return carry
+
+    lax.fori_loop(0, n, outer_body, 0)
+
+    need("co", ("dattn", 0), ("dattn", 1))
+    ctx_swap().wait_recv()
+    dattn_swap[0]().wait_recv()
+    dattn_swap[1]().wait_recv()
+    for half in range(2):
+        for g in range(hw // 256):
+            lanes = slice(g * 256, (g + 1) * 256)
+
+            def left(m):
+                if half:
+                    return CO[m, :, lanes]
+                return CX[2 * m : 2 * m + 2, :, :, lanes].reshape(rows, 256)
+
+            r = (dot_tn(left(0), DA[0]) + dot_tn(left(1), DA[1])).astype(BF)
+            group = (core + half * (1 - 2 * core)) * (hw // 256) + g
+            for u in range(gsz):
+                i = xor(group * gsz + u, f, n)
+                for ex in range(2):
+                    PO[i % 2, i // 2, ex * rs : (ex + 1) * rs] = r[
+                        u * rs : (u + 1) * rs, ex * wq : (ex + 1) * wq
+                    ]
+        for job in plan.due(36 + 3 * half):
+            job()
+    UO.start_y()
+
+    attention(1, spaced(39, 47, pairs))
+    for s in range(2, sh):
+        attention(s, spaced(47, 55, pairs))
+
+    need("x0", "x1", "vec")
+    for j, ref in enumerate((Q, K, V)):
+
+        def right(m):
+            return ref[2 * m : 2 * m + 2].reshape(rows, hw)
+
+        if j != 1:
+            total = jnp.sum(right(0).astype(F32), 0, keepdims=True)
+            total = total + jnp.sum(right(1).astype(F32), 0, keepdims=True)
+            VS[0, j // 2 : j // 2 + 1, at(core, hw)] = total
+        weight_grad(right, PQ.at[j], spaced(55 + 6 * j, 61 + 6 * j, groups))
+        UQ[j].start_y()
+
+    need("w")
+
+    def project(slot):
+        out = None
+        for j, ref in enumerate((Q, K, V)):
+            p = dot_nt(ref[slot].reshape(half_rows, hw), W[j])
+            out = p if out is None else out + p
+        return out
+
+    ig_swap = [remote(CORE, lambda ex=ex: (SB, ig_s.at[ex])) for ex in range(2)]
+    for ex in (1, 0):
+        value = project(2 + ex)
+        if ex == 0:
+            ig_swap[1]().wait_send()
+        SB[...] = value
+        ig_swap[ex]().start()
+        for job in plan.due(80 - 4 * ex):
+            job()
+
+    def rows_of(ex):
+        return pl.ds(ex * half_rows, half_rows)
+
+    ig_near = remote(NEAR, lambda: (XS, o_igr))
+    for ex in (1, 0):
+        ig_swap[ex]().wait_recv()
+        load(("ig", ex), lambda ex=ex: (ig_s.at[ex], IB))
+        value = project(ex)
+        if ex:
+            ig_swap[0]().wait_send()
+        load(("df", ex), lambda ex=ex: (dfirst.at[rows_of(ex)], SB))
+        need(("ig", ex), ("df", ex))
+        value = value + IB[...] + SB[...]
+        if ex:
+            XS[...] = value.astype(BF)
+            go(ig_near)
+        else:
+            IB[...] = value
+            go_local(lambda: (IB, o_igl))
+        for job in plan.due(88 - 4 * ex):
+            job()
+
+    for job in plan.due(1e9):
+        job()
+
+    lo_swap().wait_recv()
+    ig_near().wait_recv()
+    for build in i_core + [u_core, u_core2] + o_core + q_core:
+        build().wait_recv()
+    for i in range(n):
+        outer_copy(i).wait_send()
+    for end in ends:
+        end()
+
+
+def back_call(lens, n, act, dout, nrm, dinn, dattn, ctx, cr, xall, q, k, v, lse, dco, dcs, dfirst, w, lo, acc):
+    rows, width = nrm.shape
+    ff = act.shape[1]
+    slots, sh, part, hw = q.shape
+    A = n // 2
+    rs, ro, cq, wq = width // n, ff // n, ff // 4, width // 4
+    hops = 2 + n.bit_length() - 1
+
+    def bf(*shape):
+        return jax.ShapeDtypeStruct(shape, BF)
+
+    def f32(*shape):
+        return jax.ShapeDtypeStruct(shape, F32)
+
+    def vm(*shape):
+        return pltpu.VMEM(shape, BF)
+
+    def vf(*shape):
+        return pltpu.VMEM(shape, F32)
+
+    four = (slots, sh, part, hw)
+    return pl.pallas_call(
+        functools.partial(back_kernel, n),
+        in_specs=[pl.BlockSpec(memory_space=pltpu.SMEM)] + [ANY] * 19,
+        out_specs=[ANY] * 12,
+        out_shape=[
+            bf(2 * sh, part, width),
+            f32(rows // 2, width),
+            bf(rows // 2, width),
+            bf(rs, ff),
+            bf(ro, width),
+            bf(rs, width),
+            bf(rs, width),
+            bf(rs, width),
+            bf(rs, width),
+            f32(16, width),
+            bf(rows, ff),
+            f32(2, rows // 2, width),
         ],
-        out_specs=[out, out],
-        scratch_shapes=[pltpu.VMEM((ro, width), F32)],
+        scratch_shapes=[
+            vm(*four),
+            vm(*four),
+            vm(*four),
+            vm(*four),
+            vm(*four),
+            vf(2, *lse.shape[1:]),
+            vm(2, rows, width),
+            vm(2, 2, rows, 1024),
+            vm(2, rows, 2 * wq),
+            vm(2, rows, 2 * wq),
+            vm(2, rows, hw),
+            vm(3, width, hw),
+            vm(2, 2, A, rs, cq),
+            vm(2, 2, A, ro, wq),
+            vm(2, A, 2 * rs, wq),
+            vm(3, 2, A, rs, hw),
+            vm(2, A, rs, cq),
+            vm(2, A - 1, rs, cq),
+            vm(2, rs, cq),
+            vm(2, rs, cq),
+            vm(2, A, ro, wq),
+            vm(A, ro, wq),
+            vm(A - 1, ro, wq),
+            vm(ro, wq),
+            vm(A, 2 * rs, wq),
+            vm(A - 1, 2 * rs, wq),
+            vm(2 * rs, wq),
+            vm(2 * rs, wq),
+            vm(3, A, rs, hw),
+            vm(3, A - 1, rs, hw),
+            vm(3, rs, hw),
+            vm(3, rs, hw),
+            vf(hops + 1, 16, width),
+            vf(hops, 16, width),
+            vf(rows // 2, width),
+            vf(rows // 2, width),
+            vm(rows // 2, width),
+            pltpu.SemaphoreType.DMA((48,)),
+            pltpu.SemaphoreType.DMA((64 + 8 * n,)),
+            pltpu.SemaphoreType.DMA((64 + 8 * n,)),
+        ],
+        compiler_params=pltpu.CompilerParams(
+            vmem_limit_bytes=BACK_LIMIT, collective_id=1, has_side_effects=True
+        ),
+        name="back",
+    )(
+        lens,
+        act,
+        dout,
+        nrm,
+        dinn,
+        dattn,
+        ctx,
+        ctx.reshape(slots * sh * part, hw),
+        cr,
+        xall,
+        q,
+        k,
+        v,
+        lse,
+        dco,
+        dcs,
+        dfirst,
+        w,
+        lo,
+        acc,
     )
-    shape = jax.ShapeDtypeStruct((2, 2, n // 2, ro // 4, width), BF)
-    return pl.pallas_call(
-        outer_grad_kernel,
-        grid_spec=grid_spec,
-        out_shape=[shape, shape],
-        compiler_params=params(),
-        cost_estimate=cost(2 * rows * ff * width, 2 * (rows * ff + rows * width + ff * width)),
-        name="outer_grad",
-    )(ids, act, dout)
-
-
-def inner_grad_kernel(n, ids, nrm, dinn, keep, send, tmp):
-    rs = nrm.shape[1] // n
-    tmp[...] = dot_tn(nrm[...], dinn[...])
-
-    def put(ref):
-        for i in range(n):
-            ref[0, i % 2, i // 2] = tmp[at(ids[1] ^ i, rs), :].astype(BF)
-
-    @pl.when(pl.program_id(0) == 0)
-    def _():
-        put(send)
-
-    @pl.when(pl.program_id(0) == 1)
-    def _():
-        put(keep)
-
-
-def inner_grad_call(ids, nrm, dinn, n):
-    rows, width = nrm.shape
-    ff = dinn.shape[1]
-    cq, rs = ff // 4, width // n
-    block = (1, 2, n // 2, rs, cq)
-    grid_spec = pltpu.PrefetchScalarGridSpec(
-        num_scalar_prefetch=1,
-        grid=(2, 2),
-        in_specs=[
-            pl.BlockSpec((rows, width), lambda a, ex, s: (0, 0)),
-            pl.BlockSpec((rows, cq), lambda a, ex, s: (0, s[0] ^ (2 * ex + 1 - a))),
-        ],
-        out_specs=[
-            pl.BlockSpec(block, lambda a, ex, s: (jnp.where(a == 1, ex, 0), 0, 0, 0, 0)),
-            pl.BlockSpec(block, lambda a, ex, s: (jnp.where(a == 0, ex, 1), 0, 0, 0, 0)),
-        ],
-        scratch_shapes=[pltpu.VMEM((width, cq), F32)],
-    )
-    shape = jax.ShapeDtypeStruct((2, 2, n // 2, rs, cq), BF)
-    return pl.pallas_call(
-        functools.partial(inner_grad_kernel, n),
-        grid_spec=grid_spec,
-        out_shape=[shape, shape],
-        compiler_params=params(),
-        cost_estimate=cost(2 * rows * ff * width, 2 * (rows * ff + rows * width + ff * width)),
-        name="inner_grad",
-    )(ids, nrm, dinn)
-
-
-def out_grad_kernel(n, ids, cm, cr, dattn, keep, send, tmp):
-    width = tmp.shape[0]
-    hw, rs = width // 2, width // n
-    size = rs // 4
-    g = dattn[...]
-    core = ids[0] % 2
-    tmp[at(core, hw), :] = dot_tn(cm[...], g)
-    tmp[at(1 - core, hw), :] = dot_tn(cr[...], g)
-    for ec, ref in ((0, keep), (1, send)):
-        for ex in range(2):
-            for i in range(n):
-                first = (ids[1] ^ i) * rs + (ids[0] ^ (2 * ex + ec)) * size
-                ref[ex, i % 2, i // 2] = tmp[pl.ds(pl.multiple_of(first, size), size), :].astype(BF)
-
-
-def out_grad_call(ids, ctx, cr, dattn, n):
-    rows, width = dattn.shape
-    shape = jax.ShapeDtypeStruct((2, 2, n // 2, width // n // 4, width), BF)
-    return pl.pallas_call(
-        functools.partial(out_grad_kernel, n),
-        grid_spec=pltpu.PrefetchScalarGridSpec(
-            num_scalar_prefetch=1,
-            grid=(1,),
-            in_specs=[
-                pl.BlockSpec((rows, width // 2), lambda i, s: (0, 0)),
-                pl.BlockSpec((rows, width // 2), lambda i, s: (0, 0)),
-                pl.BlockSpec((rows, width), lambda i, s: (0, 0)),
-            ],
-            out_specs=[pl.BlockSpec(shape.shape, lambda i, s: (0, 0, 0, 0, 0))] * 2,
-            scratch_shapes=[pltpu.VMEM((width, width), F32)],
-        ),
-        out_shape=[shape, shape],
-        compiler_params=params(),
-        cost_estimate=cost(2 * rows * width * width, 4 * rows * width + 2 * width * width),
-        name="out_grad",
-    )(ids, ctx, cr, dattn)
-
-
-def qkv_grad_kernel(n, ids, xm, xs, dm, ds, out, bias, tmp):
-    tmp[...] = dot_tn(xm[...], dm[0]) + dot_tn(xs[...], ds[0])
-    bias[...] = jnp.broadcast_to(
-        jnp.sum(dm[0].astype(F32), 0, keepdims=True) + jnp.sum(ds[0].astype(F32), 0, keepdims=True),
-        bias.shape,
-    )
-    rs = tmp.shape[0] // n
-    for i in range(n):
-        out[i % 2, i // 2] = tmp[at(ids[1] ^ i, rs), :].astype(BF)
-
-
-def qkv_grad_call(ids, xall, d, n):
-    rows, width = xall.shape[0] // 2, xall.shape[1]
-    cols = d.shape[2]
-    shape = (2, n // 2, width // n, cols)
-    grid_spec = pltpu.PrefetchScalarGridSpec(
-        num_scalar_prefetch=1,
-        grid=(1,),
-        in_specs=[
-            pl.BlockSpec((rows, width), lambda i, s: (0, 0)),
-            pl.BlockSpec((rows, width), lambda i, s: (1, 0)),
-            pl.BlockSpec((1, rows, cols), lambda i, s: (0, 0, 0)),
-            pl.BlockSpec((1, rows, cols), lambda i, s: (1, 0, 0)),
-        ],
-        out_specs=[
-            pl.BlockSpec(shape, lambda i, s: (0, 0, 0, 0)),
-            pl.BlockSpec((8, cols), lambda i, s: (0, 0)),
-        ],
-        scratch_shapes=[pltpu.VMEM((width, cols), F32)],
-    )
-    return pl.pallas_call(
-        functools.partial(qkv_grad_kernel, n),
-        grid_spec=grid_spec,
-        out_shape=[jax.ShapeDtypeStruct(shape, BF), jax.ShapeDtypeStruct((8, cols), F32)],
-        compiler_params=params(),
-        cost_estimate=cost(4 * rows * width * cols, 4 * rows * width + 4 * rows * cols),
-        name="qkv_grad",
-    )(ids, xall, xall, d, d)
-
-
-def back_project_kernel(dq, dk, dv, w, out):
-    out[...] = dot_nt(dq[0], w[0]) + dot_nt(dk[0], w[1]) + dot_nt(dv[0], w[2])
-
-
-def back_project_call(which, dq, dk, dv, w):
-    _, rows, cols = dq.shape
-    width = w.shape[1]
-    block = rows // 3
-    one = pl.BlockSpec((1, block, cols), lambda i: (which, i, 0))
-    return pl.pallas_call(
-        back_project_kernel,
-        grid=(3,),
-        in_specs=[one, one, one, pl.BlockSpec((3, width, cols), lambda i: (0, 0, 0))],
-        out_specs=pl.BlockSpec((block, width), lambda i: (i, 0)),
-        out_shape=jax.ShapeDtypeStruct((rows, width), F32),
-        compiler_params=params(),
-        cost_estimate=cost(6 * rows * width * cols, 6 * rows * cols + 4 * rows * width + 6 * width * cols),
-        name="back_project",
-    )(dq, dk, dv, w)
 
 
 def per_device(
@@ -880,7 +1370,7 @@
 ):
     C = lax.axis_index("ctx")
     f = lax.axis_index("fsdp")
-    nc, n = lax.axis_size("ctx"), lax.axis_size("fsdp")
+    n = lax.axis_size("fsdp")
     x, core = C // 2, C % 2
     ids = jnp.stack([C, f]).astype(jnp.int32)
     seqs, part, width = inputs.shape
@@ -889,27 +1379,9 @@
     rows = 2 * sh * part
     rs, ro = width // n, ff // n
     hw = width // 2
-    A = n // 2
-
-    def swap(a, dc, df):
-        pairs = [
-            (c * n + g, (c ^ dc) * n + (g ^ df)) for c in range(nc) for g in range(n)
-        ]
-        return lax.ppermute(a, ("ctx", "fsdp"), pairs)
 
     def pick(bit, a, b):
         return jnp.where(bit == 0, a, b), jnp.where(bit == 0, b, a)
-
-    def xor_order(items, index):
-        items = list(items)
-        step = 1
-        while step < len(items):
-            bit = (index // step) % 2
-            items = [
-                jnp.where(bit == 0, items[i], items[i ^ step]) for i in range(len(items))
-            ]
-            step *= 2
-        return items
 
     def row_of(v):
         return jnp.pad(v.reshape(1, -1), ((0, 0), (0, hw - v.shape[0])))
@@ -948,73 +1420,37 @@
         ids, lengths, sh, ctx, cr, xall, cot.reshape(rows, width), vecs, wo, wi, wu
     )
 
-    def give_back(a):
-        mine, theirs = a[0], swap(a[1], 2, 0)
-        return jnp.concatenate(pick(x, mine, theirs), 0)
-
-    layer_out = give_back(lo.reshape(2, sh, part, width))
-
-    g_r = swap(dcs, 1, 0)
-
-    def total(*items):
-        out = items[0].astype(F32)
-        for i in items[1:]:
-            out = out + i.astype(F32)
-        return out.astype(BF)
-
-    def reduce_quarter(keep, send):
-        got = swap(send, 1, 0)
-        away = total(keep[1], got[1])
-        near = total(keep[0], got[0])
-        got = swap(away, 2, 0)
-        away = total(near[1], got[1])
-        near = total(near[0], got[0])
-        got = swap(away, 0, 1)
-        away = [total(near[a], got[a]) for a in range(A)]
-        mine = total(away[0], *[swap(away[a], 0, 2 * a) for a in range(1, A)])
-        other = swap(mine, 2, 0)
-        quarters = [mine, swap(mine, 1, 0), other, swap(other, 1, 0)]
-        return [a.astype(F32) for a in xor_order(quarters, C)]
-
-    ku, su = outer_grad_call(ids, act, dout, n)
-    ki, si = inner_grad_call(ids, nrm, dinn, n)
-    ko, so = out_grad_call(ids, ctx, cr, dattn, n)
-    grad_outer = jnp.concatenate(reduce_quarter(ku, su), 0)
-    grad_inner = jnp.concatenate(reduce_quarter(ki, si), 1)
-    grad_out = jnp.concatenate(reduce_quarter(ko, so), 0)
-
-    dq, dk, dv = attend_back_call(
-        ids, lengths, q4, k4, v4, lse, c4, dco.reshape(two), g_r.reshape(two)
+    layer_out, ig_here, ig_near, g_i, g_u, g_o, g_q, g_k, g_v, sums, _, _ = back_call(
+        lengths,
+        n,
+        act,
+        dout,
+        nrm,
+        dinn,
+        dattn,
+        c4,
+        cr,
+        xall,
+        q4,
+        k4,
+        v4,
+        lse,
+        dco.reshape(two),
+        dcs.reshape(two),
+        dfirst,
+        w_qkv,
+        lo.reshape(2, sh, part, width),
+        acc,
     )
-    flat3 = (2, rows, hw)
-    dq, dk, dv = dq.reshape(flat3), dk.reshape(flat3), dv.reshape(flat3)
-
-    def reduce_half(g):
-        got = swap(g[1], 0, 1)
-        away = [total(g[0, a], got[a]) for a in range(A)]
-        mine = total(away[0], *[swap(away[a], 0, 2 * a) for a in range(1, A)])
-        mine = total(mine, swap(mine, 2, 0))
-        return jnp.concatenate(pick(core, mine, swap(mine, 1, 0)), 1).astype(F32)
-
-    gq, bq = qkv_grad_call(ids, xall, dq, n)
-    gk, _ = qkv_grad_call(ids, xall, dk, n)
-    gv, bv = qkv_grad_call(ids, xall, dv, n)
-    grad_query, grad_key, grad_value = reduce_half(gq), reduce_half(gk), reduce_half(gv)
-
-    halves = jnp.concatenate([bq[:1], bv[:1], jnp.zeros((14, hw), F32)], 0)
-    none = jnp.zeros_like(halves)
-    sums = acc + jnp.concatenate(pick(core, halves, none), 1)
-    for dc, df in [(1, 0), (2, 0)] + [(0, 1 << b) for b in range(n.bit_length() - 1)]:
-        sums = sums + swap(sums, dc, df)
     own = lax.dynamic_slice_in_dim(sums[:8], f * rs, rs, 1)
     own_inner = lax.dynamic_slice_in_dim(sums[8 : 8 + ff // width].reshape(ff), f * ro, ro, 0)
-
-    theirs = back_project_call(1, dq, dk, dv, w_qkv)
-    from_core = swap(theirs, 1, 0)
-    own_part = back_project_call(0, dq, dk, dv, w_qkv)
-    full = (dfirst + own_part + from_core).reshape(2, sh, part, width)
-    away = swap(full[1].astype(BF), 2, 0).astype(F32)
-    input_grad = jnp.concatenate(pick(x, full[0], away), 0)
+    third = (sh, part, width)
+    input_grad = jnp.concatenate(
+        pick(x, ig_here.reshape(third), ig_near.reshape(third).astype(F32)), 0
+    )
+    grad_query, grad_key, grad_value, grad_out, grad_inner, grad_outer = (
+        g.astype(F32) for g in (g_q, g_k, g_v, g_o, g_i, g_u)
+    )
 
     return (
         layer_out,

time: 583 us -> 418 us (0.72)
  waiting for transfers between devices: 162 us -> 0 us
  Pallas kernels: 302 us -> 393 us
  starting transfers between devices: 71.1 us -> 0 us
  other arithmetic: 27.8 us -> 11.1 us
    ppermute x54 -> x0, waiting for transfers between devices: 162 us -> none  [swap(): return lax.ppermute(a, ('ctx', 'fsdp'), pairs)]
    pallas_call x9 -> x1, Pallas kernels: 88.5 us -> 179 us  [back_call(): pl.pallas_call(functools.partial(back_kernel, n), in_specs=[pl.BlockSpec(...]
    ppermute x54 -> x0, starting transfers between devices: 71.1 us -> none  [swap(): return lax.ppermute(a, ('ctx', 'fsdp'), pairs)]
    convert_element_type x24 -> x6, other arithmetic: 16.4 us -> 6.46 us  [per_device(): g.astype(F32)]
  transfers between devices with their start and end apart: 54 -> 0, of which waited for: 15 -> 0; matrix products, arithmetic and copies ran while one was open for 5% -> 0% of each run, Pallas kernels for 15% -> 0%
where the time goes in v3:
time: 418 us; the launch traced here: 415 us
  Pallas kernels  393 us (94%)
  other arithmetic  11.1 us (3%)
  local copies, waits for them, and re-layouts  9.61 us (2%)
    pallas_call x1, Pallas kernels, back_call(): pl.pallas_call(functools.partial(back_kernel, n), in_specs=[pl.BlockSpec(...  179 us
    pallas_call x1, Pallas kernels, front_call(): pl.pallas_call(functools.partial(front_kernel, n), in_specs=[pl.BlockSpec...  160 us
    pallas_call x1, Pallas kernels, ffn_call(): pl.pallas_call(functools.partial(ffn_kernel, n, sh, rows // (2 * sh)), gr...  53.4 us

profile of v3, /device:TPU:1, one launch (start us, length us, event | category | flops | bytes accessed | tf_op | source)
XLA Modules:
  0.0 414.6 jit_solution(8369027409193888451)
XLA Ops:
  0.7 0.7 pad.25
  1.3 0.7 pad.26
  2.0 0.7 pad.27
  2.6 0.7 pad.28
  3.3 0.7 pad.29
  4.0 0.7 pad.30
  4.6 0.7 pad.31
  5.3 0.7 pad.32
  5.9 0.7 reshape.101
  6.6 1.3 concatenate.6.vecs
  7.9 160.1 %front.1 = (bf16[4,3,128,1024]{3,2,1,0:T(8,128)(2,1)}, bf16[2,3,128,1024]{3,2,1,0:T(8,128)(2,1)}, bf16[3,1024,512]{2,1,0:T(8,128)(2,1)}, bf16[1024,4096]{1,0:T(8...) custom-call(s32[6]{0:T(128)} %lens.5, ...), custom_call_target="tpu_custom_call" | custom-call | tf_op jit(solution)/shard_map/front/pallas_call | solution.py:346
  168.0 0.6 pad_add_fusion.ids
  168.6 53.4 %ffn.1 = (bf16[768,1024]{1,0:T(8,128)(2,1)}, bf16[768,4096]{1,0:T(8,128)(2,1)}, bf16[768,1024]{1,0:T(8,128)(2,1)}, bf16[768,4096]{1,0:T(8,128)(2,1)}, bf16[768,1...) custom-call(s32[2]{0:T(128)} %pad_add_fusion.ids, ...), custom_call_target="tpu_custom_call" | custom-call | flops 28991029248 | bytes 42467328 | tf_op jit(solution)/shard_map/ffn/pallas_call | solution.py:617
  222.0 179.1 %back.1 = (bf16[6,128,1024]{2,1,0:T(8,128)(2,1)}, f32[384,1024]{1,0:T(8,128)}, bf16[384,1024]{1,0:T(8,128)(2,1)}, bf16[128,4096]{1,0:T(8,128)(2,1)}, bf16[512,10...) custom-call(s32[6]{0:T(128)} %lens.5, ...), custom_call_target="tpu_custom_call" | custom-call | tf_op jit(solution)/shard_map/back/pallas_call | solution.py:1263
  401.1 2.1 convert_select_fusion.1
  403.2 0.0 copy-start.2
  403.2 2.0 pad_maximum_fusion
  405.2 0.0 copy-done.2
  405.2 0.0 copy-start.1
  405.2 1.5 convert_element_type.36
  406.8 0.0 copy-done.1
  406.8 0.0 copy-start.6
  406.8 0.0 copy-start.5
  406.8 1.6 convert_element_type.37
  408.3 0.0 copy-start.4
  408.4 0.0 copy-start.3
  408.4 0.0 copy-done.6
  408.4 0.0 copy-start.7
  408.4 0.0 copy-start
  408.4 0.8 convert_element_type.32
  409.2 0.0 copy-done.5
  409.2 0.8 convert_element_type.33
  410.1 0.0 copy-done.4
  410.1 0.8 convert_element_type.34
  410.9 0.0 copy-done.3
  410.9 0.8 convert_element_type.35
  411.7 0.0 copy-done.7
  411.8 0.5 slice_bitcast_fusion.1
  412.3 0.7 dynamic_slice.7
  413.0 0.0 copy-done
  413.0 1.1 copy.39
  (5 shorter events, 0.0 us)
Async XLA Ops:
  403.2 2.0 copy-start.2
  405.2 1.5 copy-start.1
  406.8 1.6 copy-start.6
  406.8 2.4 copy-start.5
  408.3 1.7 copy-start.4
  408.4 2.6 copy-start.3
  408.4 3.4 copy-start.7
  408.4 4.6 %copy-start = (bf16[6,128,1024]{2,1,0:T(8,128)(2,1)S(1)}, bf16[6,128,1024]{2,1,0:T(8,128)(2,1)}, u32[]{:S(2)}) copy-start(bf16[6,128,1024]{2,1,0:T(8,128)(2,1)} %get-tuple-element.110) | copy-start | bytes 4718596

commit v4 on v3

--- a/solution.py
+++ b/solution.py
@@ -90,6 +90,7 @@
     vo,
     cxo,
     cro,
+    cso,
     lseo,
     X,
     W,
@@ -161,48 +162,67 @@
             seen.add(sem)
             remote(target, target, sem, dev).wait_recv()
 
-    base_x = 12 * n + 4 * n
-    X1, X2, X3, COT, CTX = (base_x + i for i in range(5))
+    X1, X2, X3, COT, CTX, CTX2 = range(6)
     send(xin.at[pl.ds((1 - x) * sh, sh)], X.at[1], X1, (2, 0))
 
-    def qkv_slot(i):
-        s = flip(f, i)
-        return [W.at[j, at(s, rs)] for j in range(3)] + [VEC.at[s]]
-
-    def qkv_sem(i):
-        return [12 * n + 4 * i + j for j in range(4)]
-
-    own_qkv = [w.at[:, at(core, hw)] for w in (wq, wk, wv)] + [vecs]
-
-    def qkv_give(tag, source_piece, source, dev):
-        place = qkv_slot(source_piece)
-        for j in range(4):
-            send(source[j], place[j], qkv_sem(tag)[j], dev)
-
-    def qkv_need(i):
-        dev = (0, i) if i % 2 == 0 else (0, 1)
-        place = qkv_slot(i)
-        for j in range(4):
-            arrive(place[j], qkv_sem(i)[j], dev)
-
-    for k in range(1, A):
-        qkv_give(2 * k, 0, own_qkv, (0, 2 * k))
-    qkv_give(1, 0, own_qkv, (0, 1))
-    x_here.wait()
-    send(X.at[0], X.at[2], X2, (1, 0))
-
-    def rest_slot(e, i):
-        qq, s = flip(C, e), flip(f, i)
-        return [
-            woo.at[pl.ds(pl.multiple_of(s * rs + qq * (rs // 4), rs // 4), rs // 4)],
-            wio.at[at(s, rs), at(qq, cq)],
-            wuo.at[pl.ds(pl.multiple_of(s * ro + qq * (ro // 4), ro // 4), ro // 4)],
-        ]
-
-    def rest_sem(e, i):
-        return [(e * n + i) * 3 + kind for kind in range(3)]
-
-    def route(e, i):
+    def rows_at(ref, first, size):
+        return ref.at[pl.ds(pl.multiple_of(first, size), size)]
+
+    hr, hu = rs // 2, ro // 2
+
+    def projection(j):
+        w = (wq, wk, wv)[j]
+        return (
+            1,
+            lambda e, s: [W.at[j, at(s, rs)]] + [VEC.at[s]] * (j == 0),
+            lambda: [w.at[:, at(core, hw)]] + [vecs] * (j == 0),
+        )
+
+    def inner_part(h):
+        return (
+            4,
+            lambda e, s: [wio.at[at(s * 2 + h, hr), at(flip(C, e), cq)]],
+            lambda: [wi_in.at[pl.ds(h * hr, hr), at(C, cq)]],
+        )
+
+    outer_a = (
+        4,
+        lambda e, s: [rows_at(wuo, s * ro + flip(C, e) * (hu // 4), hu // 4)],
+        lambda: [rows_at(wu_in, C * (hu // 4), hu // 4)],
+    )
+    out_part = (
+        4,
+        lambda e, s: [rows_at(woo, s * rs + flip(C, e) * (rs // 4), rs // 4)],
+        lambda: [rows_at(wo_in, C * (rs // 4), rs // 4)],
+    )
+
+    def outer_b(h):
+        return (
+            2,
+            lambda e, s: [rows_at(wuo, s * ro + hu + (flip(core, e) * 2 + h) * (hu // 4), hu // 4)],
+            lambda: [rows_at(wu_in, hu + (core * 2 + h) * (hu // 4), hu // 4)],
+        )
+
+    kinds = [
+        inner_part(0),
+        projection(0),
+        projection(1),
+        projection(2),
+        inner_part(1),
+        outer_a,
+        out_part,
+        outer_b(0),
+        outer_b(1),
+    ]
+    sems, ready = {}, 6
+    for k, (parts, place, _) in enumerate(kinds):
+        for e in range(parts):
+            for i in range(1, n):
+                for u in range(2 if k == 1 else 1):
+                    sems[k, e, i, u] = ready
+                    ready += 1
+
+    def route(parts, e, i):
         if e % 2:
             return (1, 0), (e - 1, i)
         if e:
@@ -211,91 +231,134 @@
             return (0, 1), (0, i - 1)
         return (0, i), (0, 0)
 
-    def rest_copies(e, i):
-        dev, (pe, pi) = route(e, i)
-        place = rest_slot(pe, pi)
-        source = [wo_in.at[at(C, rs // 4)], wi_in.at[:, at(C, cq)], wu_in.at[at(C, ro // 4)]]
-        source = source if pi == 0 else place
-        sems = rest_sem(e, i)
-        return [remote(source[kind], place[kind], sems[kind], dev) for kind in range(3)]
-
-    def rest_send(e, i):
-        for c in rest_copies(e, i):
+    def copies(k, e, i):
+        parts, place, own = kinds[k]
+        dev, (pe, pi) = route(parts, e, i)
+        target = place(pe, flip(f, pi))
+        source = target if pi else own()
+        return [
+            remote(source[u], target[u], sems[k, e, i, u], dev) for u in range(len(target))
+        ]
+
+    issued = []
+
+    def give(k, e, i):
+        for c in copies(k, e, i):
             c.start()
-
-    def rest_need(e, i):
-        dev, _ = route(e, i)
-        place = rest_slot(e, i)
-        for kind in range(3):
-            arrive(place[kind], rest_sem(e, i)[kind], dev)
-
-    def rest_hand_on(e, i):
-        rest_need(e, i)
-        if e == 0 and i % 2 == 0:
-            rest_send(0, i + 1)
-        if e == 0:
-            rest_send(2, i)
-        if e % 2 == 0:
-            rest_send(e + 1, i)
-
-    for k in range(1, A):
-        qkv_need(2 * k)
-        qkv_give(2 * k + 1, 2 * k, qkv_slot(2 * k), (0, 1))
-    for k in range(1, A):
-        rest_send(0, 2 * k)
-    arrive(X.at[1], X1, (2, 0))
-    send(X.at[1], X.at[3], X3, (1, 0))
-    send(cin.at[pl.ds((1 - x) * sh, sh)], co.at[1], COT, (2, 0))
-    rest_send(0, 1)
+        issued.append((k, e, i))
+
+    got = set()
+
+    def take(k, e, i):
+        if (k, e, i) in got:
+            return
+        got.add((k, e, i))
+        parts, place, _ = kinds[k]
+        dev, _ = route(parts, e, i)
+        for u, target in enumerate(place(e, flip(f, i))):
+            remote(target, target, sems[k, e, i, u], dev).wait_recv()
+
+    def hand_on(k, i):
+        parts = kinds[k][0]
+        if parts == 4:
+            give(k, 2, i)
+        if parts > 1:
+            give(k, 1, i)
+
+    def base(k):
+        if k < len(kinds):
+            for a in range(1, A):
+                give(k, 0, 2 * a)
+            give(k, 0, 1)
+
+    def z_in(k):
+        for a in range(1, A):
+            take(k, 0, 2 * a)
+            give(k, 0, 2 * a + 1)
+            hand_on(k, 2 * a)
+
+    def y_in(k):
+        for i in range(1, n, 2):
+            take(k, 0, i)
+            hand_on(k, i)
+
+    def x_in(k):
+        if kinds[k][0] == 4:
+            for i in range(1, n):
+                take(k, 2, i)
+                give(k, 3, i)
+
+    base(0)
+    base(1)
+    x_here.wait()
+    send(X.at[0], X.at[2], X2, (1, 0))
     keep(cin.at[pl.ds(x * sh, sh)], co.at[0])
     keep(wo_in, woo.at[at(f, rs)])
     keep(wi_in, wio.at[at(f, rs)])
     keep(wu_in, wuo.at[at(f, ro)])
     for c in w_here:
         c.wait()
-    for i in range(1, n):
-        qkv_need(i)
+    send(cin.at[pl.ds((1 - x) * sh, sh)], co.at[1], COT, (2, 0))
+
+    slots = X.shape[0]
+    pairs = hw // (2 * HD)
+
+    z_in(0)
+    base(2)
+    arrive(X.at[1], X1, (2, 0))
+    send(X.at[1], X.at[3], X3, (1, 0))
+    z_in(1)
+    base(3)
+    y_in(0)
     arrive(X.at[2], X2, (1, 0))
     arrive(X.at[3], X3, (1, 0))
     keep(X, xo)
-    keep(W, wqkvo)
+    z_in(2)
+    base(4)
+    y_in(1)
     keep(VEC, veco)
-
-    jobs = [(0, 1)] + [(0, i) for i in range(2, n, 2)] + [(2, 1)]
-    jobs += [(0, i) for i in range(3, n, 2)] + [(2, i) for i in range(2, n)]
-    slots = X.shape[0]
-    pairs = hw // (2 * HD)
-    steps = slots + sh * pairs
-    plan = [jobs[len(jobs) * t // steps : len(jobs) * (t + 1) // steps] for t in range(steps)]
-
-    def serve(step, base, count):
-        for t in range(count):
-            if plan[base + t]:
-
-                @pl.when(step == t)
-                def _():
-                    for job in plan[base + t]:
-                        rest_hand_on(*job)
 
     def bias(row):
         read = lambda s: VEC[pl.ds(core * (n // 2) + s, 1), row : row + 1, :128].reshape(1, 128).astype(F32)
         return spread(read, n // 2, rs)
 
-    bias_q, bias_v = bias(0), bias(1)
-
-    def project(slot, carry):
-        a = X[slot].reshape(sh * part, width)
-        shape = (sh, part, hw)
-        Q[slot] = (dot(a, W[0]) + bias_q).astype(BF).reshape(shape)
-        K[slot] = dot(a, W[1]).astype(BF).reshape(shape)
-        V[slot] = (dot(a, W[2]) + bias_v).astype(BF).reshape(shape)
-        serve(slot, 0, slots)
-        return carry
-
-    lax.fori_loop(0, slots, project, 0)
+    shape = (sh, part, hw)
+
+    def project(j, target, add):
+        def body(slot, carry):
+            value = dot(X[slot].reshape(sh * part, width), W[j])
+            if add is not None:
+                value = value + add
+            target[slot] = value.astype(BF).reshape(shape)
+            return carry
+
+        lax.fori_loop(0, slots, body, 0)
+
+    project(0, Q, bias(0))
+    z_in(3)
+    base(5)
+    y_in(2)
+    project(1, K, None)
+    x_in(0)
+    z_in(4)
+    base(6)
+    y_in(3)
+    keep(W, wqkvo)
+    project(2, V, bias(1))
     keep(Q, qo)
     keep(K, ko)
     keep(V, vo)
+
+    jobs = [
+        lambda: z_in(5),
+        lambda: base(7),
+        lambda: y_in(4),
+        lambda: z_in(6),
+        lambda: base(8),
+        lambda: y_in(5),
+        lambda: x_in(4),
+    ]
+    steps = sh * pairs
 
     def attend(step, carry):
         s, pair = step // pairs, step % pairs
@@ -309,20 +372,39 @@
         o, lse = attend_pair(q, k, v, mask)
         CX[:, s, :, cols] = o.reshape(slots, part, 2 * HD)
         LSE[s, :, cols] = lse
-        serve(step, slots, sh * pairs)
+        for t in range(steps):
+            now = jobs[len(jobs) * t // steps : len(jobs) * (t + 1) // steps]
+            if now:
+
+                @pl.when(step == t)
+                def _():
+                    for job in now:
+                        job()
+
         return carry
 
-    lax.fori_loop(0, sh * pairs, attend, 0)
+    lax.fori_loop(0, steps, attend, 0)
     send(CX.at[pl.ds(2, 2)], cro, CTX, (1, 0))
+    send(CX.at[pl.ds(0, 2)], cso, CTX2, (1, 0))
     keep(CX, cxo)
     keep(LSE, lseo)
-    for e in range(4):
-        for i in range(1, n):
-            rest_need(e, i)
-            for c in rest_copies(e, i):
-                c.wait_send()
+    z_in(7)
+    y_in(6)
+    x_in(5)
+    z_in(8)
+    y_in(7)
+    x_in(6)
+    y_in(8)
+    for k, (parts, _, _) in enumerate(kinds):
+        for e in range(parts):
+            for i in range(1, n):
+                take(k, e, i)
     arrive(co.at[1], COT, (2, 0))
     arrive(cro, CTX, (1, 0))
+    arrive(cso, CTX2, (1, 0))
+    for what in issued:
+        for c in copies(*what):
+            c.wait_send()
     for c in sent:
         c.wait_send()
     for c in local:
@@ -342,11 +424,11 @@
     full = 4 * part
     lse = (sh, full, hw)
     four = (4, sh, part, hw)
-    sems = 16 * n + 5
+    sems = 24 * n
     return pl.pallas_call(
         functools.partial(front_kernel, n),
         in_specs=[pl.BlockSpec(memory_space=pltpu.SMEM)] + [ANY] * 9,
-        out_specs=[ANY] * 13,
+        out_specs=[ANY] * 14,
         out_shape=[
             bf(4, sh, part, width),
             bf(2, sh, part, width),
@@ -354,18 +436,19 @@
             bf(width, ff),
             bf(ff, width),
             bf(width, width),
-            bf(n, PACK, hw),
+            bf(n, PACK, 128),
             bf(*four),
             bf(*four),
             bf(*four),
             bf(*four),
+            bf(2, sh, part, hw),
             bf(2, sh, part, hw),
             jax.ShapeDtypeStruct(lse, F32),
         ],
         scratch_shapes=[
             vm(4, sh, part, width),
             vm(3, width, hw),
-            vm(n, PACK, hw),
+            vm(n, PACK, 128),
             vm(*four),
             vm(*four),
             vm(*four),
@@ -488,12 +571,15 @@
     )
 
 
-def ffn_kernel(n, sh, part, ids, lens, cm, cr, xm, cot, vecs, wo_in, wi_in, wu_in, *refs):
-    lo, act, dout, dinn, nrm, dattn, dfirst, dco, dcs, acc = refs[:10]
-    wo, wi, wu, gp, vec, ib, sem = refs[10:]
+def ffn_kernel(n, sh, part, lens, cm, cr, xm, cot, vecs, wo_in, wi_in, wu_in, *refs):
+    dfirst, dco, acc = refs[:3]
+    homes, (o_lo, act_s, dout_s, dinn_s, nrm_s, dattn_s, dcs_s) = refs[3:8], refs[8:15]
+    wo, wi, wu, gp, vec, ib, *twice, sem, csem, hsem, ssem, rsem = refs[15:]
     width, ff = wi.shape
-    core = ids[0] % 2
+    C, f = lax.axis_index("ctx"), lax.axis_index("fsdp")
+    x, core = C // 2, C % 2
     step = pl.program_id(0)
+    turn = 2 - step
     rs, ro = width // n, ff // n
     cq, hw = ff // 4, width // 2
 
@@ -502,14 +588,110 @@
     def copy(kind):
         return pltpu.make_async_copy(*pairs[kind], sem.at[kind])
 
+    CORE, NEAR = flip(C, 1), flip(C, 2)
+    block, wq = xm.shape[0], width // 4
+
+    def remote(t, j, to, source, target):
+        return pltpu.make_async_remote_copy(
+            src_ref=source,
+            dst_ref=target,
+            send_sem=ssem.at[t, j],
+            recv_sem=rsem.at[t, j],
+            device_id=(to, f),
+            device_id_type=MESH,
+        )
+
+    KINDS = ("act", "nrm", "dout0", "dout1", "dinn0", "dinn1", "dattn0", "dattn1", "dcs")
+
+    def rows_of(t):
+        return pl.ds(pl.multiple_of(t * block, block), block)
+
+    def held(t):
+        return [ref.at[(2 - t) % 2] for ref in twice]
+
+    act, nrm, dout, dinn, dattn, dcs, lo = held(turn)
+    HOME = {"act": 0, "nrm": 1, "dout": 2, "dinn": 3, "dattn": 4}
+
+    def home(t, name):
+        j = HOME[name]
+        return pltpu.make_async_copy(held(t)[j], homes[j].at[rows_of(t)], hsem.at[t, j])
+
+    def to_core(t, *names):
+        out = []
+        for name in names or KINDS:
+            rows = rows_of(t)
+            act, nrm, dout, dinn, dattn, dcs, _ = held(t)
+            ex = int(name[-1]) if name[-1] in "01" else 0
+            other, lanes = flip(C, 2 * ex + 1), pl.ds(ex * wq, wq)
+            source, target = {
+                "act": lambda: (act, act_s.at[rows]),
+                "nrm": lambda: (nrm, nrm_s.at[rows]),
+                "dcs": lambda: (dcs, dcs_s.at[rows]),
+                "dou": lambda: (dout.at[:, at(other, wq)], dout_s.at[rows, lanes]),
+                "dat": lambda: (dattn.at[:, at(other, wq)], dattn_s.at[rows, lanes]),
+                "din": lambda: (dinn.at[:, at(other, cq)], dinn_s.at[ex, rows]),
+            }[name[:3]]()
+            out.append(remote(t, KINDS.index(name), CORE, source, target))
+        return out
+
+    def start(name):
+        for c in to_core(turn, *(k for k in KINDS if k.startswith(name))):
+            c.start()
+        if name in HOME:
+            home(turn, name).start()
+
+    def end(t, name):
+        for c in to_core(t, *(k for k in KINDS if k.startswith(name))):
+            c.wait_send()
+        if name in HOME:
+            home(t, name).wait()
+
+    def free(name):
+        @pl.when(step == 2)
+        def _():
+            end(2, name)
+
+    def slots_of(t, ex):
+        count = block // part
+        return [u for u in range(count) if (t * count + u) // sh == ex]
+
+    def place(t, u):
+        return held(t)[6].at[pl.ds(u * part, part)], o_lo.at[x * sh + (t * (block // part) + u) % sh]
+
+    def to_near(t):
+        return [remote(t, 9 + u, NEAR, *place(t, u)) for u in slots_of(t, 1)]
+
+    def stay(t):
+        return [pltpu.make_async_copy(*place(t, u), csem.at[t, u]) for u in slots_of(t, 0)]
+
+    def send(t):
+        for c in to_near(t) + stay(t):
+            c.start()
+
+    def sent(t):
+        for c in to_near(t):
+            c.wait_send()
+        for c in stay(t):
+            c.wait()
+
+    def received(t):
+        for c in to_core(t) + to_near(t):
+            c.wait_recv()
+
     @pl.when(step == 0)
     def _():
+        barrier = pltpu.get_barrier_semaphore()
+        for to in (CORE, NEAR):
+            pl.semaphore_signal(barrier, inc=1, device_id=(to, f), device_id_type=MESH)
+        pl.semaphore_wait(barrier, 2)
         for kind in range(3):
             copy(kind).start()
         acc[...] = jnp.zeros_like(acc)
         vec[...] = spread(lambda s: vecs[s, :8, :128].astype(F32), n, rs)
         for s in range(n):
-            ib[:, s * ro : (s + 1) * ro] = vecs[s, 8:9, :ro].astype(F32)
+            for t in range(ro // 128):
+                first = s * ro + t * 128
+                ib[:, first : first + 128] = vecs[s, 8 + t : 9 + t, :].astype(F32)
 
     def arrived(kind):
         @pl.when(step == 0)
@@ -519,11 +701,11 @@
     count = xm.shape[0] // part
     inside = []
     for u in range(count):
-        slot = step * count + u
+        slot = turn * count + u
         ex, s = slot // sh, slot % sh
-        first = (ids[0] ^ (2 * ex)) * part
+        first = (C + ex * (2 - 4 * x)) * part
         row = lax.broadcasted_iota(jnp.int32, (part, 1), 0) + first
-        inside.append(jnp.where(row < lens[(ids[0] // 2) * sh + s], 1.0, 0.0))
+        inside.append(jnp.where(row < lens[x * sh + s], 1.0, 0.0))
     valid = jnp.concatenate(inside, 0)
     own, other = at(core, hw), at(1 - core, hw)
 
@@ -537,69 +719,88 @@
     hat1, r1 = normalise(first)
     normed = hat1 * vec[4:5, :] + vec[5:6, :]
     low = normed.astype(BF)
+    free("act")
+    free("nrm")
     nrm[...] = low
+    start("nrm")
     arrived(1)
     for j in range(4):
         cols = slice(j * cq, (j + 1) * cq)
         g, d = gelu_pair(dot(low, wi[:, cols]) + ib[:, cols])
         act[:, cols] = g.astype(BF)
         gp[:, cols] = d
+    start("act")
     arrived(2)
     second = normed + (dot(act[...], wu[...]) + vec[3:4, :])
     hat2, r2 = normalise(second)
+    @pl.when(step == 2)
+    def _():
+        sent(2)
+
     lo[...] = (hat2 * vec[6:7, :] + vec[7:8, :]).astype(BF)
     og = cot[...].astype(F32) * valid
     add(6, og * hat2)
     add(7, og)
     d2 = normalise_back(og * vec[6:7, :], hat2, r2)
     d2low = d2.astype(BF)
+    free("dout")
     dout[...] = d2low
+    start("dout")
+    for t in range(3):
+
+        @pl.when(turn == t)
+        def _():
+            send(t)
+
     add(3, d2low.astype(F32))
+    free("dinn")
     for j in range(4):
         cols = slice(j * cq, (j + 1) * cq)
         di = (dot_nt(d2low, wu[cols, :]) * gp[:, cols]).astype(BF)
         dinn[:, cols] = di
         add(8 + j, di.astype(F32))
+    start("dinn")
     dn = d2 + dot_nt(dinn[...], wi[...])
     add(4, dn * hat1)
     add(5, dn)
     d1 = normalise_back(dn * vec[4:5, :], hat1, r1)
     dfirst[...] = d1
     d1low = d1.astype(BF)
+    free("dattn")
+    free("dcs")
     dattn[...] = d1low
+    start("dattn")
     add(2, d1low.astype(F32))
+    dcs[...] = dot_nt(d1low, wo[other]).astype(BF)
+    start("dcs")
     dco[...] = dot_nt(d1low, wo[own]).astype(BF)
-    dcs[...] = dot_nt(d1low, wo[other]).astype(BF)
-
-
-def ffn_call(ids, lens, sh, c, cr, xall, cot, vecs, wo, wi, wu):
+
+    @pl.when(turn == 0)
+    def _():
+        for t in range(2):
+            for name in ("act", "nrm", "dout", "dinn", "dattn", "dcs"):
+                end(t, name)
+            sent(t)
+        for t in range(3):
+            received(t)
+
+
+def ffn_call(lens, sh, c, cr, xall, cot, vecs, wo, wi, wu):
     width, ff = wi.shape
     n, rows = vecs.shape[0], cot.shape[0]
-    block = rows // 3
+    block, part = rows // 3, rows // (2 * sh)
     hw = width // 2
 
     def by(cols):
-        return pl.BlockSpec((block, cols), lambda i, *_: (i, 0))
+        return pl.BlockSpec((block, cols), lambda i: (2 - i, 0))
 
     def whole(*shape):
-        return pl.BlockSpec(shape, lambda i, *_: (0,) * len(shape))
-
-    grid_spec = pltpu.PrefetchScalarGridSpec(
-        num_scalar_prefetch=2,
+        return pl.BlockSpec(shape, lambda i: (0,) * len(shape))
+
+    grid_spec = pl.GridSpec(
         grid=(3,),
-        in_specs=[by(hw), by(hw), by(width), by(width), whole(*vecs.shape), ANY, ANY, ANY],
-        out_specs=[
-            by(width),
-            by(ff),
-            by(width),
-            by(ff),
-            by(width),
-            by(width),
-            by(width),
-            by(hw),
-            by(hw),
-            whole(16, width),
-        ],
+        in_specs=[pl.BlockSpec(memory_space=pltpu.SMEM), by(hw), by(hw), by(width), by(width), whole(*vecs.shape), ANY, ANY, ANY],
+        out_specs=[by(width), by(hw), whole(16, width)] + [ANY] * 12,
         scratch_shapes=[
             pltpu.VMEM((width, width), BF),
             pltpu.VMEM((width, ff), BF),
@@ -607,7 +808,15 @@
             pltpu.VMEM((block, ff), F32),
             pltpu.VMEM((8, width), F32),
             pltpu.VMEM((1, ff), F32),
+            *(
+                pltpu.VMEM((2, block, cols), BF)
+                for cols in (ff, width, width, ff, width, hw, width)
+            ),
             pltpu.SemaphoreType.DMA((3,)),
+            pltpu.SemaphoreType.DMA((3, block // part)),
+            pltpu.SemaphoreType.DMA((3, 5)),
+            pltpu.SemaphoreType.DMA((3, 9 + block // part)),
+            pltpu.SemaphoreType.DMA((3, 9 + block // part)),
         ],
     )
 
@@ -615,26 +824,31 @@
         return jax.ShapeDtypeStruct((rows, cols), dtype)
 
     return pl.pallas_call(
-        functools.partial(ffn_kernel, n, sh, rows // (2 * sh)),
+        functools.partial(ffn_kernel, n, sh, part),
         grid_spec=grid_spec,
         out_shape=[
+            shape(width, F32),
+            shape(hw),
+            jax.ShapeDtypeStruct((16, width), F32),
+            shape(ff),
+            shape(width),
             shape(width),
             shape(ff),
             shape(width),
+            jax.ShapeDtypeStruct((2 * sh, part, width), BF),
             shape(ff),
+            shape(hw),
+            jax.ShapeDtypeStruct((2, rows, ff // 4), BF),
             shape(width),
-            shape(width),
-            shape(width, F32),
             shape(hw),
             shape(hw),
-            jax.ShapeDtypeStruct((16, width), F32),
         ],
-        compiler_params=params(),
+        compiler_params=params(collective_id=2, has_side_effects=True),
         cost_estimate=cost(
             2 * rows * width * (2 * width + 4 * ff), 30 * rows * width + 2 * width * (2 * ff + width)
         ),
         name="ffn",
-    )(ids, lens, c, cr, xall, cot, vecs, wo, wi, wu)
+    )(lens, c, cr, xall, cot, vecs, wo, wi, wu)
 
 
 def xor(a, b, count):
@@ -685,7 +899,6 @@
     dinn,
     dattn,
     ctx,
-    ctx2,
     cr,
     xall,
     q_in,
@@ -693,12 +906,16 @@
     v_in,
     lse_in,
     dco,
-    dcs,
     dfirst,
     w_in,
-    lo,
     acc,
-    o_lo,
+    act_s,
+    dout_s,
+    dinn_s,
+    nrm_s,
+    dattn_s,
+    dcs_s,
+    cs,
     o_igl,
     o_igr,
     o_i,
@@ -708,7 +925,6 @@
     o_k,
     o_v,
     o_vec,
-    act_s,
     ig_s,
     Q,
     K,
@@ -812,76 +1028,41 @@
         for name in names:
             loads.pop(name)().wait()
 
+    def quarters(ref, size, ex):
+        return ref.at[:, at(flip(C, 2 * ex), size)]
+
+    load("nrm", lambda: (nrm, L.at[0]))
+    load("nrm_s", lambda: (nrm_s, L.at[1]))
+    for ex in range(2):
+        load(("dinn", ex), lambda ex=ex: (quarters(dinn, cq, ex), D.at[ex, 0]))
+        load(("dinn_s", ex), lambda ex=ex: (dinn_s.at[ex], D.at[ex, 1]))
+    for ex in range(2):
+        lanes = pl.ds(ex * wq, wq)
+        load(("dout", ex), lambda ex=ex, lanes=lanes: (quarters(dout, wq, ex), DO.at[0, :, lanes]))
+        load(
+            ("dattn", ex), lambda ex=ex, lanes=lanes: (quarters(dattn, wq, ex), DA.at[0, :, lanes])
+        )
+    load("dout_s", lambda: (dout_s, DO.at[1]))
+    load("dattn_s", lambda: (dattn_s, DA.at[1]))
+    load("co", lambda: (cr, CO.at[0]))
+    load("co_s", lambda: (cs, CO.at[1]))
+    load("c", lambda: (ctx, CX))
     load("q", lambda: (q_in, Q))
     load("k", lambda: (k_in, K))
     load("v", lambda: (v_in, V))
-    load("c", lambda: (ctx, CX))
     load("g", lambda: (dco, G.at[pl.ds(0, 2)]))
+    load("g_s", lambda: (dcs_s, G.at[pl.ds(2, 2)]))
     for s in range(2):
         load(("lse", s), lambda s=s: (lse_in.at[s], LSE.at[s]))
-    load("nrm", lambda: (nrm, L.at[0]))
     load("vec", lambda: (acc, VS.at[0]))
-
-    def quarters(ref, size, ex, ec):
-        return ref.at[:, at(flip(C, 2 * ex + ec), size)]
-
-    for ex in range(2):
-        load(("dinn", ex), lambda ex=ex: (quarters(dinn, cq, ex, 0), D.at[ex, 0]))
-
+    load("w", lambda: (w_in, W))
     pl.semaphore_wait(barrier, len(partners))
-
-    g_swap = remote(CORE, lambda: (dcs, G.at[pl.ds(2, 2)]))
-    go(g_swap)
-    lo_swap = remote(NEAR, lambda: (lo.at[1], o_lo.at[pl.ds(x * sh, sh)]))
-    go(lo_swap)
-    go_local(lambda: (lo.at[0], o_lo.at[pl.ds(x * sh, sh)]))
-    nrm_swap = remote(CORE, lambda: (nrm, L.at[1]))
-    go(nrm_swap)
-    dinn_swap = [
-        remote(CORE, lambda ex=ex: (quarters(dinn, cq, ex, 1), D.at[ex, 1])) for ex in range(2)
-    ]
-    go(dinn_swap[0])
-    go(dinn_swap[1])
-
-    for ex in range(2):
-        load(
-            ("dout", ex),
-            lambda ex=ex: (quarters(dout, wq, ex, 0), DO.at[0, :, pl.ds(ex * wq, wq)]),
-        )
-        load(
-            ("dattn", ex),
-            lambda ex=ex: (quarters(dattn, wq, ex, 0), DA.at[0, :, pl.ds(ex * wq, wq)]),
-        )
-    load("co", lambda: (cr, CO.at[0]))
-    load("w", lambda: (w_in, W))
 
     chunks = ff // 1024
     per = 1024 // ro
 
     def act_cols(t):
         return at(xor(f // per, t, chunks), 1024)
-
-    dout_swap = [
-        remote(
-            CORE, lambda ex=ex: (quarters(dout, wq, ex, 1), DO.at[1, :, pl.ds(ex * wq, wq)])
-        )
-        for ex in range(2)
-    ]
-    act_swap = [
-        remote(CORE, lambda t=t: (act.at[:, act_cols(t)], act_s.at[:, act_cols(t)]))
-        for t in range(chunks)
-    ]
-    ctx_swap = remote(CORE, lambda: (ctx2.at[pl.ds(0, rows)], CO.at[1]))
-    dattn_swap = [
-        remote(
-            CORE, lambda ex=ex: (quarters(dattn, wq, ex, 1), DA.at[1, :, pl.ds(ex * wq, wq)])
-        )
-        for ex in range(2)
-    ]
-    need("q", "k", "v", "c", "g")
-    g_swap().wait_recv()
-    for build in dout_swap + act_swap + [ctx_swap] + dattn_swap:
-        go(build)
 
     class Unit:
         def __init__(self, P, RY, RZ, M):
@@ -1055,33 +1236,30 @@
         return [first + (last - first) * (t + 1) / count for t in range(count)]
 
     for k, a in enumerate(order):
-        plan.add(27 + 6 * k, lambda a=a: UI[0].fold_y(a))
-        plan.add(51 + 6 * k, lambda a=a: UI[1].fold_y(a))
-        plan.add(78 + 3 * k, lambda a=a: UU.fold_y(a))
-        plan.add(80 + 2 * k, lambda a=a: UO.fold_y(a))
+        plan.add(15 + 6 * k, lambda a=a: UI[0].fold_y(a))
+        plan.add(39 + 6 * k, lambda a=a: UI[1].fold_y(a))
+        plan.add(66 + 3 * k, lambda a=a: UU.fold_y(a))
+        plan.add(70 + 2 * k, lambda a=a: UO.fold_y(a))
         for j in range(3):
-            plan.add(92 + 10 * j + 3 * k, lambda a=a, j=j: UQ[j].fold_y(a))
+            plan.add(80 + 10 * j + 3 * k, lambda a=a, j=j: UQ[j].fold_y(a))
     xs_order = [t * per + il for t in range(chunks) for il in reversed(range(per))]
     for k, i in enumerate(xs_order):
-        plan.add(30 + 6 * k, lambda i=i: outer_x(i))
-    plan.add(72, lambda: inner_z(0))
-    plan.add(88, lambda: inner_z(1))
-    plan.add(98, inner_x)
-    plan.add(104, outer_z)
-    plan.add(112, outer_end)
-    plan.add(106, out_z)
-    plan.add(114, out_x)
+        plan.add(19 + 6 * k, lambda i=i: outer_x(i))
+    plan.add(60, lambda: inner_z(0))
+    plan.add(76, lambda: inner_z(1))
+    plan.add(86, inner_x)
+    plan.add(92, outer_z)
+    plan.add(100, outer_end)
+    plan.add(94, out_z)
+    plan.add(102, out_x)
     for j in range(3):
-        plan.add(115 + 6 * j, lambda j=j: proj_z(j))
-        plan.add(120 + 6 * j, lambda j=j: proj_x(j))
+        plan.add(103 + 6 * j, lambda j=j: proj_z(j))
+        plan.add(108 + 6 * j, lambda j=j: proj_x(j))
     for t in range(len(hops) + 1):
         plan.add(74 + 4 * t, lambda t=t: vector_hop(t))
 
-    attention(0, spaced(5, 13, pairs))
-    need("nrm", ("dinn", 0))
-    nrm_swap().wait_recv()
-    dinn_swap[0]().wait_recv()
-    weight_grad(lambda m: D[0, m], PI.at[0], spaced(13, 17, groups))
+    need("nrm", "nrm_s", ("dinn", 0), ("dinn_s", 0))
+    weight_grad(lambda m: D[0, m], PI.at[0], spaced(4, 8, groups))
     UI[0].start_y()
 
     def act_load(t):
@@ -1099,23 +1277,17 @@
         for c in act_load(t):
             c.start()
 
-    act_swap[0]().wait_recv()
     begin_act(0)
-    need(("dinn", 1))
-    dinn_swap[1]().wait_recv()
-    weight_grad(lambda m: D[1, m], PI.at[1], spaced(17, 20, groups))
+    need(("dinn", 1), ("dinn_s", 1))
+    weight_grad(lambda m: D[1, m], PI.at[1], spaced(8, 11, groups))
     UI[1].start_y()
-    for t in range(1, chunks):
-        act_swap[t]().wait_recv()
     if chunks > 1:
         begin_act(1)
     load("x0", lambda: (xall.at[pl.ds(0, rows)], L.at[0]))
     load("x1", lambda: (xall.at[pl.ds(rows, rows)], L.at[1]))
-    need(("dout", 0), ("dout", 1))
-    dout_swap[0]().wait_recv()
-    dout_swap[1]().wait_recv()
-
-    outer_times = spaced(20, 34, n)
+    need(("dout", 0), ("dout", 1), "dout_s")
+
+    outer_times = spaced(11, 25, n)
 
     def outer_body(u, carry):
         t, il = u // per, per - 1 - u % per
@@ -1143,10 +1315,7 @@
 
     lax.fori_loop(0, n, outer_body, 0)
 
-    need("co", ("dattn", 0), ("dattn", 1))
-    ctx_swap().wait_recv()
-    dattn_swap[0]().wait_recv()
-    dattn_swap[1]().wait_recv()
+    need("co", "co_s", "c", ("dattn", 0), ("dattn", 1), "dattn_s")
     for half in range(2):
         for g in range(hw // 256):
             lanes = slice(g * 256, (g + 1) * 256)
@@ -1164,13 +1333,13 @@
                     PO[i % 2, i // 2, ex * rs : (ex + 1) * rs] = r[
                         u * rs : (u + 1) * rs, ex * wq : (ex + 1) * wq
                     ]
-        for job in plan.due(36 + 3 * half):
+        for job in plan.due(27 + 3 * half):
             job()
     UO.start_y()
 
-    attention(1, spaced(39, 47, pairs))
-    for s in range(2, sh):
-        attention(s, spaced(47, 55, pairs))
+    need("q", "k", "v", "g", "g_s")
+    for s in range(sh):
+        attention(s, spaced(30 + 8 * s, 38 + 8 * s, pairs))
 
     need("x0", "x1", "vec")
     for j, ref in enumerate((Q, K, V)):
@@ -1182,7 +1351,7 @@
             total = jnp.sum(right(0).astype(F32), 0, keepdims=True)
             total = total + jnp.sum(right(1).astype(F32), 0, keepdims=True)
             VS[0, j // 2 : j // 2 + 1, at(core, hw)] = total
-        weight_grad(right, PQ.at[j], spaced(55 + 6 * j, 61 + 6 * j, groups))
+        weight_grad(right, PQ.at[j], spaced(54 + 6 * j, 60 + 6 * j, groups))
         UQ[j].start_y()
 
     need("w")
@@ -1229,7 +1398,6 @@
     for job in plan.due(1e9):
         job()
 
-    lo_swap().wait_recv()
     ig_near().wait_recv()
     for build in i_core + [u_core, u_core2] + o_core + q_core:
         build().wait_recv()
@@ -1239,7 +1407,7 @@
         end()
 
 
-def back_call(lens, n, act, dout, nrm, dinn, dattn, ctx, cr, xall, q, k, v, lse, dco, dcs, dfirst, w, lo, acc):
+def back_call(lens, n, act, dout, nrm, dinn, dattn, ctx, cr, xall, q, k, v, lse, *rest):
     rows, width = nrm.shape
     ff = act.shape[1]
     slots, sh, part, hw = q.shape
@@ -1262,10 +1430,9 @@
     four = (slots, sh, part, hw)
     return pl.pallas_call(
         functools.partial(back_kernel, n),
-        in_specs=[pl.BlockSpec(memory_space=pltpu.SMEM)] + [ANY] * 19,
-        out_specs=[ANY] * 12,
+        in_specs=[pl.BlockSpec(memory_space=pltpu.SMEM)] + [ANY] * 23,
+        out_specs=[ANY] * 10,
         out_shape=[
-            bf(2 * sh, part, width),
             f32(rows // 2, width),
             bf(rows // 2, width),
             bf(rs, ff),
@@ -1275,7 +1442,6 @@
             bf(rs, width),
             bf(rs, width),
             f32(16, width),
-            bf(rows, ff),
             f32(2, rows // 2, width),
         ],
         scratch_shapes=[
@@ -1332,19 +1498,13 @@
         dinn,
         dattn,
         ctx,
-        ctx.reshape(slots * sh * part, hw),
         cr,
         xall,
         q,
         k,
         v,
         lse,
-        dco,
-        dcs,
-        dfirst,
-        w,
-        lo,
-        acc,
+        *rest,
     )
 
 
@@ -1372,7 +1532,6 @@
     f = lax.axis_index("fsdp")
     n = lax.axis_size("fsdp")
     x, core = C // 2, C % 2
-    ids = jnp.stack([C, f]).astype(jnp.int32)
     seqs, part, width = inputs.shape
     ff = inner_weight.shape[1]
     sh = seqs // 2
@@ -1383,10 +1542,7 @@
     def pick(bit, a, b):
         return jnp.where(bit == 0, a, b), jnp.where(bit == 0, b, a)
 
-    def row_of(v):
-        return jnp.pad(v.reshape(1, -1), ((0, 0), (0, hw - v.shape[0])))
-
-    vectors = [
+    vectors = (
         query_bias,
         value_bias,
         out_bias,
@@ -1395,12 +1551,14 @@
         first_shift,
         second_gain,
         second_shift,
-        inner_bias,
-    ]
+    )
+    vecs = jnp.concatenate([v.reshape(1, rs) for v in vectors], 0)
+    if rs < 128:
+        vecs = jnp.pad(vecs, ((0, 0), (0, 128 - rs)))
     vecs = jnp.concatenate(
-        [row_of(v) for v in vectors] + [jnp.zeros((PACK - len(vectors), hw), BF)], 0
+        [vecs, inner_bias.reshape(ro // 128, 128), jnp.zeros((PACK - 8 - ro // 128, 128), BF)], 0
     )
-    x4, cot, w_qkv, wi, wu, wo, vecs, q4, k4, v4, c4, c_r, lse = front_call(
+    x4, cot, w_qkv, wi, wu, wo, vecs, q4, k4, v4, c4, c_r, c_s, lse = front_call(
         lengths,
         inputs,
         cotangent,
@@ -1416,11 +1574,25 @@
     xall = x4.reshape(2 * rows, width)
     ctx, cr = c4.reshape(2 * rows, hw), c_r.reshape(rows, hw)
     two = (2, sh, part, hw)
-    lo, act, dout, dinn, nrm, dattn, dfirst, dco, dcs, acc = ffn_call(
-        ids, lengths, sh, ctx, cr, xall, cot.reshape(rows, width), vecs, wo, wi, wu
-    )
-
-    layer_out, ig_here, ig_near, g_i, g_u, g_o, g_q, g_k, g_v, sums, _, _ = back_call(
+    (
+        dfirst,
+        dco,
+        acc,
+        act,
+        nrm,
+        dout,
+        dinn,
+        dattn,
+        layer_out,
+        act_s,
+        dout_s,
+        dinn_s,
+        nrm_s,
+        dattn_s,
+        dcs_s,
+    ) = ffn_call(lengths, sh, ctx, cr, xall, cot.reshape(rows, width), vecs, wo, wi, wu)
+
+    ig_here, ig_near, g_i, g_u, g_o, g_q, g_k, g_v, sums, _ = back_call(
         lengths,
         n,
         act,
@@ -1436,11 +1608,16 @@
         v4,
         lse,
         dco.reshape(two),
-        dcs.reshape(two),
         dfirst,
         w_qkv,
-        lo.reshape(2, sh, part, width),
         acc,
+        act_s,
+        dout_s,
+        dinn_s,
+        nrm_s,
+        dattn_s,
+        dcs_s.reshape(two),
+        c_s.reshape(rows, hw),
     )
     own = lax.dynamic_slice_in_dim(sums[:8], f * rs, rs, 1)
     own_inner = lax.dynamic_slice_in_dim(sums[8 : 8 + ff // width].reshape(ff), f * ro, ro, 0)

time: 418 us -> 367 us (0.88)
  Pallas kernels: 393 us -> 345 us
  local copies, waits for them, and re-layouts: 9.61 us -> 5.04 us
    pallas_call x1, Pallas kernels: 160 us -> 124 us  [front_call(): pl.pallas_call(functools.partial(front_kernel, n), in_specs=[pl.BlockSpec...]
    pallas_call x1, Pallas kernels: 179 us -> 163 us  [back_call(): pl.pallas_call(functools.partial(back_kernel, n), in_specs=[pl.BlockSpec(...]
    pad x8 -> x0, local copies, waits for them, and re-layouts: 5.29 us -> none  [row_of(): return jnp.pad(v.reshape(1, -1), ((0, 0), (0, hw - v.shape[0])))]
    pallas_call x1, Pallas kernels: 53.4 us -> 58 us  [ffn_call(): pl.pallas_call(functools.partial(ffn_kernel, n, sh, part), grid_spec=grid...]
where the time goes in v4:
time: 367 us; the launch traced here: 362 us
  Pallas kernels  345 us (94%)
  other arithmetic  10.6 us (3%)
  local copies, waits for them, and re-layouts  5.04 us (1%)
    pallas_call x1, Pallas kernels, back_call(): pl.pallas_call(functools.partial(back_kernel, n), in_specs=[pl.BlockSpec(...  163 us
    pallas_call x1, Pallas kernels, front_call(): pl.pallas_call(functools.partial(front_kernel, n), in_specs=[pl.BlockSpec...  124 us
    pallas_call x1, Pallas kernels, ffn_call(): pl.pallas_call(functools.partial(ffn_kernel, n, sh, part), grid_spec=grid...  58 us

profile of v4, /device:TPU:1, one launch (start us, length us, event | category | flops | bytes accessed | tf_op | source)
XLA Modules:
  0.0 362.0 jit_solution(57869850524541116)
XLA Ops:
  0.7 2.6 concatenate.6.vecs
  3.3 124.1 %front.1 = (bf16[4,3,128,1024]{3,2,1,0:T(8,128)(2,1)}, bf16[2,3,128,1024]{3,2,1,0:T(8,128)(2,1)}, bf16[3,1024,512]{2,1,0:T(8,128)(2,1)}, bf16[1024,4096]{1,0:T(8...) custom-call(s32[6]{0:T(128)} %lens.5, ...), custom_call_target="tpu_custom_call" | custom-call | tf_op jit(solution)/shard_map/front/pallas_call | solution.py:428
  127.4 58.0 %ffn.1 = (f32[768,1024]{1,0:T(8,128)}, bf16[768,512]{1,0:T(8,128)(2,1)}, f32[16,1024]{1,0:T(8,128)}, bf16[768,4096]{1,0:T(8,128)(2,1)}, bf16[768,1024]{1,0:T(8,1...) custom-call(s32[6]{0:T(128)} %lens.5, ...), custom_call_target="tpu_custom_call" | custom-call | flops 28991029248 | bytes 42467328 | tf_op jit(solution)/shard_map/ffn/pallas_call | solution.py:826
  185.4 163.1 %back.1 = (f32[384,1024]{1,0:T(8,128)}, bf16[384,1024]{1,0:T(8,128)(2,1)}, bf16[128,4096]{1,0:T(8,128)(2,1)}, bf16[512,1024]{1,0:T(8,128)(2,1)}, bf16[128,1024]{...) custom-call(s32[6]{0:T(128)} %lens.5, ...), custom_call_target="tpu_custom_call" | custom-call | tf_op jit(solution)/shard_map/back/pallas_call | solution.py:1431
  348.6 2.1 convert_select_fusion.1
  350.7 0.0 copy-start.2
  350.7 2.0 pad_maximum_fusion
  352.7 0.0 copy-done.2
  352.7 0.0 copy-start.1
  352.7 1.5 convert_element_type.27
  354.3 0.0 copy-done.1
  354.3 0.0 copy-start.6
  354.3 0.0 copy-start.5
  354.3 1.6 convert_element_type.28
  355.8 0.0 copy-start.4
  355.8 0.0 copy-start.3
  355.8 0.0 copy-done.6
  355.8 0.0 copy-start.7
  355.8 0.0 copy-start
  355.8 0.8 convert_element_type.23
  356.7 0.0 copy-done.5
  356.7 0.8 convert_element_type.24
  357.5 0.0 copy-done.4
  357.5 0.8 convert_element_type.25
  358.4 0.0 copy-done.3
  358.4 0.8 convert_element_type.26
  359.2 0.0 copy-done.7
  359.2 0.5 slice_bitcast_fusion.1
  359.8 0.7 dynamic_slice.7
  360.5 0.0 copy-done
  360.5 1.1 copy.39
  (5 shorter events, 0.0 us)
Async XLA Ops:
  350.7 2.0 copy-start.2
  352.7 1.5 copy-start.1
  354.3 1.6 copy-start.6
  354.3 2.4 copy-start.5
  355.8 1.7 copy-start.4
  355.8 2.6 copy-start.3
  355.8 3.4 copy-start.7
  355.8 4.6 %copy-start = (bf16[6,128,1024]{2,1,0:T(8,128)(2,1)S(1)}, bf16[6,128,1024]{2,1,0:T(8,128)(2,1)}, u32[]{:S(2)}) copy-start(bf16[6,128,1024]{2,1,0:T(8,128)(2,1)} %get-tuple-element.120) | copy-start | bytes 4718596

commit v5 on v4

--- a/solution.py
+++ b/solution.py
@@ -16,6 +16,7 @@
 TN = (((0,), (0,)), ((), ()))
 VMEM_LIMIT = 58 << 20
 BACK_LIMIT = 60 << 20
+WINDOW = 3
 
 
 def dot(a, b):
@@ -1067,6 +1068,7 @@
     class Unit:
         def __init__(self, P, RY, RZ, M):
             self.P, self.RY, self.RZ, self.M = P, RY, RZ, M
+            self.left, self.then = A, []
             self.y = [
                 remote(Y, lambda a=a: (P.at[1, a], RY.at[a])) for a in range(A)
             ]
@@ -1075,14 +1077,15 @@
             ]
 
         def start_y(self, a=None):
-            for i in order if a is None else [a]:
-                go(self.y[i])
+            queue.extend((self, i) for i in (order if a is None else [a]))
+            pump()
 
         def fold_y(self, a):
             self.y[a]().wait_recv()
             self.P[0, a] = plus(self.P[0, a], self.RY[a])
             if a:
                 go(self.z[a])
+            self.left -= 1
 
         def fold_z(self):
             for a in range(1, A):
@@ -1090,6 +1093,26 @@
             self.M[...] = plus(self.P[0, 0], *[self.RZ[a - 1] for a in range(1, A)])
 
     order = list(range(1, A)) + [0]
+    queue, flying, later = [], [], []
+
+    def pump():
+        while queue and len(flying) < WINDOW:
+            unit, a = queue.pop(0)
+            go(unit.y[a])
+            flying.append((unit, a))
+
+    def fold_next():
+        if flying:
+            unit, a = flying.pop(0)
+            pump()
+            unit.fold_y(a)
+            if not unit.left:
+                later.extend((3 * t + 2, job) for t, job in enumerate(unit.then))
+        now = [job for t, job in later if t <= 0]
+        later[:] = [(t - 1, job) for t, job in later if t > 0]
+        for job in now:
+            job()
+
     UI = [Unit(PI.at[ex], RYI.at[ex], RZI.at[ex], MI.at[ex]) for ex in range(2)]
     UU = Unit(PU.at[0], RYU, RZU, MU)
     UO = Unit(PO, RYO, RZO, MO)
@@ -1235,26 +1258,27 @@
     def spaced(first, last, count):
         return [first + (last - first) * (t + 1) / count for t in range(count)]
 
-    for k, a in enumerate(order):
-        plan.add(15 + 6 * k, lambda a=a: UI[0].fold_y(a))
-        plan.add(39 + 6 * k, lambda a=a: UI[1].fold_y(a))
-        plan.add(66 + 3 * k, lambda a=a: UU.fold_y(a))
-        plan.add(70 + 2 * k, lambda a=a: UO.fold_y(a))
-        for j in range(3):
-            plan.add(80 + 10 * j + 3 * k, lambda a=a, j=j: UQ[j].fold_y(a))
-    xs_order = [t * per + il for t in range(chunks) for il in reversed(range(per))]
+    UI[0].then = [lambda: inner_z(0)]
+    UI[1].then = [lambda: inner_z(1), inner_x]
+    UU.then = [outer_z, outer_end]
+    UO.then = [out_z, out_x]
+    for j in range(3):
+        UQ[j].then = [lambda j=j: proj_z(j), lambda j=j: proj_x(j)]
+
+    xs_order = list(range(1, n, 2)) + list(range(0, n, 2))
     for k, i in enumerate(xs_order):
-        plan.add(19 + 6 * k, lambda i=i: outer_x(i))
-    plan.add(60, lambda: inner_z(0))
-    plan.add(76, lambda: inner_z(1))
-    plan.add(86, inner_x)
-    plan.add(92, outer_z)
-    plan.add(100, outer_end)
-    plan.add(94, out_z)
-    plan.add(102, out_x)
-    for j in range(3):
-        plan.add(103 + 6 * j, lambda j=j: proj_z(j))
-        plan.add(108 + 6 * j, lambda j=j: proj_x(j))
+        if k < n // 2:
+            plan.add(11 + 14 * (per * (i // per) + per - 1 - i % per + 1) / n, lambda i=i: outer_copy(i).start())
+        follow = xs_order[k + n // 2] if k < n // 2 else None
+
+        def fold_x(i=i, follow=follow):
+            if follow is not None:
+                outer_copy(follow).start()
+            outer_x(i)
+
+        plan.add(20 + 48 * k / n, fold_x)
+    for k in range(13 * A):
+        plan.add(14 + 18 * k / A, fold_next)
     for t in range(len(hops) + 1):
         plan.add(74 + 4 * t, lambda t=t: vector_hop(t))
 
@@ -1304,7 +1328,6 @@
         i = t * per + il
         for ex in range(2):
             PU[ex, i % 2, i // 2] = r[:, ex * wq : (ex + 1) * wq]
-        outer_copy(i).start()
 
         @pl.when((u % per == per - 1) & (t + 2 < chunks))
         def _():
@@ -1397,6 +1420,8 @@
 
     for job in plan.due(1e9):
         job()
+    while flying or later:
+        fold_next()
 
     ig_near().wait_recv()
     for build in i_core + [u_core, u_core2] + o_core + q_core:
@@ -1508,6 +1533,36 @@
     )
 
 
+def finish_kernel(here, near, lo, *refs):
+    o_ig, o_lo = refs[6:8]
+    x = lax.axis_index("ctx") // 2
+    o_ig[x] = here[...]
+    o_ig[1 - x] = near[...].astype(F32)
+    o_lo[...] = lo[...]
+    for source, target in zip(refs[:6], refs[8:]):
+        target[...] = source[...].astype(F32)
+
+
+def finish_call(here, near, lo, *grads):
+    steps = 4
+    rows, width = here.shape
+
+    def by(a):
+        return pl.BlockSpec((a.shape[0] // steps, a.shape[1]), lambda i: (i, 0))
+
+    return pl.pallas_call(
+        finish_kernel,
+        grid=(steps,),
+        in_specs=[by(a) for a in (here, near, lo) + grads],
+        out_specs=[pl.BlockSpec((2, rows // steps, width), lambda i: (0, i, 0)), by(lo)]
+        + [by(g) for g in grads],
+        out_shape=[jax.ShapeDtypeStruct((2, rows, width), F32), jax.ShapeDtypeStruct(lo.shape, BF)]
+        + [jax.ShapeDtypeStruct(g.shape, F32) for g in grads],
+        compiler_params=params(),
+        name="finish",
+    )(here, near, lo, *grads)
+
+
 def per_device(
     inputs,
     lengths,
@@ -1621,13 +1676,11 @@
     )
     own = lax.dynamic_slice_in_dim(sums[:8], f * rs, rs, 1)
     own_inner = lax.dynamic_slice_in_dim(sums[8 : 8 + ff // width].reshape(ff), f * ro, ro, 0)
-    third = (sh, part, width)
-    input_grad = jnp.concatenate(
-        pick(x, ig_here.reshape(third), ig_near.reshape(third).astype(F32)), 0
+    input_grad, layer_out, *grads = finish_call(
+        ig_here, ig_near, layer_out.reshape(seqs * part, width), g_q, g_k, g_v, g_o, g_i, g_u
     )
-    grad_query, grad_key, grad_value, grad_out, grad_inner, grad_outer = (
-        g.astype(F32) for g in (g_q, g_k, g_v, g_o, g_i, g_u)
-    )
+    grad_query, grad_key, grad_value, grad_out, grad_inner, grad_outer = grads
+    input_grad, layer_out = input_grad.reshape(inputs.shape), layer_out.reshape(inputs.shape)
 
     return (
         layer_out,

time: 367 us -> 353 us (0.962)
  other arithmetic: 10.6 us -> 0 us
    pallas_call x1, Pallas kernels: 163 us -> 153 us  [back_call(): pl.pallas_call(functools.partial(back_kernel, n), in_specs=[pl.BlockSpec(...]
    pallas_call x0 -> x1, Pallas kernels: none -> 7.36 us  [finish_call(): pl.pallas_call(finish_kernel, grid=(steps,), in_specs=[by(a) for a in (he...]
    convert_element_type x6 -> x0, other arithmetic: 6.46 us -> none  [per_device(): g.astype(F32)]
where the time goes in v5:
time: 353 us; the launch traced here: 348 us
  Pallas kernels  343 us (97%)
  local copies, waits for them, and re-layouts  3.87 us (1%)
    pallas_call x1, Pallas kernels, back_call(): pl.pallas_call(functools.partial(back_kernel, n), in_specs=[pl.BlockSpec(...  153 us
    pallas_call x1, Pallas kernels, front_call(): pl.pallas_call(functools.partial(front_kernel, n), in_specs=[pl.BlockSpec...  124 us
    pallas_call x1, Pallas kernels, ffn_call(): pl.pallas_call(functools.partial(ffn_kernel, n, sh, part), grid_spec=grid...  58 us
    pallas_call x1, Pallas kernels, finish_call(): pl.pallas_call(finish_kernel, grid=(steps,), in_specs=[by(a) for a in (he...  7.36 us

profile of v5, /device:TPU:1, one launch (start us, length us, event | category | flops | bytes accessed | tf_op | source)
XLA Modules:
  0.0 347.9 jit_solution(15216959383951889463)
XLA Ops:
  0.7 2.6 concatenate.3.vecs
  3.3 124.1 %front.1 = (bf16[4,3,128,1024]{3,2,1,0:T(8,128)(2,1)}, bf16[2,3,128,1024]{3,2,1,0:T(8,128)(2,1)}, bf16[3,1024,512]{2,1,0:T(8,128)(2,1)}, bf16[1024,4096]{1,0:T(8...) custom-call(s32[6]{0:T(128)} %lens.5, ...), custom_call_target="tpu_custom_call" | custom-call | tf_op jit(solution)/shard_map/front/pallas_call | solution.py:429
  127.4 58.0 %ffn.1 = (f32[768,1024]{1,0:T(8,128)}, bf16[768,512]{1,0:T(8,128)(2,1)}, f32[16,1024]{1,0:T(8,128)}, bf16[768,4096]{1,0:T(8,128)(2,1)}, bf16[768,1024]{1,0:T(8,1...) custom-call(s32[6]{0:T(128)} %lens.5, ...), custom_call_target="tpu_custom_call" | custom-call | flops 28991029248 | bytes 42467328 | tf_op jit(solution)/shard_map/ffn/pallas_call | solution.py:827
  185.4 153.4 %back.1 = (f32[384,1024]{1,0:T(8,128)}, bf16[384,1024]{1,0:T(8,128)(2,1)}, bf16[128,4096]{1,0:T(8,128)(2,1)}, bf16[512,1024]{1,0:T(8,128)(2,1)}, bf16[128,1024]{...) custom-call(s32[6]{0:T(128)} %lens.5, ...), custom_call_target="tpu_custom_call" | custom-call | tf_op jit(solution)/shard_map/back/pallas_call | solution.py:1456
  338.8 0.0 copy-start
  338.8 7.4 %finish.1 = (f32[2,384,1024]{2,1,0:T(8,128)}, bf16[768,1024]{1,0:T(8,128)(2,1)}, f32[128,1024]{1,0:T(8,128)}, f32[128,1024]{1,0:T(8,128)}, f32[128,1024]{1,0:T(8...) custom-call(f32[384,1024]{1,0:T(8,128)} %get-tuple-element.91.here, ...), custom_call_target="tpu_custom_call" | custom-call | tf_op jit(solution)/shard_map/finish/pallas_call | solution.py:1553
  346.2 0.0 copy-done
  346.2 0.5 slice_bitcast_fusion.1
  346.8 0.7 dynamic_slice.7
  (5 shorter events, 0.0 us)
Async XLA Ops:
  338.8 7.4 %copy-start = (f32[16,1024]{1,0:T(8,128)S(1)}, f32[16,1024]{1,0:T(8,128)}, u32[]{:S(2)}) copy-start(f32[16,1024]{1,0:T(8,128)} %get-tuple-element.108) | copy-start | bytes 196612
